TPU v7x, 32 devices: a whole 2x2x4 slice. The times are simulated.
32 devices in a mesh: dp: 8 (over z, y), tensor: 4 (over x, core).
Axes of the slice: x: 2, y: 2, z: 4, core: 2. Of those that a mesh axis runs over, the one named last changes fastest.
Arguments:
- token_ids: int32 [64, 256], P('dp'), may hold values from 0 to 2023
- masked_at: int32 [64, 128], P('dp'), may hold values from 0 to 255, as said below
- live_counts: int32 [64], P('dp'), may hold values from 1 to 128
- tables: bfloat16 [2281, 768], P(None, 'tensor'), may hold values from -1 to 1
- table_mom: float32 [2281, 768], P(None, 'tensor'), may hold values from -0.0234375 to 0.0234375
- vec_whole: float32 [8, 768], replicated, may hold values from -1.5 to 1.6, as said below
- vec_mom: float32 [8, 768], replicated, may hold values from -0.0625 to 0.0625
- vec_split: float32 [4, 1152], P('tensor'), may hold values from -4 to 4
- split_mom: float32 [4, 1152], P('tensor'), may hold values from -0.046875 to 0.046875
- head_bias: float32 [2025], replicated, may hold values from -4 to 4
- bias_mom: float32 [2025], replicated, may hold values from -0.015625 to 0.015625
- w_qkv: bfloat16 [768, 2304], P(None, 'tensor'), may hold values from -0.21875 to 0.21875
- w_out: bfloat16 [768, 768], P('tensor'), may hold values from -0.875 to 0.875
- w_up: bfloat16 [768, 3072], P(None, 'tensor'), may hold values from -0.21875 to 0.21875
- w_down: bfloat16 [3072, 768], P('tensor'), may hold values from -0.109375 to 0.109375
- mom_qkv: float32 [768, 2304], P(None, 'tensor'), may hold values from -0.0048828125 to 0.0048828125
- mom_out: float32 [768, 768], P('tensor'), may hold values from -0.0048828125 to 0.0048828125
- mom_up: float32 [768, 3072], P(None, 'tensor'), may hold values from -0.0048828125 to 0.0048828125
- mom_down: float32 [3072, 768], P('tensor'), may hold values from -0.0048828125 to 0.0048828125
- err_qkv: float32 [8, 768, 2304], P('dp', None, 'tensor'), may hold values from -0.00390625 to 0.00390625
- err_out: float32 [8, 768, 768], P('dp', 'tensor'), may hold values from -0.00390625 to 0.00390625
- err_up: float32 [8, 768, 3072], P('dp', None, 'tensor'), may hold values from -0.00390625 to 0.00390625
- err_down: float32 [8, 3072, 768], P('dp', 'tensor'), may hold values from -0.00390625 to 0.00390625
- start_qkv: float32 [2304, 8], P('tensor'), may hold values from -6 to 6
- start_out: float32 [3072, 8], P('tensor'), may hold values from -6 to 6
- start_up: float32 [3072, 8], P('tensor'), may hold values from -6 to 6
- start_down: float32 [3072, 8], P('tensor'), may hold values from -6 to 6
Outputs:
- loss: float32 [2], replicated
- tables_new: float32 [2281, 768], P(None, 'tensor')
- table_mom_new: float32 [2281, 768], P(None, 'tensor')
- vec_whole_new: float32 [8, 768], replicated
- vec_mom_new: float32 [8, 768], replicated
- vec_split_new: float32 [4, 1152], P('tensor')
- split_mom_new: float32 [4, 1152], P('tensor')
- head_bias_new: float32 [2025], replicated
- bias_mom_new: float32 [2025], replicated
- qkv_new: float32 [768, 2304], P(None, 'tensor')
- qkv_mom_new: float32 [768, 2304], P(None, 'tensor')
- qkv_err_new: float32 [8, 768, 2304], P('dp', None, 'tensor')
- qkv_left: float32 [4, 768, 8], P('tensor')
- qkv_right: float32 [2304, 8], P('tensor')
- out_new: float32 [768, 768], P('tensor')
- out_mom_new: float32 [768, 768], P('tensor')
- out_err_new: float32 [8, 768, 768], P('dp', 'tensor')
- out_left: float32 [4, 192, 8], P('tensor')
- out_right: float32 [3072, 8], P('tensor')
- up_new: float32 [768, 3072], P(None, 'tensor')
- up_mom_new: float32 [768, 3072], P(None, 'tensor')
- up_err_new: float32 [8, 768, 3072], P('dp', None, 'tensor')
- up_left: float32 [4, 768, 8], P('tensor')
- up_right: float32 [3072, 8], P('tensor')
- down_new: float32 [3072, 768], P('tensor')
- down_mom_new: float32 [3072, 768], P('tensor')
- down_err_new: float32 [8, 3072, 768], P('dp', 'tensor')
- down_left: float32 [4, 768, 8], P('tensor')
- down_right: float32 [3072, 8], P('tensor')
Inputs may be any that keep to these rules, and one draw needn't show every extreme that they name: `masked_at`: the positions of one image's slots are distinct. `vec_whole`: rows 0, 3 and 6 are gains, the others biases.
All inputs are finite; a program needn't handle non-finite values.
Results may differ from a plain program's by a relative error of at most 0.0078.
Values may be sent and summed in bfloat16 or wider, within the bound.
No kernel may reach another device: no remote copies, remote signals or barrier semaphores. Data moves between devices by JAX's collectives and lax.ppermute only.
A program may use at most 192 MiB of HBM per device.

v0:
```python
import functools

import jax
import jax.numpy as jnp
from jax import lax
from jax.experimental import pallas as pl
from jax.experimental.pallas import tpu as pltpu
from jax.sharding import PartitionSpec as P

HD = 48
EPSILON = 1e-05
BETA = 0.9
RATE_MAT = 100.0
RATE_VEC = 10.0
RATE_TAB = 100.0
HIGHEST = lax.Precision.HIGHEST
BF16 = jnp.bfloat16
F32 = jnp.float32
MIB = 1024 * 1024


def bdot(left, right):
    return jnp.dot(left, right, preferred_element_type=F32)


def tdot(left, right):
    return lax.dot_general(left, right, (((0,), (0,)), ((), ())), preferred_element_type=F32)


def ndot(left, right):
    return lax.dot_general(left, right, (((1,), (1,)), ((), ())), preferred_element_type=F32)


def across(x, axis, bit):
    size = lax.axis_size(axis)
    return lax.ppermute(x, axis, [(i, i ^ bit) for i in range(size)])


def core_swap(x):
    return across(x, "tensor", 1)


def chip_swap(x):
    return across(x, "tensor", 2)


def tie(x, *others):
    return lax.optimization_barrier((x,) + others)[0]


def head_mask(width, head):
    lane = lax.broadcasted_iota(jnp.int32, (1, width), 1)
    return ((lane >= head * HD) & (lane < (head + 1) * HD)).astype(BF16)


SCALE = 10.0
LIMITS = {
    "pack": (56, 3), "embed": (8, 5), "attention_first": (10, 7), "attention_second": (10, 8), "mlp_first": (12, 7),
    "mlp_second": (14, 7), "head": (24, 9), "down_send": (8, 3), "down_keep": (14, 4), "up_send": (14, 6),
    "up_keep": (20, 8), "attention_send": (14, 13), "attention_keep": (20, 15), "scatter": (8, 5),
    "orthonormal": (4, 3), "right_mlp": (16, 3), "right_attention": (12, 2), "update": (16, 4),
}


def call(kernel, name, out_shape, operands, in_specs=None, scratch=(), out_specs=None, **grid):
    limit, cost = LIMITS[name]
    cost *= 1.0 if name in ("scatter", "orthonormal", "right_mlp", "right_attention", "update") else SCALE
    if in_specs is None:
        in_specs = [pl.BlockSpec(memory_space=pltpu.VMEM)] * len(operands)
    if out_specs is not None:
        grid["out_specs"] = out_specs
    return pl.pallas_call(
        kernel,
        out_shape=out_shape,
        in_specs=in_specs,
        scratch_shapes=list(scratch),
        compiler_params=pltpu.CompilerParams(vmem_limit_bytes=limit * MIB),
        cost_estimate=pl.CostEstimate(flops=int(cost * 1150000000), bytes_accessed=int(cost * 1000000), transcendentals=0),
        name=name,
        **grid,
    )(*operands)


VMEM = pl.BlockSpec(memory_space=pltpu.VMEM)
SMEM = pl.BlockSpec(memory_space=pltpu.SMEM)
ANY = pl.BlockSpec(memory_space=pltpu.HBM)


def shape(*dims, dtype=F32):
    return jax.ShapeDtypeStruct(dims, dtype)


def normalize(x):
    center = x - jnp.mean(x, -1, keepdims=True)
    inverse = lax.rsqrt(jnp.mean(center * center, -1, keepdims=True) + EPSILON)
    return center * inverse, inverse


def norm_back(normed, inverse, gain, grad):
    inner = grad * gain
    first = jnp.mean(inner, -1, keepdims=True)
    second = jnp.mean(inner * normed, -1, keepdims=True)
    d_x = inverse * (inner - first - normed * second)
    return d_x, jnp.sum(grad * normed, 0, keepdims=True), jnp.sum(grad, 0, keepdims=True)


def split3(x):
    high = x.astype(BF16).astype(F32)
    rest = x - high
    middle = rest.astype(BF16).astype(F32)
    return jnp.concatenate([high, middle, rest - middle], 0).astype(BF16)


def fold3(x):
    rank = x.shape[0] // 3
    return x[:rank] + x[rank : 2 * rank] + x[2 * rank :]


def panel(start, right, left):
    return fold3(bdot(split3(fold3(ndot(split3(start), right))), left))


def split2(x):
    high = x.astype(BF16)
    return high, (x - high.astype(F32)).astype(BF16)


def wide(dot, start, x):
    parts = split3(start)
    high, rest = split2(x)
    return fold3(dot(parts, high) + dot(parts, rest))


class Fetch:
    def __init__(self, meta_ref, sems):
        self.half, self.sems, self.used = meta_ref[1], sems, 0

    def one(self, source, target):
        copy = pltpu.make_async_copy(source, target, self.sems.at[self.used])
        self.used += 1
        copy.start()
        return copy

    def block(self, pieces, target, first=0):
        if len(pieces) == 1:
            return [self.one(pieces[0], target.at[pl.ds(first, pieces[0].shape[0]), :])]
        size = pieces[0].shape[0]
        spots = (first + self.half * size, first + (1 - self.half) * size)
        return [
            self.one(piece, target.at[pl.ds(pl.multiple_of(spot, 32), size), :])
            for piece, spot in zip(pieces, spots)
        ]


def wait(copies):
    for copy in copies:
        copy.wait()


def pack_kernel(meta_ref, qkv_ref, out_ref, up_ref, down_ref, tables_ref, first_ref, first_half, up_half, down_half, table_ref, table_half, sems):
    near, rest = qkv_ref.shape[0], out_ref.shape[0]
    size = first_half.shape[0]
    half = meta_ref[1]
    at = pl.multiple_of(half * size, 32)
    fetch = Fetch(meta_ref, sems)
    firsts = [
        fetch.one(qkv_ref, first_ref.at[pl.ds(0, near), :]),
        fetch.one(out_ref, first_ref.at[pl.ds(near, rest), :]),
    ]
    copies = [
        fetch.one(up_ref.at[pl.ds(at, size), :], up_half),
        fetch.one(down_ref.at[pl.ds(at, size), :], down_half),
    ]
    total = tables_ref.shape[1]
    table_ref[...] = jnp.zeros_like(table_ref)
    table_ref[:, :total] = tables_ref[...]
    rows = table_half.shape[0]
    table_half[...] = table_ref[pl.ds(pl.multiple_of(half * rows, 32), rows), :]
    wait(firsts)
    first_half[...] = first_ref[pl.ds(at, size), :]
    wait(copies)


def embed_kernel(own, vocab, meta_ref, live_ref, ids_ref, slots_ref, table_ref, far_ref, near_ref, own_ref, rows_ref):
    images, length = ids_ref.shape
    slot_count = slots_ref.shape[1]
    total = table_ref.shape[1]
    member = meta_ref[0]
    ids_t = jnp.transpose(ids_ref[...].astype(F32))
    image_lane = lax.broadcasted_iota(jnp.int32, (length, images), 1)
    position = lax.broadcasted_iota(jnp.int32, (length, 1), 0)
    slot_lane = lax.broadcasted_iota(jnp.int32, (1, slot_count), 1)
    table_lane = lax.broadcasted_iota(jnp.int32, (1, total), 1)
    table = table_ref[...]

    def rows_of(ids):
        hot = jnp.where(ids == table_lane, 1.0, 0.0).astype(BF16)
        return ndot(table, hot).astype(BF16)

    targets = {
        0: (own_ref, 0), 1: (near_ref, 0), 2: (far_ref.at[0], 0), 3: (far_ref.at[1], 0),
    }
    for k in range(4):
        for i in range(own):
            image = (member ^ k) * own + i
            hit = (slots_ref[pl.ds(image, 1), :] == position) & (slot_lane < live_ref[image])
            masked = jnp.max(jnp.where(hit, 1.0, 0.0), 1, keepdims=True)
            ids = jnp.sum(jnp.where(image_lane == image, ids_t, 0.0), 1, keepdims=True)
            ids = jnp.where(masked > 0, float(vocab - 1), ids).astype(jnp.int32)
            place = k * own + i
            rows_ref[:, place : place + 1] = ids
            ref, first = targets[k]
            ref[:, first + i * length : first + (i + 1) * length] = rows_of(ids)
    at = rows_of(position + vocab)
    own_ref[:, own * length :] = at
    near_ref[:, own * length :] = at
    far_ref[0, :, own * length :] = at[:, : length // 2]
    far_ref[1, :, own * length :] = at[:, length // 2 :]


def attention_one(length, hb, w, bias_ref, qkv_ref, lse_ref, ctx_ref):
    width = ctx_ref.shape[1]
    mixed = ndot(hb, w)
    first = bias_ref.shape[1] - 6 * width
    q_bias = bias_ref[0:1, first : first + width]
    v_bias = bias_ref[0:1, first + width : first + 2 * width]
    qkv_ref[0] = ((mixed[:, :width] + q_bias) * HD ** (-0.5)).astype(BF16)
    qkv_ref[1] = mixed[:, width : 2 * width].astype(BF16)
    qkv_ref[2] = (mixed[:, 2 * width :] + v_bias).astype(BF16)
    for image in range(hb.shape[0] // length):
        rows = slice(image * length, (image + 1) * length)
        q, k, v = qkv_ref[0, rows, :], qkv_ref[1, rows, :], qkv_ref[2, rows, :]
        total = jnp.zeros((length, width), F32)
        for head in range(width // HD):
            mask = head_mask(width, head)
            scores = ndot(q * mask, k)
            top = jnp.max(scores, -1, keepdims=True)
            powers = jnp.exp(scores - top)
            weight = jnp.sum(powers, -1, keepdims=True)
            lse_ref[rows, head : head + 1] = top + jnp.log(weight)
            probs = (powers * (1.0 / weight)).astype(BF16)
            total = total + bdot(probs, v * mask)
        ctx_ref[rows, :] = total.astype(BF16)


def attention_first_kernel(
    length, meta_ref, e0, e1, e2, e3, vec_ref, b0, b1, c0, c1,
    normed_ref, inverse_ref, hb_ref, qkv0, lse0, ctx0, qkv1, lse1, ctx1, x_ref, w_ref, sems,
):
    rows, width = hb_ref.shape[0], e0.shape[0]
    member = meta_ref[0]
    fetch = Fetch(meta_ref, sems)
    used = 3 * width
    zero = fetch.one(c0.at[pl.ds(0, used), :], w_ref.at[0])
    one = fetch.one(c1.at[pl.ds(0, used), :], w_ref.at[1])
    slabs = ((e0, e0, e0), (e1, e1, e1), (e2.at[0], e2.at[0], e2.at[1]), (e3.at[1], e3.at[0], e3.at[1]))
    for k, (ref, low, high) in enumerate(slabs):
        at = low[:, rows:] if low is high else jnp.concatenate([low[:, rows:], high[:, rows:]], 1)
        at = at.astype(F32)
        place = pl.ds(pl.multiple_of((member ^ k) * width, 64), width)
        for i in range(rows // length):
            x_ref[place, i * length : (i + 1) * length] = ref[:, i * length : (i + 1) * length].astype(F32) + at
    normed, inverse = normalize(jnp.transpose(x_ref[...]))
    normed_ref[...] = normed
    inverse_ref[...] = inverse
    hb_ref[...] = (normed * vec_ref[0:1, :] + vec_ref[1:2, :]).astype(BF16)
    hb = hb_ref[...]
    zero.wait()
    attention_one(length, hb, w_ref[0], b0, qkv0, lse0, ctx0)
    one.wait()
    attention_one(length, hb, w_ref[1], b1, qkv1, lse1, ctx1)


def attention_second_kernel(
    length, meta_ref, normed_ref, hb_ref, vec_ref, b2, b3, ctx0, ctx1, c0, c1, c2a, c2b, c3a, c3b,
    normed1_ref, inverse1_ref, h1b_ref, qkv2, lse2, ctx2, qkv3, lse3, ctx3, w_ref, o_ref, sems,
):
    hb = hb_ref[...]
    width = ctx0.shape[1]
    used = 3 * width
    fetch = Fetch(meta_ref, sems)
    two = fetch.block((c2a, c2b), w_ref.at[0])
    three = fetch.block((c3a, c3b), w_ref.at[1])
    others = [fetch.one(c.at[pl.ds(used, width), :], o_ref.at[n]) for n, c in enumerate((c0, c1))]
    wait(two)
    attention_one(length, hb, w_ref[0, :used, :], b2, qkv2, lse2, ctx2)
    wait(three)
    attention_one(length, hb, w_ref[1, :used, :], b3, qkv3, lse3, ctx3)
    wait(others)
    total = bdot(ctx0[...], o_ref[0]) + bdot(ctx1[...], o_ref[1])
    total = total + bdot(ctx2[...], w_ref[0, used:, :]) + bdot(ctx3[...], w_ref[1, used:, :])
    z_one = normed_ref[...] * vec_ref[0:1, :] + vec_ref[1:2, :] + (total + vec_ref[2:3, :])
    normed, inverse = normalize(z_one)
    normed1_ref[...] = normed
    inverse1_ref[...] = inverse
    h1b_ref[...] = (normed * vec_ref[3:4, :] + vec_ref[4:5, :]).astype(BF16)


def gelu_pair(x):
    inner = 0.7978845608028654 * x * (1.0 + 0.044715 * x * x)
    curve = jnp.tanh(inner)
    value = 0.5 * x * (1.0 + curve)
    slope = 0.5 * (1.0 + curve) + 0.5 * x * (1.0 - curve * curve) * (
        0.7978845608028654 * (1.0 + 3 * 0.044715 * x * x)
    )
    return value, slope


def mlp_one(h1b, up_ref, bias_ref, active_ref, slope_ref):
    first = bias_ref.shape[1] - up_ref.shape[1]
    step = 256
    for at in range(0, up_ref.shape[1], step):
        pre = bdot(h1b, up_ref[:, at : at + step]) + bias_ref[0:1, first + at : first + at + step]
        value, slope = gelu_pair(pre)
        active_ref[:, at : at + step] = value.astype(BF16)
        slope_ref[:, at : at + step] = slope


def mlp_first_kernel(meta_ref, h1b_ref, b0, b1, u0, u1, d0, d1, a0, a1, s0, s1, low_ref, w_ref, sems):
    fetch = Fetch(meta_ref, sems)
    copies = [fetch.one(ref, w_ref.at[n]) for n, ref in enumerate((u0, d0, u1, d1))]
    h1b = h1b_ref[...]
    copies[0].wait()
    mlp_one(h1b, w_ref.at[0], b0, a0, s0)
    copies[1].wait()
    low_ref[...] = bdot(a0[...], w_ref[1])
    copies[2].wait()
    mlp_one(h1b, w_ref.at[2], b1, a1, s1)
    copies[3].wait()
    low_ref[...] += bdot(a1[...], w_ref[3])


def mlp_second_kernel(
    meta_ref, h1b_ref, b2, b3, low_ref, normed1_ref, vec_ref, u2a, u2b, u3a, u3b, d2a, d2b, d3a, d3b,
    a2, a3, s2, s3, normed2_ref, inverse2_ref, h2b_ref, w_ref, sems,
):
    fetch = Fetch(meta_ref, sems)
    pieces = ((u2a, u2b), (d2a, d2b), (u3a, u3b), (d3a, d3b))
    copies = [fetch.block(piece, w_ref.at[n]) for n, piece in enumerate(pieces)]
    h1b = h1b_ref[...]
    wait(copies[0])
    mlp_one(h1b, w_ref.at[0], b2, a2, s2)
    wait(copies[1])
    normed2_ref[...] = low_ref[...] + bdot(a2[...], w_ref[1])
    wait(copies[2])
    mlp_one(h1b, w_ref.at[2], b3, a3, s3)
    wait(copies[3])
    total = normed2_ref[...] + bdot(a3[...], w_ref[3]) + vec_ref[5:6, :]
    normed, inverse = normalize(normed1_ref[...] * vec_ref[3:4, :] + vec_ref[4:5, :] + total)
    normed2_ref[...] = normed
    inverse2_ref[...] = inverse
    h2b_ref[...] = (normed * vec_ref[6:7, :] + vec_ref[7:8, :]).astype(BF16)


def head_kernel(
    own, vocab, meta_ref, live_ref, count_ref, ids_ref, slots_ref, bias_ref, vec_ref,
    h2b_ref, normed2_ref, inverse2_ref, t0, t1, t2a, t2b, t3a, t3b,
    dz_ref, dzb_ref, loss_ref, gbias_ref, gvec_ref, send_ref, keep_ref,
    table_ref, full_ref, grad_ref, sems,
):
    images, length = ids_ref.shape
    slot_count = slots_ref.shape[1]
    total = bias_ref.shape[1]
    member = meta_ref[0]
    columns = t0.shape[0]
    fetch = Fetch(meta_ref, sems)
    copies = []
    for k, pieces in enumerate(((t0,), (t1,), (t2a, t2b), (t3a, t3b))):
        copies += fetch.block(pieces, table_ref, pl.multiple_of((member ^ k) * columns, 64))
    slots_t = jnp.transpose(slots_ref[...].astype(F32))
    image_lane = lax.broadcasted_iota(jnp.int32, (slot_count, images), 1)
    slot_row = lax.broadcasted_iota(jnp.int32, (slot_count, 1), 0)
    position = lax.broadcasted_iota(jnp.int32, (1, length), 1).astype(F32)
    picks, targets, weights, picked = [], [], [], []
    for i in range(own):
        image = member * own + i
        at = jnp.sum(jnp.where(image_lane == image, slots_t, 0.0), 1, keepdims=True)
        hit = at == position
        ids = ids_ref[pl.ds(image, 1), :].astype(F32)
        targets.append(jnp.sum(jnp.where(hit, ids, 0.0), 1, keepdims=True).astype(jnp.int32))
        weights.append(jnp.where(slot_row < live_ref[image], 1.0, 0.0))
        picks.append(jnp.where(hit, 1.0, 0.0).astype(BF16))
        picked.append(bdot(picks[i], h2b_ref[i * length : (i + 1) * length, :]).astype(BF16))
    target = jnp.concatenate(targets, 0)
    weight = jnp.concatenate(weights, 0)
    rows = jnp.concatenate(picked, 0)
    wait(copies)
    lane = lax.broadcasted_iota(jnp.int32, (1, total), 1)
    logits = bdot(rows, table_ref[...]) + bias_ref[...]
    logits = jnp.where(lane < vocab, logits, -1e30)
    top = jnp.max(logits, -1, keepdims=True)
    log_total = top + jnp.log(jnp.sum(jnp.exp(logits - top), -1, keepdims=True))
    hot = jnp.where(lane == target, 1.0, 0.0)
    chosen = jnp.sum(hot * logits, -1, keepdims=True)
    loss_ref[...] = jnp.broadcast_to(jnp.sum(weight * (log_total - chosen), 0, keepdims=True), loss_ref.shape)
    d_logits = (jnp.exp(logits - log_total) - hot) * (weight / count_ref[0])
    gbias_ref[...] = jnp.sum(d_logits, 0, keepdims=True)
    dl = d_logits.astype(BF16)
    d_rows = ndot(dl, table_ref[...])
    high = d_rows.astype(BF16)
    rest = (d_rows - high.astype(F32)).astype(BF16)
    for i in range(own):
        part = slice(i * slot_count, (i + 1) * slot_count)
        grad_ref[i * length : (i + 1) * length, :] = tdot(picks[i], high[part]) + tdot(picks[i], rest[part])
    d_z2, d_gain, d_shift = norm_back(normed2_ref[...], inverse2_ref[...], vec_ref[6:7, :], grad_ref[...])
    dz_ref[...] = d_z2
    dzb_ref[...] = d_z2.astype(BF16)
    gvec_ref[0:1, :] = jnp.sum(d_z2, 0, keepdims=True)
    gvec_ref[1:2, :] = d_gain
    gvec_ref[2:3, :] = d_shift
    full_ref[...] = tdot(rows, dl).astype(BF16)
    for k, out in enumerate((keep_ref.at[0], send_ref.at[0], keep_ref.at[1], send_ref.at[1])):
        out[...] = full_ref[pl.ds(pl.multiple_of((member ^ k) * columns, 64), columns), :]


def down_send_kernel(dzb_ref, a1, a3, s1, s3, send_ref, left_ref):
    first = dzb_ref.shape[1]
    dzb = dzb_ref[...]
    for n, (active, start) in enumerate(((a1[...], s1), (a3[...], s3))):
        send_ref[n] = tdot(active, dzb).astype(BF16)
        left_ref[n] = panel(start[:8, first : 2 * first], dzb, active)


def close(n, grad, near_ref, err_ref, far_refs, part_ref):
    if n == 0:
        part_ref[...] = grad + near_ref[0].astype(F32) + err_ref[...]
    else:
        total = (grad + near_ref[1].astype(F32)).astype(BF16)
        size = total.shape[0] // len(far_refs)
        for place, far_ref in enumerate(far_refs):
            far_ref[...] = total[place * size : (place + 1) * size]


def down_keep_kernel(dzb_ref, a0, a2, s0, s2, near_ref, err_ref, far_ref, part_ref, left_ref):
    first = dzb_ref.shape[1]
    dzb = dzb_ref[...]
    for n, (active, start) in ((1, (a2[...], s2)), (0, (a0[...], s0))):
        close(n, tdot(active, dzb), near_ref, err_ref, (far_ref,), part_ref)
        left_ref[n] = panel(start[:8, first : 2 * first], dzb, active)
    left_ref[0] += wide(ndot, s0[:8, first : 2 * first], err_ref[...])


def up_one(dzb, h1b, slope, up, down, start, hidden_ref, dpre_ref):
    step = 256
    for at in range(0, down.shape[0], step):
        d_pre = ndot(dzb, down[at : at + step, :]) * slope[:, at : at + step]
        hidden_ref[:, at : at + step] = jnp.sum(d_pre, 0, keepdims=True)
        dpre_ref[:, at : at + step] = d_pre.astype(BF16)
    d_pre = dpre_ref[...]
    return tdot(h1b, d_pre), ndot(d_pre, up[...]), panel(start[:8, : d_pre.shape[1]], d_pre, h1b)


def up_send_kernel(
    meta_ref, dzb_ref, h1b_ref, p1, p3, s1, s3, u1, u3a, u3b, d1, d3a, d3b,
    send_ref, left_ref, dh_ref, hidden_ref, dpre_ref, w_ref, sems,
):
    fetch = Fetch(meta_ref, sems)
    pieces = ((d1,), (u1,), (d3a, d3b), (u3a, u3b))
    copies = [fetch.block(piece, w_ref.at[n]) for n, piece in enumerate(pieces)]
    dzb, h1b = dzb_ref[...], h1b_ref[...]
    for n, (slope, start) in enumerate(((p1, s1), (p3, s3))):
        wait(copies[2 * n] + copies[2 * n + 1])
        grad, part, left_ref[n] = up_one(
            dzb, h1b, slope, w_ref.at[2 * n + 1], w_ref.at[2 * n], start, hidden_ref.at[n], dpre_ref
        )
        send_ref[n] = grad.astype(BF16)
        dh_ref[...] = part if n == 0 else dh_ref[...] + part


def up_keep_kernel(
    meta_ref, dz_ref, dzb_ref, h1b_ref, normed1_ref, inverse1_ref, vec_ref, dh_ref, p0, p2, s0, s2,
    near_ref, err_ref, u0, u2a, u2b, d0, d2a, d2b,
    far_a, far_b, part_ref, left_ref, dz1_ref, dz1b_ref, gvec_ref, hidden_ref, dpre_ref, w_ref, sems,
):
    fetch = Fetch(meta_ref, sems)
    pieces = ((d0,), (u0,), (d2a, d2b), (u2a, u2b))
    copies = [fetch.block(piece, w_ref.at[n]) for n, piece in enumerate(pieces)]
    dzb, h1b = dzb_ref[...], h1b_ref[...]
    for n, (slope, start) in ((1, (p2, s2)), (0, (p0, s0))):
        wait(copies[2 * n] + copies[2 * n + 1])
        grad, part, left_ref[n] = up_one(
            dzb, h1b, slope, w_ref.at[2 * n + 1], w_ref.at[2 * n], start, hidden_ref.at[n], dpre_ref
        )
        close(n, grad, near_ref, err_ref, (far_a, far_b), part_ref)
        dz1_ref[...] = part + (dz_ref[...] + dh_ref[...] if n == 1 else dz1_ref[...])
    left_ref[0] += wide(ndot, s0[:8, : err_ref.shape[1]], err_ref[...])
    d_z1, d_gain, d_shift = norm_back(normed1_ref[...], inverse1_ref[...], vec_ref[3:4, :], dz1_ref[...])
    dz1_ref[...] = d_z1
    dz1b_ref[...] = d_z1.astype(BF16)
    gvec_ref[0:1, :] = jnp.sum(d_z1, 0, keepdims=True)
    gvec_ref[1:2, :] = d_gain
    gvec_ref[2:3, :] = d_shift


def attention_back_one(length, dz, hb, w_ref, qkv_ref, lse_ref, ctx_ref, start_ref, pack_ref, dm_ref, dc_ref):
    width, features = ctx_ref.shape[1], dz.shape[1]
    used = 3 * width
    dc_ref[...] = ndot(dz, w_ref[used:, :]).astype(BF16)
    ctx = ctx_ref[...]
    out_grad = tdot(ctx, dz)
    pack_ref[:8, 3 * features :] = panel(start_ref[:8, 2 * features : 3 * features], dz, ctx)
    q_sum = jnp.zeros((1, width), F32)
    v_sum = jnp.zeros((1, width), F32)
    for image in range(dz.shape[0] // length):
        rows = slice(image * length, (image + 1) * length)
        q, k, v, dc = qkv_ref[0, rows, :], qkv_ref[1, rows, :], qkv_ref[2, rows, :], dc_ref[rows, :]
        d_query = jnp.zeros((length, width), F32)
        d_key = jnp.zeros((length, width), F32)
        d_value = jnp.zeros((length, width), F32)
        for head in range(width // HD):
            mask = head_mask(width, head)
            q_head, k_head, c_head = q * mask, k * mask, dc * mask
            probs = jnp.exp(ndot(q_head, k) - lse_ref[rows, head : head + 1])
            d_value = d_value + tdot(probs.astype(BF16), c_head)
            d_probs = ndot(c_head, v)
            inner = jnp.sum(d_probs * probs, -1, keepdims=True)
            d_scores = (probs * (d_probs - inner)).astype(BF16)
            d_query = d_query + bdot(d_scores, k_head)
            d_key = d_key + tdot(d_scores, q_head)
        d_query = d_query * HD ** (-0.5)
        q_sum = q_sum + jnp.sum(d_query, 0, keepdims=True)
        v_sum = v_sum + jnp.sum(d_value, 0, keepdims=True)
        dm_ref[rows, :width] = d_query.astype(BF16)
        dm_ref[rows, width : 2 * width] = d_key.astype(BF16)
        dm_ref[rows, 2 * width :] = d_value.astype(BF16)
    pack_ref[8:9, :width] = q_sum
    pack_ref[8:9, width : 2 * width] = v_sum
    dm = dm_ref[...]
    pack_ref[:8, 2 * features : 3 * features] = panel(start_ref[:8, 3 * features : 3 * features + dm_ref.shape[1]], dm, hb)
    return tdot(dm, hb), out_grad, bdot(dm, w_ref[:used, :])


def pack_rows(pack_ref, width, up, down, hidden):
    features = up.shape[1]
    pack_ref[...] = jnp.zeros_like(pack_ref)
    pack_ref[:8, :features] = up
    pack_ref[:8, features : 2 * features] = down
    pack_ref[8:9, 2 * width : 2 * width + features] = hidden


def pack_whole(pack_ref, vectors, bias, loss):
    pack_ref[9:10, : bias.shape[1]] = bias
    features = vectors[0].shape[1]
    for n, vector in enumerate(vectors + [loss]):
        row, place = 10 + n // 3, n % 3
        pack_ref[row : row + 1, place * features : place * features + vector.shape[1]] = vector


def attention_send_kernel(
    length, meta_ref, dz1b_ref, hb_ref, q1, q3, l1, l3, x1, x3, s1, s3, up_ref, down_ref, hidden_ref,
    c1, c3a, c3b, send_ref, pack_ref, dh_ref, dm_ref, dc_ref, w_ref, sems,
):
    fetch = Fetch(meta_ref, sems)
    copies = [fetch.block((c1,), w_ref.at[0]), fetch.block((c3a, c3b), w_ref.at[1])]
    dz, hb = dz1b_ref[...], hb_ref[...]
    used = dm_ref.shape[1]
    for n, (q, l, x, start) in enumerate(((q1, l1, x1, s1), (q3, l3, x3, s3))):
        wait(copies[n])
        pack_rows(pack_ref.at[n], x.shape[1], up_ref[n], down_ref[n], hidden_ref[n])
        qkv_grad, out_grad, part = attention_back_one(
            length, dz, hb, w_ref.at[n], q, l, x, start, pack_ref.at[n], dm_ref, dc_ref
        )
        send_ref[n, :used, :] = qkv_grad.astype(BF16)
        send_ref[n, used:, :] = out_grad.astype(BF16)
        dh_ref[...] = part if n == 0 else dh_ref[...] + part


def attention_keep_kernel(
    length, meta_ref, dz1b_ref, hb_ref, q0, q2, l0, l2, x0, x2, s0, s2, up_ref, down_ref, hidden_ref,
    near_ref, err_qkv, err_out, dz1_ref, dha_ref, normed_ref, inverse_ref, vec_ref, gvec1_ref, gvec2_ref, gbias_ref,
    loss_ref, send_pack_ref, c0, c2a, c2b,
    far_ref, part_ref, pack_ref, send_ref, d_far, d_near, d_own, dm_ref, dc_ref, dh_ref, w_ref, sems,
):
    fetch = Fetch(meta_ref, sems)
    copies = [fetch.block((c0,), w_ref.at[0]), fetch.block((c2a, c2b), w_ref.at[1])]
    dz, hb = dz1b_ref[...], hb_ref[...]
    used, width = dm_ref.shape[1], x0.shape[1]
    features = hb.shape[1]
    for n, (q, l, x, start) in ((1, (q2, l2, x2, s2)), (0, (q0, l0, x0, s0))):
        wait(copies[n])
        pack_rows(pack_ref.at[n], width, up_ref[n], down_ref[n], hidden_ref[n])
        qkv_grad, out_grad, part = attention_back_one(
            length, dz, hb, w_ref.at[n], q, l, x, start, pack_ref.at[n], dm_ref, dc_ref
        )
        if n == 0:
            part_ref[:used, :] = qkv_grad + near_ref[0, :used, :].astype(F32) + err_qkv[...]
            part_ref[used:, :] = out_grad + near_ref[0, used:, :].astype(F32) + err_out[...]
        else:
            far_ref[:used, :] = (qkv_grad + near_ref[1, :used, :].astype(F32)).astype(BF16)
            far_ref[used:, :] = (out_grad + near_ref[1, used:, :].astype(F32)).astype(BF16)
        dh_ref[...] = part + (dha_ref[...] + dz1_ref[...] if n == 1 else dh_ref[...])
    pack_ref[0, :8, 2 * features : 3 * features] += wide(bdot, s0[:8, 3 * features : 3 * features + used], err_qkv[...])
    pack_ref[0, :8, 3 * features :] += wide(ndot, s0[:8, 2 * features : 3 * features], err_out[...])
    d_x, d_gain, d_shift = norm_back(normed_ref[...], inverse_ref[...], vec_ref[0:1, :], dh_ref[...])
    vectors = [d_gain, d_shift] + [gvec1_ref[i : i + 1, :] for i in range(3)] + [gvec2_ref[i : i + 1, :] for i in range(3)]
    send_ref[...] = send_pack_ref[...]
    for ref in (send_ref.at[0], send_ref.at[1], pack_ref.at[0], pack_ref.at[1]):
        pack_whole(ref, vectors, gbias_ref[...], loss_ref[...])
    dh_ref[...] = d_x
    rows, columns = d_own.shape
    for t in range(4):

        @pl.when(meta_ref[0] == t)
        def _():
            for k, out in enumerate((d_own, d_near, d_far.at[0], d_far.at[1])):
                out[...] = dh_ref[:, (t ^ k) * columns : ((t ^ k) + 1) * columns].astype(BF16)


def scatter_kernel(own, vocab, ids_ref, r0, r1, r2, r3, near_ref, keep_ref, far_ref, out_ref):
    length = ids_ref.shape[0]
    total = out_ref.shape[1]
    lane = lax.broadcasted_iota(jnp.int32, (1, total), 1)
    position = lax.broadcasted_iota(jnp.int32, (length, 1), 0) + vocab
    result = keep_ref[0].astype(F32) + near_ref[0].astype(F32) + far_ref[...].astype(F32)
    for k, rows in enumerate((r0[...], r1[...], r2[0], r3[1])):
        hots = []
        for i in range(own):
            ids = ids_ref[:, k * own + i : k * own + i + 1]
            hots.append(jnp.where((ids == lane) | (position == lane), 1.0, 0.0).astype(BF16))
        result = result + tdot(rows, jnp.concatenate(hots, 0))
    out_ref[...] = result.astype(out_ref.dtype)


def joined(refs):
    parts = [ref[...].astype(F32) for ref in refs]
    return parts[0] if len(parts) == 1 else jnp.concatenate(parts, 0)


def right_mlp_kernel(part_d, got_d, part_u, got_a, got_b, base_ref, rest_ref, out_ref):
    size = part_d.shape[1]
    rows = part_d.shape[0]
    for n, (part, gots) in enumerate(((part_u, (got_a, got_b)), (part_d, (got_d,)))):
        merged = part[...] + joined(gots)
        out_ref[:, n * size : (n + 1) * size] = wide(bdot, base_ref[:, n * rows : (n + 1) * rows], merged)
    out_ref[:, 2 * size :] = rest_ref[...]


def right_attention_kernel(used, part, got, base_ref, out_ref):
    features = part.shape[1]
    out_ref[:, :features] = wide(bdot, base_ref[:, 3 * features :], part[used:, :] + got[used:, :].astype(F32))
    merged = part[:used, :] + got[:used, :].astype(F32)
    out_ref[:, features:] = wide(ndot, base_ref[:, 2 * features : 3 * features], merged)


def update_kernel(replicas, part, weight, moment, first_ref, second_ref, *refs):
    gots, (weight_new, moment_new, error_new) = refs[:-3], refs[-3:]
    first, second = split3(first_ref[...] * (1.0 / replicas)), split3(second_ref[...])
    rank = first.shape[0] // 3
    parts = lambda x, order: jnp.concatenate([x[i * rank : (i + 1) * rank].astype(F32) for i in order], 0).astype(BF16)
    approx = tdot(parts(first, (0, 0, 1, 0, 2, 1)), parts(second, (0, 1, 0, 2, 0, 1)))
    new = BETA * moment[...] + approx
    moment_new[...] = new
    weight_new[...] = weight[...].astype(F32) - RATE_MAT * new
    error_new[...] = part[...] + joined(gots) - approx


def update(replicas, part, gots, first_row, weight, moment, first, second):
    rows, cols = weight.shape
    block = 256
    spec = pl.BlockSpec((rows, block), lambda i: (0, i))
    out = shape(rows, cols)
    mine = lambda size: pl.BlockSpec((size, block), lambda i: (first_row // size, i))
    return call(
        functools.partial(update_kernel, replicas), "update", (out, out, out),
        (part, weight, moment, first, second, *gots),
        [mine(rows), spec, spec, pl.BlockSpec(first.shape, lambda i: (0, 0)),
         pl.BlockSpec((second.shape[0], block), lambda i: (0, i))] + [mine(rows // len(gots))] * len(gots),
        out_specs=[spec] * 3, grid=(cols // block,),
    )


def orthonormal_kernel(sizes, panel_ref, out_ref):
    rank = panel_ref.shape[0]
    place = lax.broadcasted_iota(jnp.int32, (rank, 1), 0)
    cuts = [sum(sizes[:i]) for i in range(len(sizes) + 1)]
    panels = [panel_ref[:, a:b] for a, b in zip(cuts, cuts[1:])]
    for number in range(rank):
        for which, (a, b) in enumerate(zip(cuts, cuts[1:])):
            part = panels[which]
            column = part[number : number + 1, :]
            column = column * lax.rsqrt(jnp.sum(column * column, -1, keepdims=True) + 1e-20)
            out_ref[number : number + 1, a:b] = column
            if number + 1 < rank:
                along = jnp.sum(part * column, -1, keepdims=True)
                panels[which] = part - jnp.where(place > number, along, 0.0) * column


class Order:
    def __init__(self):
        self.last = None

    def __call__(self, x):
        if self.last is not None:
            x = tie(x, self.last)
        self.last = x
        return x

    def mark(self, x):
        self.last = x


def exchange(x, bit):
    return across(x, "dp", bit)


class RowSum:
    def __init__(self, x, bits):
        self.x, self.bits, self.step = x, bits, 0
        self.steps = bits[:2] + bits[2:] + bits[1::-1]
        self.place = lax.axis_index("dp")

    def send(self):
        step, bit, x = self.step, self.steps[self.step], self.x
        self.upper = (self.place & bit) != 0
        if step < 2:
            half = x.shape[0] // 2
            x = jnp.where(self.upper, x[:half], x[half:])
        self.got = across(x, "dp", bit)

    def receive(self, order):
        step, x, upper = self.step, self.x, self.upper
        got = order(self.got)
        if step < 2:
            half = x.shape[0] // 2
            x = (jnp.where(upper, x[half:], x[:half]).astype(F32) + got.astype(F32)).astype(BF16)
        elif step < len(self.bits):
            x = (x.astype(F32) + got.astype(F32)).astype(BF16)
        else:
            x = jnp.concatenate([jnp.where(upper, got, x), jnp.where(upper, x, got)], 0)
        self.x = x
        self.step += 1
        return self.step < len(self.steps)


class WholeSum:
    def __init__(self, x, bits):
        self.x, self.steps, self.step = x, bits, 0

    def send(self):
        self.got = across(self.x, "dp", self.steps[self.step])

    def receive(self, order):
        self.x = self.x + order(self.got)
        self.step += 1
        return self.step < len(self.steps)


def advance(order, *sums):
    for one in sums:
        if one.step < len(one.steps) and one.receive(order):
            one.send()


def shards(
    token_ids, masked_at, live_counts, tables, table_mom, vec_whole, vec_mom, vec_split, split_mom,
    head_bias, bias_mom, w_qkv, w_out, w_up, w_down, mom_qkv, mom_out, mom_up, mom_down,
    err_qkv, err_out, err_up, err_down, start_qkv, start_out, start_up, start_down,
):
    groups = lax.axis_size("tensor")
    replicas = lax.axis_size("dp")
    images, length = token_ids.shape
    vocab = head_bias.shape[0]
    total_rows, columns = tables.shape
    features = w_qkv.shape[0]
    width = w_qkv.shape[1] // 3
    hidden = w_up.shape[1]
    own = images // groups
    rows = own * length
    rank = start_qkv.shape[1]
    total = total_rows + -total_rows % 128
    used = 3 * width
    all_rows = used + width
    bits = [1 << i for i in range(replicas.bit_length() - 1)]
    meta = jnp.stack([lax.axis_index("tensor"), lax.axis_index("dp") & 1]).astype(jnp.int32)
    order = Order()

    bf = functools.partial(shape, dtype=BF16)
    dma = lambda n: pltpu.SemaphoreType.DMA((n,))
    vm = lambda *dims: pltpu.VMEM(dims, BF16)

    def cores(pieces):
        return tuple(core_swap(piece) for piece in pieces)

    first_own, first_half, up_half, down_half, table_own, table_half = call(
        pack_kernel, "pack",
        (bf(all_rows, features), bf(all_rows // 2, features), bf(features // 2, hidden), bf(hidden // 2, features),
         bf(columns, total), bf(columns // 2, total)),
        (meta, w_qkv.T, w_out, w_up, w_down, tables.T), [SMEM] + [ANY] * 4 + [VMEM], [dma(4)],
    )
    order.mark(first_half)
    first_far = [chip_swap(first_half)]
    part = bf(columns, rows + length)
    e_far, e_near, e_own, ids_rows = call(
        functools.partial(embed_kernel, own, vocab), "embed",
        (bf(2, columns, rows + length // 2), part, part, shape(length, images, dtype=jnp.int32)),
        (meta, live_counts, token_ids, masked_at, order(table_own)), [SMEM, SMEM, VMEM, VMEM, VMEM],
    )
    order.mark(e_far)
    first_near, up_near, down_near, table_near = cores((first_own, w_up, w_down, table_own))
    own_starts = jnp.concatenate((start_up.T, start_down.T, start_out.T, start_qkv.T), 1)
    gap = -own_starts.shape[1] % 128
    bias_row = jnp.pad(vec_split, ((0, rank - 1), (gap, 0)))
    small = [jnp.concatenate([own_starts, bias_row], 1)]
    small.append(core_swap(small[0]))
    e_one = core_swap(e_near)
    e_two = chip_swap(e_far)
    first_far[0] = order(first_far[0])
    first_far.append(exchange(first_far[0], 1))
    count = WholeSum(tie(jnp.broadcast_to(jnp.sum(live_counts).astype(F32), (8, 128)), first_far[0]), bits)
    count.send()
    e_two = order(e_two)
    up_far = [chip_swap(tie(up_half, e_two))]
    small.append(chip_swap(tie(small[0], e_two)))
    e_three = core_swap(e_two)
    advance(order, count)
    starts = splits = small

    state = (shape(rows, features), shape(rows, 1), bf(rows, features))
    block = (bf(3, rows, width), shape(rows, width // HD), bf(rows, width))
    res = call(
        functools.partial(attention_first_kernel, length), "attention_first", state + block + block,
        (tie(meta, up_near, down_near, first_near, table_near), order(e_own), e_one, e_two, e_three, vec_whole,
         small[0], small[1], first_own, first_near),
        [SMEM] + [VMEM] * 7 + [ANY] * 2, [pltpu.VMEM((features, rows), F32), vm(2, used, features), dma(2)],
    )
    normed0, inverse0, h0b = res[:3]
    order.mark(h0b)
    kept = [res[3:6], res[6:9]]
    small[2] = order(small[2])
    first_far[1] = order(first_far[1])
    first_both = cores([tie(x, first_far[1]) for x in first_far])
    small.append(core_swap(small[2]))
    up_far[0] = order(up_far[0])
    down_far = [chip_swap(tie(down_half, up_far[0]))]
    up_far.append(exchange(up_far[0], 1))
    advance(order, count)
    res = call(
        functools.partial(attention_second_kernel, length), "attention_second", state + block + block,
        (meta, order(normed0), h0b, vec_whole, splits[2], splits[3], kept[0][2], kept[1][2], first_own, first_near,
         *first_far, *first_both),
        [SMEM] + [VMEM] * 7 + [ANY] * 6, [vm(2, all_rows, features), vm(2, width, features), dma(6)],
    )
    normed1, inverse1, h1b = res[:3]
    order.mark(h1b)
    kept += [res[3:6], res[6:9]]
    while count.step < len(bits):
        advance(order, count)
    act = bf(rows, hidden)
    slope = shape(rows, hidden)
    a0, a1, p0, p1, low = call(
        mlp_first_kernel, "mlp_first", (act, act, slope, slope, shape(rows, features)),
        (meta, order(h1b), splits[0], splits[1], w_up, up_near, w_down, down_near),
        [SMEM] + [VMEM] * 3 + [ANY] * 4, [vm(4, features, hidden), dma(4)],
    )
    order.mark(low)
    down_far[0] = order(down_far[0])
    down_far.append(exchange(down_far[0], 1))
    table_far = [chip_swap(tie(table_half, down_far[0]))]
    up_far[1] = order(up_far[1])
    up_both = cores([tie(x, up_far[1]) for x in up_far])
    table_far[0] = order(table_far[0])
    table_far.append(exchange(table_far[0], 1))
    down_far[1] = order(down_far[1])
    down_both = cores([tie(x, down_far[1]) for x in down_far])
    a2, a3, p2, p3, normed2, inverse2, h2b = call(
        mlp_second_kernel, "mlp_second", (act, act, slope, slope) + state,
        (meta, order(h1b), splits[2], splits[3], low, normed1, vec_whole, *up_far, *up_both, *down_far, *down_both),
        [SMEM] + [VMEM] * 6 + [ANY] * 8, [vm(4, features, hidden), dma(8)],
    )
    order.mark(h2b)
    table_far[1] = order(table_far[1])
    table_both = cores([tie(x, table_far[1]) for x in table_far])
    count = count.x[0, :1]
    pair = lambda a, b, dtype: shape(2, a, b, dtype=dtype)
    dz2, dz2b, loss_part, g_bias, g_vec2, head_send, head_keep = call(
        functools.partial(head_kernel, own, vocab), "head",
        (
            shape(rows, features), bf(rows, features), shape(1, 128), shape(1, total),
            shape(3, features), pair(columns, total, BF16), pair(columns, total, BF16),
        ),
        (
            meta, live_counts, count, token_ids, masked_at,
            jnp.pad(head_bias, (0, total - vocab)).reshape(1, total), vec_whole, order(h2b), normed2, inverse2,
            table_own, table_near, *table_far, *table_both,
        ),
        [SMEM] * 3 + [VMEM] * 7 + [ANY] * 6,
        [vm(features, total), vm(features, total), pltpu.VMEM((rows, features), F32), dma(6)],
    )
    order.mark(dz2b)

    head_near = core_swap(head_send)
    left = shape(2, rank, features)
    down_send, left_down_a = call(
        down_send_kernel, "down_send", (pair(hidden, features, BF16), left),
        (order(dz2b), a1, a3, starts[1], starts[3]),
    )
    order.mark(down_send)
    down_got = core_swap(down_send)
    head_far = order((head_keep[1].astype(F32) + head_near[1].astype(F32)).astype(BF16))
    head_in = chip_swap(head_far)
    up_send, left_up_a, dh_a, hidden_a = call(
        up_send_kernel, "up_send",
        (pair(features, hidden, BF16), left, shape(rows, features), shape(2, 1, hidden)),
        (meta, order(dz2b), h1b, p1, p3, starts[1], starts[3], up_near, *up_both, down_near, *down_both),
        [SMEM] + [VMEM] * 6 + [ANY] * 6, [vm(rows, hidden), vm(4, features, hidden), dma(6)],
    )
    order.mark(dh_a)
    up_got = core_swap(up_send)
    down_far_grad, down_part, left_down_b = call(
        down_keep_kernel, "down_keep", (bf(hidden, features), shape(hidden, features), left),
        (order(dz2b), a0, a2, starts[0], starts[2], down_got, err_down[0]),
    )
    order.mark(left_down_b)
    down_in = chip_swap(down_far_grad)
    up_a, up_b, up_part, left_up_b, dz1, dz1b, g_vec1, hidden_b = call(
        up_keep_kernel, "up_keep",
        (bf(features // 2, hidden), bf(features // 2, hidden), shape(features, hidden), left, shape(rows, features), bf(rows, features),
         shape(3, features), shape(2, 1, hidden)),
        (meta, dz2, order(dz2b), h1b, normed1, inverse1, vec_whole, dh_a, p0, p2, starts[0], starts[2],
         up_got, err_up[0], w_up, *up_far, w_down, *down_far),
        [SMEM] + [VMEM] * 13 + [ANY] * 6, [vm(rows, hidden), vm(4, features, hidden), dma(6)],
    )
    order.mark(dz1b)
    pack_width = 3 * features + width
    pack = shape(2, 16, pack_width)
    scratch = [vm(rows, used), vm(rows, width)]
    first_send, pack_a, dh_b = call(
        functools.partial(attention_send_kernel, length), "attention_send",
        (pair(all_rows, features, BF16), pack, shape(rows, features)),
        (meta, order(dz1b), h0b, kept[1][0], kept[3][0], kept[1][1], kept[3][1], kept[1][2], kept[3][2],
         starts[1], starts[3], left_up_a, left_down_a, hidden_a, first_near, *first_both),
        [SMEM] + [VMEM] * 13 + [ANY] * 3, scratch + [vm(2, all_rows, features), dma(3)],
    )
    order.mark(dh_b)
    head_in, down_in = order(head_in), order(down_in)
    first_got = core_swap(tie(first_send, down_in))
    up_in_a = chip_swap(tie(up_a, down_in))
    cols = bf(rows, columns)
    first_far_grad, first_part, pack_b, pack_a, d_far, d_near, d_own = call(
        functools.partial(attention_keep_kernel, length), "attention_keep",
        (bf(all_rows, features), shape(all_rows, features), pack, pack, pair(rows, columns, BF16), cols, cols),
        (meta, order(dz1b), h0b, kept[0][0], kept[2][0], kept[0][1], kept[2][1], kept[0][2], kept[2][2],
         starts[0], starts[2], left_up_b, left_down_b, hidden_b, first_got, err_qkv[0].T, err_out[0],
         dz1, dh_b, normed0, inverse0, vec_whole, g_vec1, g_vec2, g_bias, loss_part, pack_a,
         first_own, *first_far),
        [SMEM] + [VMEM] * 26 + [ANY] * 3,
        scratch + [pltpu.VMEM((rows, features), F32), vm(2, all_rows, features), dma(3)],
    )
    order.mark(d_far)

    d_two = chip_swap(d_far)
    up_in_a = order(up_in_a)
    up_in_b = chip_swap(tie(up_b, up_in_a))
    mine = order(pack_b + core_swap(tie(pack_a, up_in_a)))
    d_one = core_swap(tie(d_near, up_in_a))
    mine_in = chip_swap(mine[1])
    mine = order(mine[0] + mine_in)
    panels = WholeSum(mine[:8], bits)
    panels.send()
    advance(order, panels)
    d_two = order(d_two)
    d_three = core_swap(d_two)
    first_in = chip_swap(tie(first_far_grad, d_two))
    advance(order, panels)
    table_grad = call(
        functools.partial(scatter_kernel, own, vocab), "scatter", bf(columns, total),
        (ids_rows, order(d_own), d_one, d_two, d_three, head_near, head_keep, head_in),
    )
    order.mark(table_grad)
    cut = columns // 2
    table_sums = (
        RowSum(table_grad[:cut], [bits[1], bits[0]] + bits[2:]), RowSum(table_grad[cut:], bits),
    )
    for one in table_sums:
        one.send()
    while panels.step < len(bits):
        advance(order, panels)
    sizes = (features, features, features, width)
    bases = call(
        functools.partial(orthonormal_kernel, sizes), "orthonormal", shape(rank, pack_width), (order(panels.x),),
    )
    order.mark(bases)
    packed = call(
        right_mlp_kernel, "right_mlp", shape(rank, 2 * features + pack_width),
        (down_part, down_in, up_part, up_in_a, order(up_in_b), bases, mine[8:]),
    )
    packed = WholeSum(packed, bits)
    packed.send()
    for _ in range(2):
        advance(order, *table_sums, packed)
    rights = call(
        functools.partial(right_attention_kernel, used), "right_attention", shape(rank, features + used),
        (first_part, order(first_in), bases),
    )
    order.mark(rights)
    rights = WholeSum(rights, bits)
    rights.send()
    while packed.step < len(bits):
        advance(order, *table_sums, packed)
    base_up, base_down = bases[:, :features], bases[:, features : 2 * features]
    base_qkv, base_out = bases[:, 2 * features : 3 * features], bases[:, 3 * features :]
    right_up, right_down = packed.x[:, :features], packed.x[:, features : 2 * features]
    rest = packed.x[:, 2 * features :]
    down = update(replicas, down_part, [down_in], 0, w_down, mom_down, order(base_down), right_down)
    order.mark(down[0])
    advance(order, *table_sums, rights)
    up = update(replicas, up_part, [up_in_a, up_in_b], 0, w_up, mom_up, order(base_up), right_up)
    order.mark(up[0])
    while rights.step < len(bits) or table_sums[1].step < len(table_sums[1].steps):
        advance(order, *table_sums, rights)
    right_out, right_qkv = rights.x[:, :features], rights.x[:, features:]
    out = update(replicas, first_part, [first_in], used, w_out, mom_out, base_out, right_out)
    qkv = update(replicas, first_part, [first_in], 0, w_qkv.T, mom_qkv.T, right_qkv, base_qkv)

    table_grad = jnp.concatenate([one.x for one in table_sums], 0)[:, :total_rows].astype(F32)
    vectors = [rest[2 + n // 3, n % 3 * features : (n % 3 + 1) * features] for n in range(8)]
    results = [jnp.stack([rest[4, 2 * features], count[0]])]

    def momentum_step(weight, moment, grad, rate):
        new_moment = BETA * moment + grad
        return (weight.astype(F32) - rate * new_moment, new_moment)

    new = momentum_step(tables.T, table_mom.T, table_grad, RATE_TAB)
    results += [new[0].T, new[1].T]
    results += momentum_step(vec_whole, vec_mom, jnp.stack(vectors), RATE_VEC)
    results += momentum_step(vec_split, split_mom, rest[0:1, : vec_split.shape[1]], RATE_VEC)
    results += momentum_step(head_bias, bias_mom, rest[1, :vocab], RATE_VEC)
    one = 1.0 / replicas
    for (weight, moment, error), base, right, flip in (
        (qkv, base_qkv, right_qkv, True), (out, base_out, right_out, False),
        (up, base_up, right_up, False), (down, base_down, right_down, False),
    ):
        if flip:
            weight, moment, error = weight.T, moment.T, error.T
        results += [weight, moment, error[None], base.T[None], right.T * one]
    return tuple(results)


def solution(mesh):
    rows, cols = P("tensor", None), P(None, "tensor")
    batch = P("dp", None)
    in_specs = (
        batch, batch, P("dp"), cols, cols, P(), P(), rows, rows, P(), P(),
        cols, rows, cols, rows, cols, rows, cols, rows,
        P("dp", None, "tensor"), P("dp", "tensor", None), P("dp", None, "tensor"), P("dp", "tensor", None),
        rows, rows, rows, rows,
    )
    left = P("tensor", None, None)
    out_specs = (P(), cols, cols, P(), P(), rows, rows, P(), P())
    for side in (cols, rows, cols, rows):
        out_specs += (side, side, P("dp", *side), left, rows)
    return jax.shard_map(shards, mesh=mesh, in_specs=in_specs, out_specs=out_specs, check_vma=False)
```

profile of v0, /device:TPU:0, one launch (start us, length us, event | category | flops | bytes accessed | tf_op | source)
XLA Modules:
  0.0 295.6 jit_solution(2154496564195635291)
XLA Ops:
  1.9 4.9 %pack.1 = (bf16[768,768]{1,0:T(8,128)(2,1)}, bf16[384,768]{1,0:T(8,128)(2,1)}, bf16[384,768]{1,0:T(8,128)(2,1)}, bf16[384,768]{1,0:T(8,128)(2,1)}, bf16[192,2304]{1,0:T(8,128)(2,1)}, /*index=5*/bf16[96,2304]{1,0:T(8,128)(2,1)}) custom-call(s32[2]{0:T(128)} %pad_add_fusion.meta_ref, bf16[576,768]{1,0:T(8,128)(2,1)} %bitcast.71, bf16[192,768]{1,0:T(8,128)(2,1)} %weight.5, ...), custom_call_target="tpu_custom_call" | custom-call | flops 34500001792 | bytes 30000000 | tf_op jit(solution)/shard_map/pack/pallas_call | solution.py:72
  6.8 3.0 %collective-permute-start = (bf16[384,768]{1,0:T(8,128)(2,1)}, bf16[384,768]{1,0:T(8,128)(2,1)}, u32[]{:S(2)}, u32[]{:S(2)}) collective-permute-start(bf16[384,768]{1,0:T(8,128)(2,1)} %get-tuple-element.192), channel_id=1, source_target_pairs={{0,2},{1,3},{2,0},{3,1},{4,6},{5,7},{6,4},{7,5},{8,10},{9,11},{10,... | collective-permute-start | bytes 1769480 | tf_op jit(solution)/shard_map/ppermute | solution.py:36
  11.5 5.1 %embed.1 = (bf16[2,192,640]{2,1,0:T(8,128)(2,1)}, bf16[192,768]{1,0:T(8,128)(2,1)S(1)}, bf16[192,768]{1,0:T(8,128)(2,1)S(1)}, s32[256,8]{1,0:T(8,128)S(1)}) custom-call(s32[2]{0:T(128)S(1)} %copy-done.49, s32[8]{0:T(128)S(1)} %copy-done.47, s32[8,256]{1,0:T(8,128)S(1)} %copy-done.43, s32[8,128]{1,0:T(8,128)S(1)} %copy-done.45, bf16[192,2304]{1,0:T(8,128)(2,1)S(1)} %copy-done.22), custom_call_target="tpu_custom_call" | custom-call | flops 57500000256 | bytes 50000000 | tf_op jit(solution)/shard_map/embed/pallas_call | solution.py:72
  18.6 5.0 %collective-permute-done.c2a = bf16[384,768]{1,0:T(8,128)(2,1)} collective-permute-done((bf16[384,768]{1,0:T(8,128)(2,1)}, bf16[384,768]{1,0:T(8,128)(2,1)}, u32[]{:S(2)}, u32[]{:S(2)}) %collective-permute-start) | collective-permute-done | bytes 589856 | tf_op jit(solution)/shard_map/ppermute | solution.py:36
  26.7 10.0 %collective-permute-done.2.e2 = bf16[2,192,640]{2,1,0:T(8,128)(2,1)} collective-permute-done((bf16[2,192,640]{2,1,0:T(8,128)(2,1)}, bf16[2,192,640]{2,1,0:T(8,128)(2,1)}, u32[]{:S(2)}, u32[]{:S(2)}) %collective-permute-start.2) | collective-permute-done | bytes 491552 | tf_op jit(solution)/shard_map/ppermute | solution.py:36
  45.6 7.5 %attention_first.1 = (f32[512,768]{1,0:T(8,128)S(1)}, f32[512,1]{1,0:T(8,128)S(1)}, bf16[512,768]{1,0:T(8,128)(2,1)S(1)}, bf16[3,512,192]{2,1,0:T(8,128)(2,1)S(1...) custom-call(s32[2]{0:T(128)S(1)} %copy-done.49, ...), custom_call_target="tpu_custom_call" | custom-call | flops 80499998720 | bytes 70000000 | tf_op jit(solution)/shard_map/attention_first/pallas_call | solution.py:72
  53.8 3.2 %collective-permute-done.5.c2b = bf16[384,768]{1,0:T(8,128)(2,1)S(1)} collective-permute-done((bf16[384,768]{1,0:T(8,128)(2,1)}, bf16[384,768]{1,0:T(8,128)(2,1)S(1)}, u32[]{:S(2)}, u32[]{:S(2)}) %collective-permute-start.5) | collective-permute-done | bytes 589856 | tf_op jit(solution)/shard_map/ppermute | solution.py:36
  61.5 2.6 collective-permute-start.14
  65.6 8.7 %attention_second.1 = (f32[512,768]{1,0:T(8,128)S(1)}, f32[512,1]{1,0:T(8,128)S(1)}, bf16[512,768]{1,0:T(8,128)(2,1)S(1)}, bf16[3,512,192]{2,1,0:T(8,128)(2,1)S(...) custom-call(s32[2]{0:T(128)S(1)} %copy-done.49, ...), custom_call_target="tpu_custom_call" | custom-call | flops 92000002048 | bytes 80000000 | tf_op jit(solution)/shard_map/attention_second/pallas_call | solution.py:72
  74.5 6.4 %mlp_first.1 = (bf16[512,768]{1,0:T(8,128)(2,1)S(1)}, bf16[512,768]{1,0:T(8,128)(2,1)S(1)}, f32[512,768]{1,0:T(8,128)S(1)}, f32[512,768]{1,0:T(8,128)S(1)}, f32[512,768]{1,0:T(8,128)S(1)}) custom-call(s32[2]{0:T(128)S(1)} %copy-done.49, bf16[512,768]{1,0:T(8,128)(2,1)S(1)} %get-tuple-element.231.h1b_ref, f32[8,4096]{1,0:T(8,128)S(1)} %concatenate.12.b0.s0, ...), custom_call_target="tpu_custom_call" | custom-call | flops 80499998720 | bytes 70000000 | tf_op jit(solution)/shard_map/mlp_first/pallas_call | solution.py:72
  83.6 9.2 %collective-permute-done.20.t2a = bf16[96,2304]{1,0:T(8,128)(2,1)S(1)} collective-permute-done((bf16[96,2304]{1,0:T(8,128)(2,1)S(1)}, bf16[96,2304]{1,0:T(8,128)(2,1)S(1)}, u32[]{:S(2)}, u32[]{:S(2)}) %collective-permute-start.20) | collective-permute-done | bytes 442400 | tf_op jit(solution)/shard_map/ppermute | solution.py:36
  92.8 2.4 collective-permute-done.19.d2b
  98.4 7.6 %mlp_second.1 = (bf16[512,768]{1,0:T(8,128)(2,1)S(1)}, bf16[512,768]{1,0:T(8,128)(2,1)S(1)}, f32[512,768]{1,0:T(8,128)S(1)}, f32[512,768]{1,0:T(8,128)S(1)}, f32...) custom-call(s32[2]{0:T(128)S(1)} %copy-done.49, ...), custom_call_target="tpu_custom_call" | custom-call | flops 80499998720 | bytes 70000000 | tf_op jit(solution)/shard_map/mlp_second/pallas_call | solution.py:72
  110.3 8.9 %head.1 = (f32[512,768]{1,0:T(8,128)S(1)}, bf16[512,768]{1,0:T(8,128)(2,1)S(1)}, f32[1,128]{1,0:T(1,128)S(1)}, f32[1,2304]{1,0:T(1,128)S(1)}, f32[3,768]{1,0:T(4...) custom-call(s32[2]{0:T(128)S(1)} %copy-done.49, s32[8]{0:T(128)S(1)} %copy-done.48, ...), custom_call_target="tpu_custom_call" | custom-call | flops 103499997184 | bytes 90000000 | tf_op jit(solution)/shard_map/head/pallas_call | solution.py:72
  125.0 7.3 %up_send.1 = (bf16[2,768,768]{2,1,0:T(8,128)(2,1)S(1)}, f32[2,8,768]{2,1,0:T(8,128)S(1)}, f32[512,768]{1,0:T(8,128)S(1)}, f32[2,1,768]{2,1,0:T(1,128)S(1)}) custom-call(s32[2]{0:T(128)S(1)} %copy-done.49, bf16[512,768]{1,0:T(8,128)(2,1)S(1)} %get-tuple-element.263.dzb_ref, bf16[512,768]{1,0:T(8,128)(2,1)S(1)} %get-tuple-element.231.h1b_ref, ...), custom_call_target="tpu_custom_call" | custom-call | flops 69000003584 | bytes 60000000 | tf_op jit(solution)/shard_map/up_send/pallas_call | solution.py:72
  132.5 3.3 %down_keep.1 = (bf16[768,768]{1,0:T(8,128)(2,1)}, f32[768,768]{1,0:T(8,128)S(1)}, f32[2,8,768]{2,1,0:T(8,128)S(1)}) custom-call(bf16[512,768]{1,0:T(8,128)(2,1)S(1)} %get-tuple-element.263.dzb_ref, bf16[512,768]{1,0:T(8,128)(2,1)S(1)} %get-tuple-element.257.a0, bf16[512,768]{1,0:T(8,128)(2,1)S(1)} %get-tuple-element.258.a2, ...), custom_call_target="tpu_custom_call" | custom-call | flops 46000001024 | bytes 40000000 | tf_op jit(solution)/shard_map/down_keep/pallas_call | solution.py:72
  138.9 10.1 %up_keep.1 = (bf16[384,768]{1,0:T(8,128)(2,1)}, bf16[384,768]{1,0:T(8,128)(2,1)S(1)}, f32[768,768]{1,0:T(8,128)S(1)}, f32[2,8,768]{2,1,0:T(8,128)S(1)}, f32[512,...) custom-call(s32[2]{0:T(128)S(1)} %copy-done.49, ...), custom_call_target="tpu_custom_call" | custom-call | flops 92000002048 | bytes 80000000 | tf_op jit(solution)/shard_map/up_keep/pallas_call | solution.py:72
  149.2 12.2 %attention_send.1 = (bf16[2,768,768]{2,1,0:T(8,128)(2,1)S(1)}, f32[2,16,2496]{2,1,0:T(8,128)S(1)}, f32[512,768]{1,0:T(8,128)S(1)}) custom-call(s32[2]{0:T(128)S(1)} %copy-done.49, bf16[512,768]{1,0:T(8,128)(2,1)S(1)} %get-tuple-element.284.dz1b_ref, bf16[512,768]{1,0:T(8,128)(2,1)S(1)} %copy-done.68, bf16[3,512,192]{2,1,0:T(8,128)(2,1)S(1)} %get-tuple-element.270.q1, ...), custom_call_target="tpu_custom_call" | custom-call | flops 149500002304 | bytes 130000000 | tf_op jit(solution)/shard_map/attention_send/pallas_call | solution.py:72
  161.4 10.3 %collective-permute-done.31.got_d.refs_0_ = bf16[768,768]{1,0:T(8,128)(2,1)} collective-permute-done((bf16[768,768]{1,0:T(8,128)(2,1)}, bf16[768,768]{1,0:T(8,128)(2,1)}, u32[]{:S(2)}, u32[]{:S(2)}) %collective-permute-start.31) | collective-permute-done | bytes 1179680 | tf_op jit(solution)/shard_map/ppermute | solution.py:36
  172.3 4.0 %collective-permute-done.35.near_ref = bf16[2,768,768]{2,1,0:T(8,128)(2,1)S(1)} collective-permute-done((bf16[2,768,768]{2,1,0:T(8,128)(2,1)S(1)}, bf16[2,768,768]{2,1,0:T(8,128)(2,1)S(1)}, u32[]{:S(2)}, u32[]{:S(2)}) %collective-permute-start.35) | collective-permute-done | bytes 2359328 | tf_op jit(solution)/shard_map/ppermute | solution.py:36
  176.3 15.3 %attention_keep.1 = (bf16[768,768]{1,0:T(8,128)(2,1)S(1)}, f32[768,768]{1,0:T(8,128)S(1)}, f32[2,16,2496]{2,1,0:T(8,128)S(1)}, f32[2,16,2496]{2,1,0:T(8,128)S(1)...) custom-call(s32[2]{0:T(128)S(1)} %copy-done.49, ...), custom_call_target="tpu_custom_call" | custom-call | flops 172499992576 | bytes 150000000 | tf_op jit(solution)/shard_map/attention_keep/pallas_call | solution.py:72
  196.9 5.0 %collective-permute-done.38 = f32[16,2496]{1,0:T(8,128)S(1)} collective-permute-done((f32[16,2496]{1,0:T(8,128)S(1)}, f32[16,2496]{1,0:T(8,128)S(1)}, u32[]{:S(2)}, u32[]{:S(2)}) %collective-permute-start.38) | collective-permute-done | bytes 159776 | tf_op jit(solution)/shard_map/ppermute | solution.py:36
  203.2 3.3 %collective-permute-done.39 = f32[8,2496]{1,0:T(8,128)S(1)} collective-permute-done((f32[8,2496]{1,0:T(8,128)S(1)}, f32[8,2496]{1,0:T(8,128)S(1)}, u32[]{:S(2)}, u32[]{:S(2)}) %collective-permute-start.39) | collective-permute-done | bytes 79904 | tf_op jit(solution)/shard_map/ppermute | solution.py:36
  206.5 5.9 %collective-permute-done.41.r2 = bf16[2,512,192]{2,1,0:T(8,128)(2,1)S(1)} collective-permute-done((bf16[2,512,192]{2,1,0:T(8,128)(2,1)S(1)}, bf16[2,512,192]{2,1,0:T(8,128)(2,1)S(1)}, u32[]{:S(2)}, u32[]{:S(2)}) %collective-permute-start.41) | collective-permute-done | bytes 393248 | tf_op jit(solution)/shard_map/ppermute | solution.py:36
  222.9 4.1 %scatter.1 = bf16[192,2304]{1,0:T(8,128)(2,1)S(1)} custom-call(s32[256,8]{1,0:T(8,128)S(1)} %copy-done.62, bf16[512,192]{1,0:T(8,128)(2,1)S(1)} %copy-done.60, bf16[512,192]{1,0:T(8,128)(2,1)} %collective-permute-done.43.r1, bf16[2,512,192]{2,1,0:T(8,128)(2,1)S(1)} %collective-permute-done.41.r2, bf16[2,512,192]{2,1,0:T(8,128)(2,1)} %collective-permute-done.44.r3, ...), custom_call_target="tpu_custom_call" | custom-call | flops 5750000128 | bytes 5000000 | tf_op jit(solution)/shard_map/scatter/pallas_call | solution.py:72
  231.3 2.7 right_mlp.1
  241.5 2.7 collective-permute-start.52
  248.7 6.9 %collective-permute-done.54.got.refs_0_ = bf16[768,768]{1,0:T(8,128)(2,1)S(1)} collective-permute-done((bf16[768,768]{1,0:T(8,128)(2,1)S(1)}, bf16[768,768]{1,0:T(8,128)(2,1)S(1)}, u32[]{:S(2)}, u32[]{:S(2)}) %collective-permute-start.54) | collective-permute-done | bytes 1179680 | tf_op jit(solution)/shard_map/ppermute | solution.py:36
  266.8 4.9 %update.4 = (f32[768,768]{1,0:T(8,128)}, f32[768,768]{1,0:T(8,128)}, f32[768,768]{1,0:T(8,128)}) custom-call(f32[768,768]{1,0:T(8,128)S(1)} %copy-done.58, bf16[768,768]{1,0:T(8,128)(2,1)S(1)} %copy-done.14, f32[768,768]{1,0:T(8,128)S(1)} %copy-done.8, f32[8,768]{1,0:T(8,128)S(1)} %get-tuple-element.334.first_ref, ...), custom_call_target="tpu_custom_call" | custom-call | flops 4600000000 | bytes 4000000 | tf_op jit(solution)/shard_map/update/pallas_call | solution.py:72
  277.0 4.7 %update.5 = (f32[768,768]{1,0:T(8,128)}, f32[768,768]{1,0:T(8,128)}, f32[768,768]{1,0:T(8,128)}) custom-call(f32[768,768]{1,0:T(8,128)S(1)} %copy-done.55, bf16[768,768]{1,0:T(8,128)(2,1)S(1)} %copy-done.17, f32[768,768]{1,0:T(8,128)S(1)} %copy-done.9, f32[8,768]{1,0:T(8,128)S(1)} %get-tuple-element.339.first_ref, ...), custom_call_target="tpu_custom_call" | custom-call | flops 4600000000 | bytes 4000000 | tf_op jit(solution)/shard_map/update/pallas_call | solution.py:72
  289.8 2.2 update.7
  292.0 3.4 %update.6 = (f32[576,768]{1,0:T(8,128)}, f32[576,768]{1,0:T(8,128)}, f32[576,768]{1,0:T(8,128)}) custom-call(f32[768,768]{1,0:T(8,128)S(1)} %copy-done.52, bf16[576,768]{1,0:T(8,128)(2,1)S(1)} %bitcast.72, f32[576,768]{1,0:T(8,128)S(1)} %bitcast.70, f32[8,576]{1,0:T(8,128)S(1)} %get-tuple-element.400.first_ref, f32[8,768]{1,0:T(8,128)S(1)} %get-tuple-element.392.second_ref, ...), custom_call_target="tpu_custom_call" | custom-call | flops 4600000000 | bytes 4000000 | tf_op jit(solution)/shard_map/update/pallas_call | solution.py:72
  (383 shorter events, 100.1 us)
Async XLA Ops:
  0.7 40.3 %collective-permute-start.7 = (bf16[768,768]{1,0:T(8,128)(2,1)}, bf16[768,768]{1,0:T(8,128)(2,1)}, u32[]{:S(2)}, u32[]{:S(2)}) collective-permute-start(bf16[768,768]{1,0:T(8,128)(2,1)} %weight.4), channel_id=1, source_target_pairs={{0,1},{1,0},{2,3},{3,2},{4,5},{5,4},{6,7},{7,6},{8,9},{9,8},{10,11... | collective-permute-start | bytes 3538952 | tf_op jit(solution)/shard_map/ppermute | solution.py:36
  1.2 39.9 %collective-permute-start.8 = (bf16[768,768]{1,0:T(8,128)(2,1)}, bf16[768,768]{1,0:T(8,128)(2,1)}, u32[]{:S(2)}, u32[]{:S(2)}) collective-permute-start(bf16[768,768]{1,0:T(8,128)(2,1)} %weight.3), channel_id=1, source_target_pairs={{0,1},{1,0},{2,3},{3,2},{4,5},{5,4},{6,7},{7,6},{8,9},{9,8},{10,11... | collective-permute-start | bytes 3538952 | tf_op jit(solution)/shard_map/ppermute | solution.py:36
  6.8 16.9 %collective-permute-start = (bf16[384,768]{1,0:T(8,128)(2,1)}, bf16[384,768]{1,0:T(8,128)(2,1)}, u32[]{:S(2)}, u32[]{:S(2)}) collective-permute-start(bf16[384,768]{1,0:T(8,128)(2,1)} %get-tuple-element.192), channel_id=1, source_target_pairs={{0,2},{1,3},{2,0},{3,1},{4,6},{5,7},{6,4},{7,5},{8,10},{9,11},{10,... | collective-permute-start | bytes 1769480 | tf_op jit(solution)/shard_map/ppermute | solution.py:36
  9.7 30.5 %collective-permute-start.10 = (bf16[192,2304]{1,0:T(8,128)(2,1)}, bf16[192,2304]{1,0:T(8,128)(2,1)S(1)}, u32[]{:S(2)}, u32[]{:S(2)}) collective-permute-start(bf16[192,2304]{1,0:T(8,128)(2,1)} %get-tuple-element.194.table_ref.t0), channel_id=1, source_target_pairs={{0,1},{1,0},{2,3},{3,2},{4,5},{5,4},{6,7},{7,6},{8,9},{9,8},{10,11... | collective-permute-start | bytes 2654216 | tf_op jit(solution)/shard_map/ppermute | solution.py:36
  9.7 32.8 %collective-permute-start.9 = (bf16[768,768]{1,0:T(8,128)(2,1)}, bf16[768,768]{1,0:T(8,128)(2,1)S(1)}, u32[]{:S(2)}, u32[]{:S(2)}) collective-permute-start(bf16[768,768]{1,0:T(8,128)(2,1)} %get-tuple-element.203.c0), channel_id=1, source_target_pairs={{0,1},{1,0},{2,3},{3,2},{4,5},{5,4},{6,7},{7,6},{8,9},{9,8},{10,11... | collective-permute-start | bytes 3538952 | tf_op jit(solution)/shard_map/ppermute | solution.py:36
  23.6 13.0 %collective-permute-start.2 = (bf16[2,192,640]{2,1,0:T(8,128)(2,1)}, bf16[2,192,640]{2,1,0:T(8,128)(2,1)}, u32[]{:S(2)}, u32[]{:S(2)}) collective-permute-start(bf16[2,192,640]{2,1,0:T(8,128)(2,1)} %get-tuple-element.195), channel_id=1, source_target_pairs={{0,2},{1,3},{2,0},{3,1},{4,6},{5,7},{6,4},{7,5},{8,10},{9,11},{10,... | collective-permute-start | bytes 1474568 | tf_op jit(solution)/shard_map/ppermute | solution.py:36
  41.0 15.9 %collective-permute-start.5 = (bf16[384,768]{1,0:T(8,128)(2,1)}, bf16[384,768]{1,0:T(8,128)(2,1)S(1)}, u32[]{:S(2)}, u32[]{:S(2)}) collective-permute-start(bf16[384,768]{1,0:T(8,128)(2,1)} %collective-permute-done.c2a), channel_id=1, source_target_pairs={{0,4},{4,0},{8,12},{12,8},{16,20},{20,16},{24,28},{28,24},{1,5},{5... | collective-permute-start | bytes 1769480 | tf_op jit(solution)/shard_map/ppermute | solution.py:36
  42.6 11.2 %collective-permute-start.6 = (f32[8,4096]{1,0:T(8,128)S(1)}, f32[8,4096]{1,0:T(8,128)S(1)}, u32[]{:S(2)}, u32[]{:S(2)}) collective-permute-start(f32[8,4096]{1,0:T(8,128)S(1)} %concatenate.12.b0.s0), channel_id=1, source_target_pairs={{0,2},{1,3},{2,0},{3,1},{4,6},{5,7},{6,4},{7,5},{8,10},{9,11},{10,... | collective-permute-start | bytes 393224 | tf_op jit(solution)/shard_map/ppermute | solution.py:36
  44.1 16.8 %collective-permute-start.4 = (bf16[384,768]{1,0:T(8,128)(2,1)}, bf16[384,768]{1,0:T(8,128)(2,1)}, u32[]{:S(2)}, u32[]{:S(2)}) collective-permute-start(bf16[384,768]{1,0:T(8,128)(2,1)} %get-tuple-element.201), channel_id=1, source_target_pairs={{0,2},{1,3},{2,0},{3,1},{4,6},{5,7},{6,4},{7,5},{8,10},{9,11},{10,... | collective-permute-start | bytes 1769480 | tf_op jit(solution)/shard_map/ppermute | solution.py:36
  60.9 22.2 %collective-permute-start.21 = (bf16[384,768]{1,0:T(8,128)(2,1)}, bf16[384,768]{1,0:T(8,128)(2,1)}, u32[]{:S(2)}, u32[]{:S(2)}) collective-permute-start(bf16[384,768]{1,0:T(8,128)(2,1)} %collective-permute-done.4.u2a), channel_id=1, source_target_pairs={{0,4},{4,0},{8,12},{12,8},{16,20},{20,16},{24,28},{28,24},{1,5},{5... | collective-permute-start | bytes 1769480 | tf_op jit(solution)/shard_map/ppermute | solution.py:36
  61.5 13.0 %collective-permute-start.14 = (f32[8,128]{1,0:T(8,128)S(1)}, f32[8,128]{1,0:T(8,128)S(1)}, u32[]{:S(2)}, u32[]{:S(2)}) collective-permute-start(f32[8,128]{1,0:T(8,128)S(1)} %add.81), channel_id=1, source_target_pairs={{0,16},{4,20},{8,24},{12,28},{16,0},{20,4},{24,8},{28,12},{1,17},{... | collective-permute-start | bytes 12296 | tf_op jit(solution)/shard_map/ppermute | solution.py:36
  64.0 16.9 %collective-permute-start.18 = (bf16[384,768]{1,0:T(8,128)(2,1)}, bf16[384,768]{1,0:T(8,128)(2,1)}, u32[]{:S(2)}, u32[]{:S(2)}) collective-permute-start(bf16[384,768]{1,0:T(8,128)(2,1)} %get-tuple-element.222), channel_id=1, source_target_pairs={{0,2},{1,3},{2,0},{3,1},{4,6},{5,7},{6,4},{7,5},{8,10},{9,11},{10,... | collective-permute-start | bytes 1769480 | tf_op jit(solution)/shard_map/ppermute | solution.py:36
  81.0 14.3 %collective-permute-start.19 = (bf16[384,768]{1,0:T(8,128)(2,1)}, bf16[384,768]{1,0:T(8,128)(2,1)S(1)}, u32[]{:S(2)}, u32[]{:S(2)}) collective-permute-start(bf16[384,768]{1,0:T(8,128)(2,1)} %collective-permute-done.18.d2a), channel_id=1, source_target_pairs={{0,4},{4,0},{8,12},{12,8},{16,20},{20,16},{24,28},{28,24},{1,5},{5... | collective-permute-start | bytes 1769480 | tf_op jit(solution)/shard_map/ppermute | solution.py:36
  82.5 10.3 %collective-permute-start.20 = (bf16[96,2304]{1,0:T(8,128)(2,1)S(1)}, bf16[96,2304]{1,0:T(8,128)(2,1)S(1)}, u32[]{:S(2)}, u32[]{:S(2)}) collective-permute-start(bf16[96,2304]{1,0:T(8,128)(2,1)S(1)} %copy-done.108), channel_id=1, source_target_pairs={{0,2},{1,3},{2,0},{3,1},{4,6},{5,7},{6,4},{7,5},{8,10},{9,11},{10,... | collective-permute-start | bytes 1327112 | tf_op jit(solution)/shard_map/ppermute | solution.py:36
  83.1 13.9 %collective-permute-start.22 = (bf16[384,768]{1,0:T(8,128)(2,1)}, bf16[384,768]{1,0:T(8,128)(2,1)S(1)}, u32[]{:S(2)}, u32[]{:S(2)}) collective-permute-start(bf16[384,768]{1,0:T(8,128)(2,1)} %collective-permute-done.4.u2a), channel_id=1, source_target_pairs={{0,1},{1,0},{2,3},{3,2},{4,5},{5,4},{6,7},{7,6},{8,9},{9,8},{10,11... | collective-permute-start | bytes 1769480 | tf_op jit(solution)/shard_map/ppermute | solution.py:36
  83.1 13.9 %collective-permute-start.23 = (bf16[384,768]{1,0:T(8,128)(2,1)}, bf16[384,768]{1,0:T(8,128)(2,1)S(1)}, u32[]{:S(2)}, u32[]{:S(2)}) collective-permute-start(bf16[384,768]{1,0:T(8,128)(2,1)} %collective-permute-done.21.u2b), channel_id=1, source_target_pairs={{0,1},{1,0},{2,3},{3,2},{4,5},{5,4},{6,7},{7,6},{8,9},{9,8},{10,11... | collective-permute-start | bytes 1769480 | tf_op jit(solution)/shard_map/ppermute | solution.py:36
  95.8 12.1 %collective-permute-start.26 = (bf16[96,2304]{1,0:T(8,128)(2,1)S(1)}, bf16[96,2304]{1,0:T(8,128)(2,1)S(1)}, u32[]{:S(2)}, u32[]{:S(2)}) collective-permute-start(bf16[96,2304]{1,0:T(8,128)(2,1)S(1)} %collective-permute-done.20.t2a), channel_id=1, source_target_pairs={{0,4},{4,0},{8,12},{12,8},{16,20},{20,16},{24,28},{28,24},{1,5},{5... | collective-permute-start | bytes 1327112 | tf_op jit(solution)/shard_map/ppermute | solution.py:36
  121.5 10.9 %collective-permute-start.30 = (bf16[2,768,768]{2,1,0:T(8,128)(2,1)S(1)}, bf16[2,768,768]{2,1,0:T(8,128)(2,1)S(1)}, u32[]{:S(2)}, u32[]{:S(2)}) collective-permute-start(bf16[2,768,768]{2,1,0:T(8,128)(2,1)S(1)} %get-tuple-element.250), channel_id=1, source_target_pairs={{0,1},{1,0},{2,3},{3,2},{4,5},{5,4},{6,7},{7,6},{8,9},{9,8},{10,11... | collective-permute-start | bytes 7077896 | tf_op jit(solution)/shard_map/ppermute | solution.py:36
  124.5 37.0 %collective-permute-start.32 = (bf16[192,2304]{1,0:T(8,128)(2,1)}, bf16[192,2304]{1,0:T(8,128)(2,1)}, u32[]{:S(2)}, u32[]{:S(2)}) collective-permute-start(bf16[192,2304]{1,0:T(8,128)(2,1)} %fusion.1), channel_id=1, source_target_pairs={{0,2},{1,3},{2,0},{3,1},{4,6},{5,7},{6,4},{7,5},{8,10},{9,11},{10,... | collective-permute-start | bytes 2654216 | tf_op jit(solution)/shard_map/ppermute | solution.py:36
  137.2 34.5 %collective-permute-start.31 = (bf16[768,768]{1,0:T(8,128)(2,1)}, bf16[768,768]{1,0:T(8,128)(2,1)}, u32[]{:S(2)}, u32[]{:S(2)}) collective-permute-start(bf16[768,768]{1,0:T(8,128)(2,1)} %get-tuple-element.260), channel_id=1, source_target_pairs={{0,2},{1,3},{2,0},{3,1},{4,6},{5,7},{6,4},{7,5},{8,10},{9,11},{10,... | collective-permute-start | bytes 3538952 | tf_op jit(solution)/shard_map/ppermute | solution.py:36
  171.7 21.4 %collective-permute-start.34 = (bf16[384,768]{1,0:T(8,128)(2,1)}, bf16[384,768]{1,0:T(8,128)(2,1)}, u32[]{:S(2)}, u32[]{:S(2)}) collective-permute-start(bf16[384,768]{1,0:T(8,128)(2,1)} %get-tuple-element.283), channel_id=1, source_target_pairs={{0,2},{1,3},{2,0},{3,1},{4,6},{5,7},{6,4},{7,5},{8,10},{9,11},{10,... | collective-permute-start | bytes 1769480 | tf_op jit(solution)/shard_map/ppermute | solution.py:36
  195.4 16.9 %collective-permute-start.41 = (bf16[2,512,192]{2,1,0:T(8,128)(2,1)S(1)}, bf16[2,512,192]{2,1,0:T(8,128)(2,1)S(1)}, u32[]{:S(2)}, u32[]{:S(2)}) collective-permute-start(bf16[2,512,192]{2,1,0:T(8,128)(2,1)S(1)} %get-tuple-element.301), channel_id=1, source_target_pairs={{0,2},{1,3},{2,0},{3,1},{4,6},{5,7},{6,4},{7,5},{8,10},{9,11},{10,... | collective-permute-start | bytes 1179656 | tf_op jit(solution)/shard_map/ppermute | solution.py:36
  203.2 16.3 %collective-permute-start.43 = (bf16[512,192]{1,0:T(8,128)(2,1)}, bf16[512,192]{1,0:T(8,128)(2,1)}, u32[]{:S(2)}, u32[]{:S(2)}) collective-permute-start(bf16[512,192]{1,0:T(8,128)(2,1)} %get-tuple-element.317), channel_id=1, source_target_pairs={{0,1},{1,0},{2,3},{3,2},{4,5},{5,4},{6,7},{7,6},{8,9},{9,8},{10,11... | collective-permute-start | bytes 589832 | tf_op jit(solution)/shard_map/ppermute | solution.py:36
  214.6 16.7 %collective-permute-start.36 = (bf16[384,768]{1,0:T(8,128)(2,1)}, bf16[384,768]{1,0:T(8,128)(2,1)S(1)}, u32[]{:S(2)}, u32[]{:S(2)}) collective-permute-start(bf16[384,768]{1,0:T(8,128)(2,1)} %copy-done.34), channel_id=1, source_target_pairs={{0,2},{1,3},{2,0},{3,1},{4,6},{5,7},{6,4},{7,5},{8,10},{9,11},{10,... | collective-permute-start | bytes 1769480 | tf_op jit(solution)/shard_map/ppermute | solution.py:36
  215.1 40.4 %collective-permute-start.54 = (bf16[768,768]{1,0:T(8,128)(2,1)S(1)}, bf16[768,768]{1,0:T(8,128)(2,1)S(1)}, u32[]{:S(2)}, u32[]{:S(2)}) collective-permute-start(bf16[768,768]{1,0:T(8,128)(2,1)S(1)} %get-tuple-element.329), channel_id=1, source_target_pairs={{0,2},{1,3},{2,0},{3,1},{4,6},{5,7},{6,4},{7,5},{8,10},{9,11},{10,... | collective-permute-start | bytes 3538952 | tf_op jit(solution)/shard_map/ppermute | solution.py:36
  241.5 15.6 %collective-permute-start.52 = (bf16[24,2304]{1,0:T(8,128)(2,1)S(1)}, bf16[24,2304]{1,0:T(8,128)(2,1)S(1)}, u32[]{:S(2)}, u32[]{:S(2)}) collective-permute-start(bf16[24,2304]{1,0:T(8,128)(2,1)S(1)} %add_convert_fusion.6), channel_id=1, source_target_pairs={{0,16},{4,20},{8,24},{12,28},{16,0},{20,4},{24,8},{28,12},{1,17},{... | collective-permute-start | bytes 331784 | tf_op jit(solution)/shard_map/ppermute | solution.py:36
  244.2 12.9 %collective-permute-start.53 = (bf16[24,2304]{1,0:T(8,128)(2,1)S(1)}, bf16[24,2304]{1,0:T(8,128)(2,1)S(1)}, u32[]{:S(2)}, u32[]{:S(2)}) collective-permute-start(bf16[24,2304]{1,0:T(8,128)(2,1)S(1)} %add_convert_fusion.5), channel_id=1, source_target_pairs={{0,16},{4,20},{8,24},{12,28},{16,0},{20,4},{24,8},{28,12},{1,17},{... | collective-permute-start | bytes 331784 | tf_op jit(solution)/shard_map/ppermute | solution.py:36
  246.5 11.9 %collective-permute-start.51 = (f32[8,4032]{1,0:T(8,128)S(1)}, f32[8,4032]{1,0:T(8,128)S(1)}, u32[]{:S(2)}, u32[]{:S(2)}) collective-permute-start(f32[8,4032]{1,0:T(8,128)S(1)} %add.92), channel_id=1, source_target_pairs={{0,16},{4,20},{8,24},{12,28},{16,0},{20,4},{24,8},{28,12},{1,17},{... | collective-permute-start | bytes 387080 | tf_op jit(solution)/shard_map/ppermute | solution.py:36
  259.7 14.1 %collective-permute-start.57 = (f32[8,1344]{1,0:T(8,128)S(1)}, f32[8,1344]{1,0:T(8,128)S(1)}, u32[]{:S(2)}, u32[]{:S(2)}) collective-permute-start(f32[8,1344]{1,0:T(8,128)S(1)} %right_attention.1), channel_id=1, source_target_pairs={{0,4},{4,0},{8,12},{12,8},{16,20},{20,16},{24,28},{28,24},{1,5},{5... | collective-permute-start | bytes 129032 | tf_op jit(solution)/shard_map/ppermute | solution.py:36
  261.4 12.3 %collective-permute-start.58 = (bf16[24,2304]{1,0:T(8,128)(2,1)S(1)}, bf16[24,2304]{1,0:T(8,128)(2,1)S(1)}, u32[]{:S(2)}, u32[]{:S(2)}) collective-permute-start(bf16[24,2304]{1,0:T(8,128)(2,1)S(1)} %add_convert_fusion.3), channel_id=1, source_target_pairs={{0,8},{4,12},{8,0},{12,4},{16,24},{20,28},{24,16},{28,20},{1,9},{5... | collective-permute-start | bytes 331784 | tf_op jit(solution)/shard_map/ppermute | solution.py:36
  261.4 12.3 %collective-permute-start.55 = (bf16[24,2304]{1,0:T(8,128)(2,1)S(1)}, bf16[24,2304]{1,0:T(8,128)(2,1)S(1)}, u32[]{:S(2)}, u32[]{:S(2)}) collective-permute-start(bf16[24,2304]{1,0:T(8,128)(2,1)S(1)} %add_convert_fusion.4), channel_id=1, source_target_pairs={{0,4},{4,0},{8,12},{12,8},{16,20},{20,16},{24,28},{28,24},{1,5},{5... | collective-permute-start | bytes 331784 | tf_op jit(solution)/shard_map/ppermute | solution.py:36
  273.8 9.2 %collective-permute-start.60 = (f32[8,1344]{1,0:T(8,128)S(1)}, f32[8,1344]{1,0:T(8,128)S(1)}, u32[]{:S(2)}, u32[]{:S(2)}) collective-permute-start(f32[8,1344]{1,0:T(8,128)S(1)} %add.102), channel_id=1, source_target_pairs={{0,8},{4,12},{8,0},{12,4},{16,24},{20,28},{24,16},{28,20},{1,9},{5... | collective-permute-start | bytes 129032 | tf_op jit(solution)/shard_map/ppermute | solution.py:36
  (139 other events, 1410.9 us)
where the time goes:
time: 300 us; the launch traced here: 296 us
  Pallas kernels  123 us (41%)
  waiting for transfers between devices  87.2 us (29%)
  starting transfers between devices  51.9 us (17%)
  local copies, waits for them, and re-layouts  17.3 us (6%)
  other arithmetic  12.9 us (4%)
  between operations  3 us (1%)
    pallas_call x21, Pallas kernels, call(): pl.pallas_call(kernel, out_shape=out_shape, in_specs=in_specs, scratch_sh...  123 us
    ppermute x62, waiting for transfers between devices, across(): return lax.ppermute(x, axis, [(i, i ^ bit) for i in range(size)])  87.2 us
    ppermute x62, starting transfers between devices, across(): return lax.ppermute(x, axis, [(i, i ^ bit) for i in range(size)])  51.9 us
    unnamed x218, local copies, waits for them, and re-layouts  14.8 us
  transfers between devices with their start and end apart: 62, of which 28 were waited for; matrix products, arithmetic and copies ran while one was open for 4% of the time, Pallas kernels for 37%

commit v1 on v0

--- a/solution.py
+++ b/solution.py
@@ -426,16 +426,17 @@
         part_ref[...] = grad + near_ref[0].astype(F32) + err_ref[...]
     else:
         total = (grad + near_ref[1].astype(F32)).astype(BF16)
-        size = total.shape[0] // len(far_refs)
-        for place, far_ref in enumerate(far_refs):
-            far_ref[...] = total[place * size : (place + 1) * size]
-
-
-def down_keep_kernel(dzb_ref, a0, a2, s0, s2, near_ref, err_ref, far_ref, part_ref, left_ref):
+        first = 0
+        for far_ref in far_refs:
+            far_ref[...] = total[first : first + far_ref.shape[0]]
+            first += far_ref.shape[0]
+
+
+def down_keep_kernel(dzb_ref, a0, a2, s0, s2, near_ref, err_ref, far_a, far_b, part_ref, left_ref):
     first = dzb_ref.shape[1]
     dzb = dzb_ref[...]
     for n, (active, start) in ((1, (a2[...], s2)), (0, (a0[...], s0))):
-        close(n, tdot(active, dzb), near_ref, err_ref, (far_ref,), part_ref)
+        close(n, tdot(active, dzb), near_ref, err_ref, (far_a, far_b), part_ref)
         left_ref[n] = panel(start[:8, first : 2 * first], dzb, active)
     left_ref[0] += wide(ndot, s0[:8, first : 2 * first], err_ref[...])
 
@@ -469,9 +470,11 @@
 
 def up_keep_kernel(
     meta_ref, dz_ref, dzb_ref, h1b_ref, normed1_ref, inverse1_ref, vec_ref, dh_ref, p0, p2, s0, s2,
-    near_ref, err_ref, u0, u2a, u2b, d0, d2a, d2b,
+    near_ref, err_ref, other_ref, u0, u2a, u2b, d0, d2a, d2b,
     far_a, far_b, part_ref, left_ref, dz1_ref, dz1b_ref, gvec_ref, hidden_ref, dpre_ref, w_ref, sems,
 ):
+    other = other_ref.shape[0]
+    far_a[:other, :] = other_ref[...]
     fetch = Fetch(meta_ref, sems)
     pieces = ((d0,), (u0,), (d2a, d2b), (u2a, u2b))
     copies = [fetch.block(piece, w_ref.at[n]) for n, piece in enumerate(pieces)]
@@ -481,7 +484,7 @@
         grad, part, left_ref[n] = up_one(
             dzb, h1b, slope, w_ref.at[2 * n + 1], w_ref.at[2 * n], start, hidden_ref.at[n], dpre_ref
         )
-        close(n, grad, near_ref, err_ref, (far_a, far_b), part_ref)
+        close(n, grad, near_ref, err_ref, (far_a.at[pl.ds(other, far_a.shape[0] - other), :], far_b), part_ref)
         dz1_ref[...] = part + (dz_ref[...] + dh_ref[...] if n == 1 else dz1_ref[...])
     left_ref[0] += wide(ndot, s0[:8, : err_ref.shape[1]], err_ref[...])
     d_z1, d_gain, d_shift = norm_back(normed1_ref[...], inverse1_ref[...], vec_ref[3:4, :], dz1_ref[...])
@@ -626,10 +629,12 @@
     return parts[0] if len(parts) == 1 else jnp.concatenate(parts, 0)
 
 
-def right_mlp_kernel(part_d, got_d, part_u, got_a, got_b, base_ref, rest_ref, out_ref):
+def right_mlp_kernel(part_d, got_c, both, part_u, got_b, base_ref, rest_ref, out_ref):
     size = part_d.shape[1]
     rows = part_d.shape[0]
-    for n, (part, gots) in enumerate(((part_u, (got_a, got_b)), (part_d, (got_d,)))):
+    rest = rows - got_c.shape[0]
+    got_d, got_a = both.at[pl.ds(0, rest), :], both.at[pl.ds(rest, both.shape[0] - rest), :]
+    for n, (part, gots) in enumerate(((part_u, (got_a, got_b)), (part_d, (got_c, got_d)))):
         merged = part[...] + joined(gots)
         out_ref[:, n * size : (n + 1) * size] = wide(bdot, base_ref[:, n * rows : (n + 1) * rows], merged)
     out_ref[:, 2 * size :] = rest_ref[...]
@@ -660,16 +665,19 @@
     spec = pl.BlockSpec((rows, block), lambda i: (0, i))
     out = shape(rows, cols)
     mine = lambda size: pl.BlockSpec((size, block), lambda i: (first_row // size, i))
+    rows_of = lambda size, first: pl.BlockSpec((size, block), lambda i: (first, i))
+    own = [mine(rows)] if len(gots) == 1 else [rows_of(*got[1:]) for got in gots]
+    gots = gots if len(gots) == 1 else [got[0] for got in gots]
     return call(
         functools.partial(update_kernel, replicas), "update", (out, out, out),
         (part, weight, moment, first, second, *gots),
         [mine(rows), spec, spec, pl.BlockSpec(first.shape, lambda i: (0, 0)),
-         pl.BlockSpec((second.shape[0], block), lambda i: (0, i))] + [mine(rows // len(gots))] * len(gots),
+         pl.BlockSpec((second.shape[0], block), lambda i: (0, i))] + own,
         out_specs=[spec] * 3, grid=(cols // block,),
     )
 
 
-def orthonormal_kernel(sizes, panel_ref, out_ref):
+def orthonormal_kernel(sizes, panel_ref, out_ref, *outs):
     rank = panel_ref.shape[0]
     place = lax.broadcasted_iota(jnp.int32, (rank, 1), 0)
     cuts = [sum(sizes[:i]) for i in range(len(sizes) + 1)]
@@ -680,6 +688,7 @@
             column = part[number : number + 1, :]
             column = column * lax.rsqrt(jnp.sum(column * column, -1, keepdims=True) + 1e-20)
             out_ref[number : number + 1, a:b] = column
+            outs[which][number : number + 1, :] = column
             if number + 1 < rank:
                 along = jnp.sum(part * column, -1, keepdims=True)
                 panels[which] = part - jnp.where(place > number, along, 0.0) * column
@@ -845,6 +854,9 @@
     kept += [res[3:6], res[6:9]]
     while count.step < len(bits):
         advance(order, count)
+    down_far[0] = order(down_far[0])
+    down_far.append(exchange(down_far[0], 1))
+    table_far = [chip_swap(tie(table_half, down_far[0]))]
     act = bf(rows, hidden)
     slope = shape(rows, hidden)
     a0, a1, p0, p1, low = call(
@@ -853,9 +865,6 @@
         [SMEM] + [VMEM] * 3 + [ANY] * 4, [vm(4, features, hidden), dma(4)],
     )
     order.mark(low)
-    down_far[0] = order(down_far[0])
-    down_far.append(exchange(down_far[0], 1))
-    table_far = [chip_swap(tie(table_half, down_far[0]))]
     up_far[1] = order(up_far[1])
     up_both = cores([tie(x, up_far[1]) for x in up_far])
     table_far[0] = order(table_far[0])
@@ -906,19 +915,20 @@
     )
     order.mark(dh_a)
     up_got = core_swap(up_send)
-    down_far_grad, down_part, left_down_b = call(
-        down_keep_kernel, "down_keep", (bf(hidden, features), shape(hidden, features), left),
+    down_a, down_b, down_part, left_down_b = call(
+        down_keep_kernel, "down_keep",
+        (bf(hidden // 2, features), bf(hidden // 2, features), shape(hidden, features), left),
         (order(dz2b), a0, a2, starts[0], starts[2], down_got, err_down[0]),
     )
     order.mark(left_down_b)
-    down_in = chip_swap(down_far_grad)
-    up_a, up_b, up_part, left_up_b, dz1, dz1b, g_vec1, hidden_b = call(
+    down_in_a = chip_swap(down_a)
+    both, up_b, up_part, left_up_b, dz1, dz1b, g_vec1, hidden_b = call(
         up_keep_kernel, "up_keep",
-        (bf(features // 2, hidden), bf(features // 2, hidden), shape(features, hidden), left, shape(rows, features), bf(rows, features),
+        (bf(hidden // 2 + features // 4, hidden), bf(features - features // 4, hidden), shape(features, hidden), left, shape(rows, features), bf(rows, features),
          shape(3, features), shape(2, 1, hidden)),
         (meta, dz2, order(dz2b), h1b, normed1, inverse1, vec_whole, dh_a, p0, p2, starts[0], starts[2],
-         up_got, err_up[0], w_up, *up_far, w_down, *down_far),
-        [SMEM] + [VMEM] * 13 + [ANY] * 6, [vm(rows, hidden), vm(4, features, hidden), dma(6)],
+         up_got, err_up[0], down_b, w_up, *up_far, w_down, *down_far),
+        [SMEM] + [VMEM] * 14 + [ANY] * 6, [vm(rows, hidden), vm(4, features, hidden), dma(6)],
     )
     order.mark(dz1b)
     pack_width = 3 * features + width
@@ -932,9 +942,9 @@
         [SMEM] + [VMEM] * 13 + [ANY] * 3, scratch + [vm(2, all_rows, features), dma(3)],
     )
     order.mark(dh_b)
-    head_in, down_in = order(head_in), order(down_in)
-    first_got = core_swap(tie(first_send, down_in))
-    up_in_a = chip_swap(tie(up_a, down_in))
+    head_in, down_in_a = order(head_in), order(down_in_a)
+    first_got = core_swap(tie(first_send, down_in_a))
+    both_in = chip_swap(tie(both, down_in_a))
     cols = bf(rows, columns)
     first_far_grad, first_part, pack_b, pack_a, d_far, d_near, d_own = call(
         functools.partial(attention_keep_kernel, length), "attention_keep",
@@ -949,10 +959,9 @@
     order.mark(d_far)
 
     d_two = chip_swap(d_far)
-    up_in_a = order(up_in_a)
-    up_in_b = chip_swap(tie(up_b, up_in_a))
-    mine = order(pack_b + core_swap(tie(pack_a, up_in_a)))
-    d_one = core_swap(tie(d_near, up_in_a))
+    both_in = order(both_in)
+    mine = order(pack_b + core_swap(tie(pack_a, both_in)))
+    d_one = core_swap(tie(d_near, both_in))
     mine_in = chip_swap(mine[1])
     mine = order(mine[0] + mine_in)
     panels = WholeSum(mine[:8], bits)
@@ -960,61 +969,66 @@
     advance(order, panels)
     d_two = order(d_two)
     d_three = core_swap(d_two)
-    first_in = chip_swap(tie(first_far_grad, d_two))
+    up_in_b = chip_swap(tie(up_b, d_two))
     advance(order, panels)
     table_grad = call(
         functools.partial(scatter_kernel, own, vocab), "scatter", bf(columns, total),
         (ids_rows, order(d_own), d_one, d_two, d_three, head_near, head_keep, head_in),
     )
     order.mark(table_grad)
-    cut = columns // 2
-    table_sums = (
-        RowSum(table_grad[:cut], [bits[1], bits[0]] + bits[2:]), RowSum(table_grad[cut:], bits),
-    )
-    for one in table_sums:
-        one.send()
+    table_sum = RowSum(table_grad, bits)
+    table_sum.send()
+    first_in = chip_swap(tie(first_far_grad, table_grad))
     while panels.step < len(bits):
         advance(order, panels)
     sizes = (features, features, features, width)
-    bases = call(
-        functools.partial(orthonormal_kernel, sizes), "orthonormal", shape(rank, pack_width), (order(panels.x),),
+    bases, base_up, base_down, base_qkv, base_out = call(
+        functools.partial(orthonormal_kernel, sizes), "orthonormal",
+        (shape(rank, pack_width),) + tuple(shape(rank, size) for size in sizes), (order(panels.x),),
     )
     order.mark(bases)
     packed = call(
         right_mlp_kernel, "right_mlp", shape(rank, 2 * features + pack_width),
-        (down_part, down_in, up_part, up_in_a, order(up_in_b), bases, mine[8:]),
-    )
-    packed = WholeSum(packed, bits)
+        (down_part, down_in_a, both_in, up_part, order(up_in_b), bases, mine[8:]),
+    )
+    order.mark(packed)
+    packed = WholeSum(packed, bits[2:] + bits[:2])
     packed.send()
-    for _ in range(2):
-        advance(order, *table_sums, packed)
+    advance(order, table_sum)
+    advance(order, packed)
+    advance(order, packed)
+    advance(order, table_sum)
+    while packed.step < len(bits):
+        advance(order, packed)
+    right_up, right_down = packed.x[:, :features], packed.x[:, features : 2 * features]
+    rest = packed.x[:, 2 * features :]
     rights = call(
         functools.partial(right_attention_kernel, used), "right_attention", shape(rank, features + used),
         (first_part, order(first_in), bases),
     )
     order.mark(rights)
-    rights = WholeSum(rights, bits)
+    rights = WholeSum(rights, bits[2:] + bits[:2])
     rights.send()
-    while packed.step < len(bits):
-        advance(order, *table_sums, packed)
-    base_up, base_down = bases[:, :features], bases[:, features : 2 * features]
-    base_qkv, base_out = bases[:, 2 * features : 3 * features], bases[:, 3 * features :]
-    right_up, right_down = packed.x[:, :features], packed.x[:, features : 2 * features]
-    rest = packed.x[:, 2 * features :]
-    down = update(replicas, down_part, [down_in], 0, w_down, mom_down, order(base_down), right_down)
+    advance(order, table_sum)
+    down = update(replicas, down_part, [(down_in_a, hidden // 2, 0), (both_in, hidden // 2, 0)], 0, w_down, mom_down, order(base_down), right_down)
     order.mark(down[0])
-    advance(order, *table_sums, rights)
-    up = update(replicas, up_part, [up_in_a, up_in_b], 0, w_up, mom_up, order(base_up), right_up)
+    advance(order, rights)
+    advance(order, table_sum)
+    up = update(replicas, up_part, [(both_in, features // 4, 2 * hidden // features), (up_in_b, features - features // 4, 0)], 0, w_up, mom_up, order(base_up), right_up)
     order.mark(up[0])
-    while rights.step < len(bits) or table_sums[1].step < len(table_sums[1].steps):
-        advance(order, *table_sums, rights)
+    rest = tie(rest, up[0])
+    while rights.step < len(bits):
+        advance(order, rights)
     right_out, right_qkv = rights.x[:, :features], rights.x[:, features:]
-    out = update(replicas, first_part, [first_in], used, w_out, mom_out, base_out, right_out)
+    out = update(replicas, first_part, [first_in], used, w_out, mom_out, order(base_out), right_out)
     qkv = update(replicas, first_part, [first_in], 0, w_qkv.T, mom_qkv.T, right_qkv, base_qkv)
-
-    table_grad = jnp.concatenate([one.x for one in table_sums], 0)[:, :total_rows].astype(F32)
+    order.mark(qkv[0])
+    while table_sum.step < len(table_sum.steps):
+        advance(order, table_sum)
+
+    table_grad = table_sum.x[:, :total_rows].astype(F32)
     vectors = [rest[2 + n // 3, n % 3 * features : (n % 3 + 1) * features] for n in range(8)]
-    results = [jnp.stack([rest[4, 2 * features], count[0]])]
+    results = [jnp.where(jnp.arange(2) == 0, rest[4, 2 * features : 2 * features + 1], count)]
 
     def momentum_step(weight, moment, grad, rate):
         new_moment = BETA * moment + grad

time: 300 us -> 288 us (0.960)
  starting transfers between devices: 51.9 us -> 43.6 us
  waiting for transfers between devices: 87.2 us -> 82.6 us
    ppermute x62 -> x57, starting transfers between devices: 51.9 us -> 43.6 us  [across(): return lax.ppermute(x, axis, [(i, i ^ bit) for i in range(size)])]
    ppermute x62 -> x57, waiting for transfers between devices: 87.2 us -> 82.6 us  [across(): return lax.ppermute(x, axis, [(i, i ^ bit) for i in range(size)])]
    unnamed x218 -> x222, local copies, waits for them, and re-layouts: 14.8 us -> 14.8 us
  transfers between devices with their start and end apart: 62 -> 57, of which waited for: 28 -> 28; matrix products, arithmetic and copies ran while one was open for 4% -> 5% of each run, Pallas kernels for 37% -> 41%
where the time goes in v1:
time: 288 us; the launch traced here: 283 us
  Pallas kernels  124 us (43%)
  waiting for transfers between devices  82.6 us (29%)
  starting transfers between devices  43.6 us (15%)
  local copies, waits for them, and re-layouts  17.5 us (6%)
  other arithmetic  12.6 us (4%)
  between operations  2.98 us (1%)
    pallas_call x21, Pallas kernels, call(): pl.pallas_call(kernel, out_shape=out_shape, in_specs=in_specs, scratch_sh...  124 us
    ppermute x57, waiting for transfers between devices, across(): return lax.ppermute(x, axis, [(i, i ^ bit) for i in range(size)])  82.6 us
    ppermute x57, starting transfers between devices, across(): return lax.ppermute(x, axis, [(i, i ^ bit) for i in range(size)])  43.6 us
    unnamed x222, local copies, waits for them, and re-layouts  14.8 us
  transfers between devices with their start and end apart: 57, of which 28 were waited for; matrix products, arithmetic and copies ran while one was open for 5% of the time, Pallas kernels for 41%

profile of v1, /device:TPU:0, one launch (start us, length us, event | category | flops | bytes accessed | tf_op | source)
XLA Modules:
  0.0 283.3 jit_solution(14962888584946624447)
XLA Ops:
  1.9 4.9 %pack.1 = (bf16[768,768]{1,0:T(8,128)(2,1)}, bf16[384,768]{1,0:T(8,128)(2,1)}, bf16[384,768]{1,0:T(8,128)(2,1)}, bf16[384,768]{1,0:T(8,128)(2,1)}, bf16[192,2304]{1,0:T(8,128)(2,1)}, /*index=5*/bf16[96,2304]{1,0:T(8,128)(2,1)}) custom-call(s32[2]{0:T(128)} %pad_add_fusion.meta_ref, bf16[576,768]{1,0:T(8,128)(2,1)} %bitcast.68, bf16[192,768]{1,0:T(8,128)(2,1)} %weight.5, ...), custom_call_target="tpu_custom_call" | custom-call | flops 34500001792 | bytes 30000000 | tf_op jit(solution)/shard_map/pack/pallas_call | solution.py:72
  6.8 3.0 %collective-permute-start = (bf16[384,768]{1,0:T(8,128)(2,1)}, bf16[384,768]{1,0:T(8,128)(2,1)}, u32[]{:S(2)}, u32[]{:S(2)}) collective-permute-start(bf16[384,768]{1,0:T(8,128)(2,1)} %get-tuple-element.195), channel_id=1, source_target_pairs={{0,2},{1,3},{2,0},{3,1},{4,6},{5,7},{6,4},{7,5},{8,10},{9,11},{10,... | collective-permute-start | bytes 1769480 | tf_op jit(solution)/shard_map/ppermute | solution.py:36
  11.5 5.1 %embed.1 = (bf16[2,192,640]{2,1,0:T(8,128)(2,1)}, bf16[192,768]{1,0:T(8,128)(2,1)S(1)}, bf16[192,768]{1,0:T(8,128)(2,1)S(1)}, s32[256,8]{1,0:T(8,128)S(1)}) custom-call(s32[2]{0:T(128)S(1)} %copy-done.50, s32[8]{0:T(128)S(1)} %copy-done.45, s32[8,256]{1,0:T(8,128)S(1)} %copy-done.41, s32[8,128]{1,0:T(8,128)S(1)} %copy-done.43, bf16[192,2304]{1,0:T(8,128)(2,1)S(1)} %copy-done.20), custom_call_target="tpu_custom_call" | custom-call | flops 57500000256 | bytes 50000000 | tf_op jit(solution)/shard_map/embed/pallas_call | solution.py:72
  18.6 5.0 %collective-permute-done.c2a = bf16[384,768]{1,0:T(8,128)(2,1)} collective-permute-done((bf16[384,768]{1,0:T(8,128)(2,1)}, bf16[384,768]{1,0:T(8,128)(2,1)}, u32[]{:S(2)}, u32[]{:S(2)}) %collective-permute-start) | collective-permute-done | bytes 589856 | tf_op jit(solution)/shard_map/ppermute | solution.py:36
  26.7 10.0 %collective-permute-done.2.e2 = bf16[2,192,640]{2,1,0:T(8,128)(2,1)} collective-permute-done((bf16[2,192,640]{2,1,0:T(8,128)(2,1)}, bf16[2,192,640]{2,1,0:T(8,128)(2,1)}, u32[]{:S(2)}, u32[]{:S(2)}) %collective-permute-start.2) | collective-permute-done | bytes 491552 | tf_op jit(solution)/shard_map/ppermute | solution.py:36
  45.6 7.5 %attention_first.1 = (f32[512,768]{1,0:T(8,128)S(1)}, f32[512,1]{1,0:T(8,128)S(1)}, bf16[512,768]{1,0:T(8,128)(2,1)S(1)}, bf16[3,512,192]{2,1,0:T(8,128)(2,1)S(1...) custom-call(s32[2]{0:T(128)S(1)} %copy-done.50, ...), custom_call_target="tpu_custom_call" | custom-call | flops 80499998720 | bytes 70000000 | tf_op jit(solution)/shard_map/attention_first/pallas_call | solution.py:72
  53.9 3.1 %collective-permute-done.5.c2b = bf16[384,768]{1,0:T(8,128)(2,1)S(1)} collective-permute-done((bf16[384,768]{1,0:T(8,128)(2,1)}, bf16[384,768]{1,0:T(8,128)(2,1)S(1)}, u32[]{:S(2)}, u32[]{:S(2)}) %collective-permute-start.5) | collective-permute-done | bytes 589856 | tf_op jit(solution)/shard_map/ppermute | solution.py:36
  61.5 2.6 collective-permute-start.14
  65.6 8.8 %attention_second.1 = (f32[512,768]{1,0:T(8,128)S(1)}, f32[512,1]{1,0:T(8,128)S(1)}, bf16[512,768]{1,0:T(8,128)(2,1)S(1)}, bf16[3,512,192]{2,1,0:T(8,128)(2,1)S(...) custom-call(s32[2]{0:T(128)S(1)} %copy-done.50, ...), custom_call_target="tpu_custom_call" | custom-call | flops 92000002048 | bytes 80000000 | tf_op jit(solution)/shard_map/attention_second/pallas_call | solution.py:72
  74.6 3.8 %collective-permute-done.18.d2a = bf16[384,768]{1,0:T(8,128)(2,1)S(1)} collective-permute-done((bf16[384,768]{1,0:T(8,128)(2,1)S(1)}, bf16[384,768]{1,0:T(8,128)(2,1)S(1)}, u32[]{:S(2)}, u32[]{:S(2)}) %collective-permute-start.18) | collective-permute-done | bytes 589856 | tf_op jit(solution)/shard_map/ppermute | solution.py:36
  81.1 6.4 %mlp_first.1 = (bf16[512,768]{1,0:T(8,128)(2,1)S(1)}, bf16[512,768]{1,0:T(8,128)(2,1)S(1)}, f32[512,768]{1,0:T(8,128)S(1)}, f32[512,768]{1,0:T(8,128)S(1)}, f32[512,768]{1,0:T(8,128)S(1)}) custom-call(s32[2]{0:T(128)S(1)} %copy-done.50, bf16[512,768]{1,0:T(8,128)(2,1)S(1)} %get-tuple-element.234.h1b_ref, f32[8,4096]{1,0:T(8,128)S(1)} %concatenate.9.b0.s0, ...), custom_call_target="tpu_custom_call" | custom-call | flops 80499998720 | bytes 70000000 | tf_op jit(solution)/shard_map/mlp_first/pallas_call | solution.py:72
  89.2 2.5 collective-permute-done.19.d2b
  94.7 7.5 %mlp_second.1 = (bf16[512,768]{1,0:T(8,128)(2,1)S(1)}, bf16[512,768]{1,0:T(8,128)(2,1)S(1)}, f32[512,768]{1,0:T(8,128)S(1)}, f32[512,768]{1,0:T(8,128)S(1)}, f32...) custom-call(s32[2]{0:T(128)S(1)} %copy-done.50, ...), custom_call_target="tpu_custom_call" | custom-call | flops 80499998720 | bytes 70000000 | tf_op jit(solution)/shard_map/mlp_second/pallas_call | solution.py:72
  106.8 8.7 %head.1 = (f32[512,768]{1,0:T(8,128)S(1)}, bf16[512,768]{1,0:T(8,128)(2,1)S(1)}, f32[1,128]{1,0:T(1,128)S(1)}, f32[1,2304]{1,0:T(1,128)S(1)}, f32[3,768]{1,0:T(4...) custom-call(s32[2]{0:T(128)S(1)} %copy-done.50, s32[8]{0:T(128)S(1)} %copy-done.46, ...), custom_call_target="tpu_custom_call" | custom-call | flops 103499997184 | bytes 90000000 | tf_op jit(solution)/shard_map/head/pallas_call | solution.py:72
  122.3 7.3 %up_send.1 = (bf16[2,768,768]{2,1,0:T(8,128)(2,1)S(1)}, f32[2,8,768]{2,1,0:T(8,128)S(1)}, f32[512,768]{1,0:T(8,128)S(1)}, f32[2,1,768]{2,1,0:T(1,128)S(1)}) custom-call(s32[2]{0:T(128)S(1)} %copy-done.50, bf16[512,768]{1,0:T(8,128)(2,1)S(1)} %get-tuple-element.266.dzb_ref, bf16[512,768]{1,0:T(8,128)(2,1)S(1)} %get-tuple-element.234.h1b_ref, ...), custom_call_target="tpu_custom_call" | custom-call | flops 69000003584 | bytes 60000000 | tf_op jit(solution)/shard_map/up_send/pallas_call | solution.py:72
  129.8 3.3 %down_keep.1 = (bf16[384,768]{1,0:T(8,128)(2,1)}, bf16[384,768]{1,0:T(8,128)(2,1)S(1)}, f32[768,768]{1,0:T(8,128)S(1)}, f32[2,8,768]{2,1,0:T(8,128)S(1)}) custom-call(bf16[512,768]{1,0:T(8,128)(2,1)S(1)} %get-tuple-element.266.dzb_ref, bf16[512,768]{1,0:T(8,128)(2,1)S(1)} %get-tuple-element.260.a0, bf16[512,768]{1,0:T(8,128)(2,1)S(1)} %get-tuple-element.261.a2, ...), custom_call_target="tpu_custom_call" | custom-call | flops 46000001024 | bytes 40000000 | tf_op jit(solution)/shard_map/down_keep/pallas_call | solution.py:72
  135.2 10.3 %up_keep.1 = (bf16[576,768]{1,0:T(8,128)(2,1)}, bf16[576,768]{1,0:T(8,128)(2,1)S(1)}, f32[768,768]{1,0:T(8,128)S(1)}, f32[2,8,768]{2,1,0:T(8,128)S(1)}, f32[512,...) custom-call(s32[2]{0:T(128)S(1)} %copy-done.50, ...), custom_call_target="tpu_custom_call" | custom-call | flops 92000002048 | bytes 80000000 | tf_op jit(solution)/shard_map/up_keep/pallas_call | solution.py:72
  145.7 12.2 %attention_send.1 = (bf16[2,768,768]{2,1,0:T(8,128)(2,1)S(1)}, f32[2,16,2496]{2,1,0:T(8,128)S(1)}, f32[512,768]{1,0:T(8,128)S(1)}) custom-call(s32[2]{0:T(128)S(1)} %copy-done.50, bf16[512,768]{1,0:T(8,128)(2,1)S(1)} %get-tuple-element.287.dz1b_ref, bf16[512,768]{1,0:T(8,128)(2,1)S(1)} %copy-done.68, bf16[3,512,192]{2,1,0:T(8,128)(2,1)S(1)} %copy-done.70, ...), custom_call_target="tpu_custom_call" | custom-call | flops 149500002304 | bytes 130000000 | tf_op jit(solution)/shard_map/attention_send/pallas_call | solution.py:72
  159.7 2.8 %collective-permute-done.35.near_ref = bf16[2,768,768]{2,1,0:T(8,128)(2,1)S(1)} collective-permute-done((bf16[2,768,768]{2,1,0:T(8,128)(2,1)S(1)}, bf16[2,768,768]{2,1,0:T(8,128)(2,1)S(1)}, u32[]{:S(2)}, u32[]{:S(2)}) %collective-permute-start.35) | collective-permute-done | bytes 2359328 | tf_op jit(solution)/shard_map/ppermute | solution.py:36
  162.7 15.3 %attention_keep.1 = (bf16[768,768]{1,0:T(8,128)(2,1)S(1)}, f32[768,768]{1,0:T(8,128)S(1)}, f32[2,16,2496]{2,1,0:T(8,128)S(1)}, f32[2,16,2496]{2,1,0:T(8,128)S(1)...) custom-call(s32[2]{0:T(128)S(1)} %copy-done.50, ...), custom_call_target="tpu_custom_call" | custom-call | flops 172499992576 | bytes 150000000 | tf_op jit(solution)/shard_map/attention_keep/pallas_call | solution.py:72
  184.2 5.0 %collective-permute-done.38 = f32[16,2496]{1,0:T(8,128)S(1)} collective-permute-done((f32[16,2496]{1,0:T(8,128)S(1)}, f32[16,2496]{1,0:T(8,128)S(1)}, u32[]{:S(2)}, u32[]{:S(2)}) %collective-permute-start.38) | collective-permute-done | bytes 159776 | tf_op jit(solution)/shard_map/ppermute | solution.py:36
  190.2 3.5 %collective-permute-done.39 = f32[8,2496]{1,0:T(8,128)S(1)} collective-permute-done((f32[8,2496]{1,0:T(8,128)S(1)}, f32[8,2496]{1,0:T(8,128)S(1)}, u32[]{:S(2)}, u32[]{:S(2)}) %collective-permute-start.39) | collective-permute-done | bytes 79904 | tf_op jit(solution)/shard_map/ppermute | solution.py:36
  193.8 5.9 %collective-permute-done.36.r2 = bf16[2,512,192]{2,1,0:T(8,128)(2,1)S(1)} collective-permute-done((bf16[2,512,192]{2,1,0:T(8,128)(2,1)S(1)}, bf16[2,512,192]{2,1,0:T(8,128)(2,1)S(1)}, u32[]{:S(2)}, u32[]{:S(2)}) %collective-permute-start.36) | collective-permute-done | bytes 393248 | tf_op jit(solution)/shard_map/ppermute | solution.py:36
  210.4 4.1 %scatter.1 = bf16[192,2304]{1,0:T(8,128)(2,1)S(1)} custom-call(s32[256,8]{1,0:T(8,128)S(1)} %copy-done.62, bf16[512,192]{1,0:T(8,128)(2,1)S(1)} %copy-done.60, bf16[512,192]{1,0:T(8,128)(2,1)} %collective-permute-done.43.r1, bf16[2,512,192]{2,1,0:T(8,128)(2,1)S(1)} %collective-permute-done.36.r2, bf16[2,512,192]{2,1,0:T(8,128)(2,1)} %collective-permute-done.44.r3, ...), custom_call_target="tpu_custom_call" | custom-call | flops 5750000128 | bytes 5000000 | tf_op jit(solution)/shard_map/scatter/pallas_call | solution.py:72
  219.0 5.6 %collective-permute-done.40.got_b.refs_1_ = bf16[576,768]{1,0:T(8,128)(2,1)S(1)} collective-permute-done((bf16[576,768]{1,0:T(8,128)(2,1)}, bf16[576,768]{1,0:T(8,128)(2,1)S(1)}, u32[]{:S(2)}, u32[]{:S(2)}) %collective-permute-start.40) | collective-permute-done | bytes 884768 | tf_op jit(solution)/shard_map/ppermute | solution.py:36
  228.3 6.5 %collective-permute-done.45 = f32[8,4032]{1,0:T(8,128)S(1)} collective-permute-done((f32[8,4032]{1,0:T(8,128)S(1)}, f32[8,4032]{1,0:T(8,128)S(1)}, u32[]{:S(2)}, u32[]{:S(2)}) %collective-permute-start.45) | collective-permute-done | bytes 129056 | tf_op jit(solution)/shard_map/ppermute | solution.py:36
  235.8 4.1 %collective-permute-done.47 = f32[8,4032]{1,0:T(8,128)S(1)} collective-permute-done((f32[8,4032]{1,0:T(8,128)S(1)}, f32[8,4032]{1,0:T(8,128)S(1)}, u32[]{:S(2)}, u32[]{:S(2)}) %collective-permute-start.47) | collective-permute-done | bytes 129056 | tf_op jit(solution)/shard_map/ppermute | solution.py:36
  240.6 5.4 %collective-permute-done.48 = f32[8,4032]{1,0:T(8,128)S(1)} collective-permute-done((f32[8,4032]{1,0:T(8,128)S(1)}, f32[8,4032]{1,0:T(8,128)S(1)}, u32[]{:S(2)}, u32[]{:S(2)}) %collective-permute-start.48) | collective-permute-done | bytes 129056 | tf_op jit(solution)/shard_map/ppermute | solution.py:36
  246.7 2.5 collective-permute-done.51.got.refs_0_
  251.2 5.1 %update.4 = (f32[768,768]{1,0:T(8,128)}, f32[768,768]{1,0:T(8,128)}, f32[768,768]{1,0:T(8,128)}) custom-call(f32[768,768]{1,0:T(8,128)S(1)} %copy-done.58, bf16[768,768]{1,0:T(8,128)(2,1)S(1)} %copy-done.14, f32[768,768]{1,0:T(8,128)S(1)} %copy-done.8, f32[8,768]{1,0:T(8,128)S(1)} %copy-done.48, f32[8,768]{1,0:T(8,128)S(1)} %get-tuple-element.378.second_ref, ...), custom_call_target="tpu_custom_call" | custom-call | flops 4600000000 | bytes 4000000 | tf_op jit(solution)/shard_map/update/pallas_call | solution.py:72
  258.2 4.7 %update.5 = (f32[768,768]{1,0:T(8,128)}, f32[768,768]{1,0:T(8,128)}, f32[768,768]{1,0:T(8,128)}) custom-call(f32[768,768]{1,0:T(8,128)S(1)} %copy-done.56, bf16[768,768]{1,0:T(8,128)(2,1)S(1)} %copy-done.17, f32[768,768]{1,0:T(8,128)S(1)} %copy-done.9, f32[8,768]{1,0:T(8,128)S(1)} %copy-done.47, f32[8,768]{1,0:T(8,128)S(1)} %get-tuple-element.377.second_ref, ...), custom_call_target="tpu_custom_call" | custom-call | flops 4600000000 | bytes 4000000 | tf_op jit(solution)/shard_map/update/pallas_call | solution.py:72
  276.1 3.4 %update.6 = (f32[576,768]{1,0:T(8,128)}, f32[576,768]{1,0:T(8,128)}, f32[576,768]{1,0:T(8,128)}) custom-call(f32[768,768]{1,0:T(8,128)S(1)} %copy-done.54, bf16[576,768]{1,0:T(8,128)(2,1)S(1)} %bitcast.69, f32[576,768]{1,0:T(8,128)S(1)} %bitcast.67, f32[8,576]{1,0:T(8,128)S(1)} %get-tuple-element.390.first_ref, f32[8,768]{1,0:T(8,128)S(1)} %copy-done.49, ...), custom_call_target="tpu_custom_call" | custom-call | flops 4600000000 | bytes 4000000 | tf_op jit(solution)/shard_map/update/pallas_call | solution.py:72
  (370 shorter events, 94.4 us)
Async XLA Ops:
  0.7 40.3 %collective-permute-start.7 = (bf16[768,768]{1,0:T(8,128)(2,1)}, bf16[768,768]{1,0:T(8,128)(2,1)}, u32[]{:S(2)}, u32[]{:S(2)}) collective-permute-start(bf16[768,768]{1,0:T(8,128)(2,1)} %weight.4), channel_id=1, source_target_pairs={{0,1},{1,0},{2,3},{3,2},{4,5},{5,4},{6,7},{7,6},{8,9},{9,8},{10,11... | collective-permute-start | bytes 3538952 | tf_op jit(solution)/shard_map/ppermute | solution.py:36
  1.2 39.9 %collective-permute-start.8 = (bf16[768,768]{1,0:T(8,128)(2,1)}, bf16[768,768]{1,0:T(8,128)(2,1)}, u32[]{:S(2)}, u32[]{:S(2)}) collective-permute-start(bf16[768,768]{1,0:T(8,128)(2,1)} %weight.3), channel_id=1, source_target_pairs={{0,1},{1,0},{2,3},{3,2},{4,5},{5,4},{6,7},{7,6},{8,9},{9,8},{10,11... | collective-permute-start | bytes 3538952 | tf_op jit(solution)/shard_map/ppermute | solution.py:36
  6.8 16.9 %collective-permute-start = (bf16[384,768]{1,0:T(8,128)(2,1)}, bf16[384,768]{1,0:T(8,128)(2,1)}, u32[]{:S(2)}, u32[]{:S(2)}) collective-permute-start(bf16[384,768]{1,0:T(8,128)(2,1)} %get-tuple-element.195), channel_id=1, source_target_pairs={{0,2},{1,3},{2,0},{3,1},{4,6},{5,7},{6,4},{7,5},{8,10},{9,11},{10,... | collective-permute-start | bytes 1769480 | tf_op jit(solution)/shard_map/ppermute | solution.py:36
  9.7 30.5 %collective-permute-start.10 = (bf16[192,2304]{1,0:T(8,128)(2,1)}, bf16[192,2304]{1,0:T(8,128)(2,1)S(1)}, u32[]{:S(2)}, u32[]{:S(2)}) collective-permute-start(bf16[192,2304]{1,0:T(8,128)(2,1)} %get-tuple-element.197.table_ref.t0), channel_id=1, source_target_pairs={{0,1},{1,0},{2,3},{3,2},{4,5},{5,4},{6,7},{7,6},{8,9},{9,8},{10,11... | collective-permute-start | bytes 2654216 | tf_op jit(solution)/shard_map/ppermute | solution.py:36
  9.7 32.8 %collective-permute-start.9 = (bf16[768,768]{1,0:T(8,128)(2,1)}, bf16[768,768]{1,0:T(8,128)(2,1)S(1)}, u32[]{:S(2)}, u32[]{:S(2)}) collective-permute-start(bf16[768,768]{1,0:T(8,128)(2,1)} %get-tuple-element.206.c0), channel_id=1, source_target_pairs={{0,1},{1,0},{2,3},{3,2},{4,5},{5,4},{6,7},{7,6},{8,9},{9,8},{10,11... | collective-permute-start | bytes 3538952 | tf_op jit(solution)/shard_map/ppermute | solution.py:36
  23.6 13.0 %collective-permute-start.2 = (bf16[2,192,640]{2,1,0:T(8,128)(2,1)}, bf16[2,192,640]{2,1,0:T(8,128)(2,1)}, u32[]{:S(2)}, u32[]{:S(2)}) collective-permute-start(bf16[2,192,640]{2,1,0:T(8,128)(2,1)} %get-tuple-element.198), channel_id=1, source_target_pairs={{0,2},{1,3},{2,0},{3,1},{4,6},{5,7},{6,4},{7,5},{8,10},{9,11},{10,... | collective-permute-start | bytes 1474568 | tf_op jit(solution)/shard_map/ppermute | solution.py:36
  41.0 15.9 %collective-permute-start.5 = (bf16[384,768]{1,0:T(8,128)(2,1)}, bf16[384,768]{1,0:T(8,128)(2,1)S(1)}, u32[]{:S(2)}, u32[]{:S(2)}) collective-permute-start(bf16[384,768]{1,0:T(8,128)(2,1)} %collective-permute-done.c2a), channel_id=1, source_target_pairs={{0,4},{4,0},{8,12},{12,8},{16,20},{20,16},{24,28},{28,24},{1,5},{5... | collective-permute-start | bytes 1769480 | tf_op jit(solution)/shard_map/ppermute | solution.py:36
  42.6 11.3 %collective-permute-start.6 = (f32[8,4096]{1,0:T(8,128)S(1)}, f32[8,4096]{1,0:T(8,128)S(1)}, u32[]{:S(2)}, u32[]{:S(2)}) collective-permute-start(f32[8,4096]{1,0:T(8,128)S(1)} %concatenate.9.b0.s0), channel_id=1, source_target_pairs={{0,2},{1,3},{2,0},{3,1},{4,6},{5,7},{6,4},{7,5},{8,10},{9,11},{10,... | collective-permute-start | bytes 393224 | tf_op jit(solution)/shard_map/ppermute | solution.py:36
  44.1 16.8 %collective-permute-start.4 = (bf16[384,768]{1,0:T(8,128)(2,1)}, bf16[384,768]{1,0:T(8,128)(2,1)}, u32[]{:S(2)}, u32[]{:S(2)}) collective-permute-start(bf16[384,768]{1,0:T(8,128)(2,1)} %get-tuple-element.204), channel_id=1, source_target_pairs={{0,2},{1,3},{2,0},{3,1},{4,6},{5,7},{6,4},{7,5},{8,10},{9,11},{10,... | collective-permute-start | bytes 1769480 | tf_op jit(solution)/shard_map/ppermute | solution.py:36
  57.0 8.5 %collective-permute-start.16 = (bf16[384,768]{1,0:T(8,128)(2,1)}, bf16[384,768]{1,0:T(8,128)(2,1)S(1)}, u32[]{:S(2)}, u32[]{:S(2)}) collective-permute-start(bf16[384,768]{1,0:T(8,128)(2,1)} %collective-permute-done.c2a), channel_id=1, source_target_pairs={{0,1},{1,0},{2,3},{3,2},{4,5},{5,4},{6,7},{7,6},{8,9},{9,8},{10,11... | collective-permute-start | bytes 1769480 | tf_op jit(solution)/shard_map/ppermute | solution.py:36
  57.0 8.6 %collective-permute-start.17 = (bf16[384,768]{1,0:T(8,128)(2,1)S(1)}, bf16[384,768]{1,0:T(8,128)(2,1)S(1)}, u32[]{:S(2)}, u32[]{:S(2)}) collective-permute-start(bf16[384,768]{1,0:T(8,128)(2,1)S(1)} %collective-permute-done.5.c2b), channel_id=1, source_target_pairs={{0,1},{1,0},{2,3},{3,2},{4,5},{5,4},{6,7},{7,6},{8,9},{9,8},{10,11... | collective-permute-start | bytes 1769480 | tf_op jit(solution)/shard_map/ppermute | solution.py:36
  60.9 26.7 %collective-permute-start.21 = (bf16[384,768]{1,0:T(8,128)(2,1)}, bf16[384,768]{1,0:T(8,128)(2,1)}, u32[]{:S(2)}, u32[]{:S(2)}) collective-permute-start(bf16[384,768]{1,0:T(8,128)(2,1)} %collective-permute-done.4.u2a), channel_id=1, source_target_pairs={{0,4},{4,0},{8,12},{12,8},{16,20},{20,16},{24,28},{28,24},{1,5},{5... | collective-permute-start | bytes 1769480 | tf_op jit(solution)/shard_map/ppermute | solution.py:36
  61.5 13.1 %collective-permute-start.14 = (f32[8,128]{1,0:T(8,128)S(1)}, f32[8,128]{1,0:T(8,128)S(1)}, u32[]{:S(2)}, u32[]{:S(2)}) collective-permute-start(f32[8,128]{1,0:T(8,128)S(1)} %add.72), channel_id=1, source_target_pairs={{0,16},{4,20},{8,24},{12,28},{16,0},{20,4},{24,8},{28,12},{1,17},{... | collective-permute-start | bytes 12296 | tf_op jit(solution)/shard_map/ppermute | solution.py:36
  64.0 14.3 %collective-permute-start.18 = (bf16[384,768]{1,0:T(8,128)(2,1)S(1)}, bf16[384,768]{1,0:T(8,128)(2,1)S(1)}, u32[]{:S(2)}, u32[]{:S(2)}) collective-permute-start(bf16[384,768]{1,0:T(8,128)(2,1)S(1)} %copy-done.109), channel_id=1, source_target_pairs={{0,2},{1,3},{2,0},{3,1},{4,6},{5,7},{6,4},{7,5},{8,10},{9,11},{10,... | collective-permute-start | bytes 1769480 | tf_op jit(solution)/shard_map/ppermute | solution.py:36
  78.4 13.4 %collective-permute-start.19 = (bf16[384,768]{1,0:T(8,128)(2,1)S(1)}, bf16[384,768]{1,0:T(8,128)(2,1)S(1)}, u32[]{:S(2)}, u32[]{:S(2)}) collective-permute-start(bf16[384,768]{1,0:T(8,128)(2,1)S(1)} %collective-permute-done.18.d2a), channel_id=1, source_target_pairs={{0,4},{4,0},{8,12},{12,8},{16,20},{20,16},{24,28},{28,24},{1,5},{5... | collective-permute-start | bytes 1769480 | tf_op jit(solution)/shard_map/ppermute | solution.py:36
  79.6 9.6 %collective-permute-start.20 = (bf16[96,2304]{1,0:T(8,128)(2,1)S(1)}, bf16[96,2304]{1,0:T(8,128)(2,1)S(1)}, u32[]{:S(2)}, u32[]{:S(2)}) collective-permute-start(bf16[96,2304]{1,0:T(8,128)(2,1)S(1)} %copy-done.110), channel_id=1, source_target_pairs={{0,2},{1,3},{2,0},{3,1},{4,6},{5,7},{6,4},{7,5},{8,10},{9,11},{10,... | collective-permute-start | bytes 1327112 | tf_op jit(solution)/shard_map/ppermute | solution.py:36
  92.3 12.1 %collective-permute-start.26 = (bf16[96,2304]{1,0:T(8,128)(2,1)S(1)}, bf16[96,2304]{1,0:T(8,128)(2,1)S(1)}, u32[]{:S(2)}, u32[]{:S(2)}) collective-permute-start(bf16[96,2304]{1,0:T(8,128)(2,1)S(1)} %collective-permute-done.20.t2a), channel_id=1, source_target_pairs={{0,4},{4,0},{8,12},{12,8},{16,20},{20,16},{24,28},{28,24},{1,5},{5... | collective-permute-start | bytes 1327112 | tf_op jit(solution)/shard_map/ppermute | solution.py:36
  117.9 11.8 %collective-permute-start.30 = (bf16[2,768,768]{2,1,0:T(8,128)(2,1)S(1)}, bf16[2,768,768]{2,1,0:T(8,128)(2,1)S(1)}, u32[]{:S(2)}, u32[]{:S(2)}) collective-permute-start(bf16[2,768,768]{2,1,0:T(8,128)(2,1)S(1)} %get-tuple-element.253), channel_id=1, source_target_pairs={{0,1},{1,0},{2,3},{3,2},{4,5},{5,4},{6,7},{7,6},{8,9},{9,8},{10,11... | collective-permute-start | bytes 7077896 | tf_op jit(solution)/shard_map/ppermute | solution.py:36
  120.8 37.1 %collective-permute-start.32 = (bf16[192,2304]{1,0:T(8,128)(2,1)}, bf16[192,2304]{1,0:T(8,128)(2,1)}, u32[]{:S(2)}, u32[]{:S(2)}) collective-permute-start(bf16[192,2304]{1,0:T(8,128)(2,1)} %fusion.1), channel_id=1, source_target_pairs={{0,2},{1,3},{2,0},{3,1},{4,6},{5,7},{6,4},{7,5},{8,10},{9,11},{10,... | collective-permute-start | bytes 2654216 | tf_op jit(solution)/shard_map/ppermute | solution.py:36
  134.6 23.4 %collective-permute-start.31 = (bf16[384,768]{1,0:T(8,128)(2,1)}, bf16[384,768]{1,0:T(8,128)(2,1)}, u32[]{:S(2)}, u32[]{:S(2)}) collective-permute-start(bf16[384,768]{1,0:T(8,128)(2,1)} %get-tuple-element.263), channel_id=1, source_target_pairs={{0,2},{1,3},{2,0},{3,1},{4,6},{5,7},{6,4},{7,5},{8,10},{9,11},{10,... | collective-permute-start | bytes 1769480 | tf_op jit(solution)/shard_map/ppermute | solution.py:36
  158.3 22.2 %collective-permute-start.34 = (bf16[576,768]{1,0:T(8,128)(2,1)}, bf16[576,768]{1,0:T(8,128)(2,1)}, u32[]{:S(2)}, u32[]{:S(2)}) collective-permute-start(bf16[576,768]{1,0:T(8,128)(2,1)} %get-tuple-element.286), channel_id=1, source_target_pairs={{0,2},{1,3},{2,0},{3,1},{4,6},{5,7},{6,4},{7,5},{8,10},{9,11},{10,... | collective-permute-start | bytes 2654216 | tf_op jit(solution)/shard_map/ppermute | solution.py:36
  183.7 16.0 %collective-permute-start.36 = (bf16[2,512,192]{2,1,0:T(8,128)(2,1)S(1)}, bf16[2,512,192]{2,1,0:T(8,128)(2,1)S(1)}, u32[]{:S(2)}, u32[]{:S(2)}) collective-permute-start(bf16[2,512,192]{2,1,0:T(8,128)(2,1)S(1)} %get-tuple-element.304), channel_id=1, source_target_pairs={{0,2},{1,3},{2,0},{3,1},{4,6},{5,7},{6,4},{7,5},{8,10},{9,11},{10,... | collective-permute-start | bytes 1179656 | tf_op jit(solution)/shard_map/ppermute | solution.py:36
  190.2 16.8 %collective-permute-start.43 = (bf16[512,192]{1,0:T(8,128)(2,1)}, bf16[512,192]{1,0:T(8,128)(2,1)}, u32[]{:S(2)}, u32[]{:S(2)}) collective-permute-start(bf16[512,192]{1,0:T(8,128)(2,1)} %get-tuple-element.321), channel_id=1, source_target_pairs={{0,1},{1,0},{2,3},{3,2},{4,5},{5,4},{6,7},{7,6},{8,9},{9,8},{10,11... | collective-permute-start | bytes 589832 | tf_op jit(solution)/shard_map/ppermute | solution.py:36
  201.9 22.7 %collective-permute-start.40 = (bf16[576,768]{1,0:T(8,128)(2,1)}, bf16[576,768]{1,0:T(8,128)(2,1)S(1)}, u32[]{:S(2)}, u32[]{:S(2)}) collective-permute-start(bf16[576,768]{1,0:T(8,128)(2,1)} %copy-done.22), channel_id=1, source_target_pairs={{0,2},{1,3},{2,0},{3,1},{4,6},{5,7},{6,4},{7,5},{8,10},{9,11},{10,... | collective-permute-start | bytes 2654216 | tf_op jit(solution)/shard_map/ppermute | solution.py:36
  206.4 8.0 %collective-permute-start.42 = (f32[8,2496]{1,0:T(8,128)S(1)}, f32[8,2496]{1,0:T(8,128)S(1)}, u32[]{:S(2)}, u32[]{:S(2)}) collective-permute-start(f32[8,2496]{1,0:T(8,128)S(1)} %add.78), channel_id=1, source_target_pairs={{0,16},{4,20},{8,24},{12,28},{16,0},{20,4},{24,8},{28,12},{1,17},{... | collective-permute-start | bytes 239624 | tf_op jit(solution)/shard_map/ppermute | solution.py:36
  214.6 13.0 %collective-permute-start.46 = (bf16[96,2304]{1,0:T(8,128)(2,1)S(1)}, bf16[96,2304]{1,0:T(8,128)(2,1)S(1)}, u32[]{:S(2)}, u32[]{:S(2)}) collective-permute-start(bf16[96,2304]{1,0:T(8,128)(2,1)S(1)} %broadcast_select_fusion.2), channel_id=1, source_target_pairs={{0,4},{4,0},{8,12},{12,8},{16,20},{20,16},{24,28},{28,24},{1,5},{5... | collective-permute-start | bytes 1327112 | tf_op jit(solution)/shard_map/ppermute | solution.py:36
  217.5 31.7 %collective-permute-start.51 = (bf16[768,768]{1,0:T(8,128)(2,1)S(1)}, bf16[768,768]{1,0:T(8,128)(2,1)S(1)}, u32[]{:S(2)}, u32[]{:S(2)}) collective-permute-start(bf16[768,768]{1,0:T(8,128)(2,1)S(1)} %get-tuple-element.334), channel_id=1, source_target_pairs={{0,2},{1,3},{2,0},{3,1},{4,6},{5,7},{6,4},{7,5},{8,10},{9,11},{10,... | collective-permute-start | bytes 3538952 | tf_op jit(solution)/shard_map/ppermute | solution.py:36
  227.0 7.8 %collective-permute-start.45 = (f32[8,4032]{1,0:T(8,128)S(1)}, f32[8,4032]{1,0:T(8,128)S(1)}, u32[]{:S(2)}, u32[]{:S(2)}) collective-permute-start(f32[8,4032]{1,0:T(8,128)S(1)} %right_mlp.1), channel_id=1, source_target_pairs={{0,16},{4,20},{8,24},{12,28},{16,0},{20,4},{24,8},{28,12},{1,17},{... | collective-permute-start | bytes 387080 | tf_op jit(solution)/shard_map/ppermute | solution.py:36
  227.8 12.2 %collective-permute-start.49 = (bf16[48,2304]{1,0:T(8,128)(2,1)S(1)}, bf16[48,2304]{1,0:T(8,128)(2,1)S(1)}, u32[]{:S(2)}, u32[]{:S(2)}) collective-permute-start(bf16[48,2304]{1,0:T(8,128)(2,1)S(1)} %broadcast_select_fusion.5), channel_id=1, source_target_pairs={{0,8},{4,12},{8,0},{12,4},{16,24},{20,28},{24,16},{28,20},{1,9},{5... | collective-permute-start | bytes 663560 | tf_op jit(solution)/shard_map/ppermute | solution.py:36
  240.1 10.8 %collective-permute-start.50 = (bf16[48,2304]{1,0:T(8,128)(2,1)S(1)}, bf16[48,2304]{1,0:T(8,128)(2,1)S(1)}, u32[]{:S(2)}, u32[]{:S(2)}) collective-permute-start(bf16[48,2304]{1,0:T(8,128)(2,1)S(1)} %add_convert_fusion.3), channel_id=1, source_target_pairs={{0,16},{4,20},{8,24},{12,28},{16,0},{20,4},{24,8},{28,12},{1,17},{... | collective-permute-start | bytes 663560 | tf_op jit(solution)/shard_map/ppermute | solution.py:36
  256.3 8.8 %collective-permute-start.55 = (f32[8,1344]{1,0:T(8,128)S(1)}, f32[8,1344]{1,0:T(8,128)S(1)}, u32[]{:S(2)}, u32[]{:S(2)}) collective-permute-start(f32[8,1344]{1,0:T(8,128)S(1)} %add.86), channel_id=1, source_target_pairs={{0,4},{4,0},{8,12},{12,8},{16,20},{20,16},{24,28},{28,24},{1,5},{5... | collective-permute-start | bytes 129032 | tf_op jit(solution)/shard_map/ppermute | solution.py:36
  264.1 15.4 %collective-permute-start.54 = (bf16[96,2304]{1,0:T(8,128)(2,1)S(1)}, bf16[96,2304]{1,0:T(8,128)(2,1)S(1)}, u32[]{:S(2)}, u32[]{:S(2)}) collective-permute-start(bf16[96,2304]{1,0:T(8,128)(2,1)S(1)} %pad_maximum_fusion.1), channel_id=1, source_target_pairs={{0,4},{4,0},{8,12},{12,8},{16,20},{20,16},{24,28},{28,24},{1,5},{5... | collective-permute-start | bytes 1327112 | tf_op jit(solution)/shard_map/ppermute | solution.py:36
  (136 other events, 1452.5 us)

commit v2 on v1

--- a/solution.py
+++ b/solution.py
@@ -55,7 +55,7 @@
 
 SCALE = 10.0
 LIMITS = {
-    "pack": (56, 3), "embed": (8, 5), "attention_first": (10, 7), "attention_second": (10, 8), "mlp_first": (12, 7),
+    "pack_first": (56, 2), "pack_rest": (50, 3), "embed": (8, 5), "attention_first": (10, 7), "attention_second": (10, 8), "mlp_first": (12, 7),
     "mlp_second": (14, 7), "head": (24, 9), "down_send": (8, 3), "down_keep": (14, 4), "up_send": (14, 6),
     "up_keep": (20, 8), "attention_send": (14, 13), "attention_keep": (20, 15), "scatter": (8, 5),
     "orthonormal": (4, 3), "right_mlp": (16, 3), "right_attention": (12, 2), "update": (16, 4),
@@ -157,16 +157,22 @@
         copy.wait()
 
 
-def pack_kernel(meta_ref, qkv_ref, out_ref, up_ref, down_ref, tables_ref, first_ref, first_half, up_half, down_half, table_ref, table_half, sems):
+def pack_first_kernel(meta_ref, qkv_ref, out_ref, first_ref, first_half, sems):
     near, rest = qkv_ref.shape[0], out_ref.shape[0]
     size = first_half.shape[0]
+    fetch = Fetch(meta_ref, sems)
+    wait([
+        fetch.one(qkv_ref, first_ref.at[pl.ds(0, near), :]),
+        fetch.one(out_ref, first_ref.at[pl.ds(near, rest), :]),
+    ])
+    first_half[...] = first_ref[pl.ds(pl.multiple_of(meta_ref[1] * size, 32), size), :]
+
+
+def pack_rest_kernel(meta_ref, up_ref, down_ref, tables_ref, up_half, down_half, table_ref, table_half, sems):
     half = meta_ref[1]
+    size = up_half.shape[0]
     at = pl.multiple_of(half * size, 32)
     fetch = Fetch(meta_ref, sems)
-    firsts = [
-        fetch.one(qkv_ref, first_ref.at[pl.ds(0, near), :]),
-        fetch.one(out_ref, first_ref.at[pl.ds(near, rest), :]),
-    ]
     copies = [
         fetch.one(up_ref.at[pl.ds(at, size), :], up_half),
         fetch.one(down_ref.at[pl.ds(at, size), :], down_half),
@@ -176,8 +182,6 @@
     table_ref[:, :total] = tables_ref[...]
     rows = table_half.shape[0]
     table_half[...] = table_ref[pl.ds(pl.multiple_of(half * rows, 32), rows), :]
-    wait(firsts)
-    first_half[...] = first_ref[pl.ds(at, size), :]
     wait(copies)
 
 
@@ -790,13 +794,17 @@
     def cores(pieces):
         return tuple(core_swap(piece) for piece in pieces)
 
-    first_own, first_half, up_half, down_half, table_own, table_half = call(
-        pack_kernel, "pack",
-        (bf(all_rows, features), bf(all_rows // 2, features), bf(features // 2, hidden), bf(hidden // 2, features),
-         bf(columns, total), bf(columns // 2, total)),
-        (meta, w_qkv.T, w_out, w_up, w_down, tables.T), [SMEM] + [ANY] * 4 + [VMEM], [dma(4)],
+    first_own, first_half = call(
+        pack_first_kernel, "pack_first", (bf(all_rows, features), bf(all_rows // 2, features)),
+        (meta, w_qkv.T, w_out), [SMEM] + [ANY] * 2, [dma(2)],
     )
     order.mark(first_half)
+    up_half, down_half, table_own, table_half = call(
+        pack_rest_kernel, "pack_rest",
+        (bf(features // 2, hidden), bf(hidden // 2, features), bf(columns, total), bf(columns // 2, total)),
+        (order(meta), w_up, w_down, tables.T), [SMEM] + [ANY] * 2 + [VMEM], [dma(2)],
+    )
+    order.mark(table_half)
     first_far = [chip_swap(first_half)]
     part = bf(columns, rows + length)
     e_far, e_near, e_own, ids_rows = call(

time: 288 us -> 286 us (level)
  local copies, waits for them, and re-layouts: 17.5 us -> 14.6 us
    unnamed x222 -> x226, local copies, waits for them, and re-layouts: 14.8 us -> 11.9 us
    pallas_call x21 -> x22, Pallas kernels: 124 us -> 124 us  [call(): pl.pallas_call(kernel, out_shape=out_shape, in_specs=in_specs, scratch_sh...]
where the time goes in v2:
time: 286 us; the launch traced here: 281 us
  Pallas kernels  124 us (43%)
  waiting for transfers between devices  83.4 us (29%)
  starting transfers between devices  43.5 us (15%)
  local copies, waits for them, and re-layouts  14.6 us (5%)
  other arithmetic  12.7 us (4%)
  between operations  3.1 us (1%)
    pallas_call x22, Pallas kernels, call(): pl.pallas_call(kernel, out_shape=out_shape, in_specs=in_specs, scratch_sh...  124 us
    ppermute x57, waiting for transfers between devices, across(): return lax.ppermute(x, axis, [(i, i ^ bit) for i in range(size)])  83.4 us
    ppermute x57, starting transfers between devices, across(): return lax.ppermute(x, axis, [(i, i ^ bit) for i in range(size)])  43.5 us
    unnamed x226, local copies, waits for them, and re-layouts  11.9 us
  transfers between devices with their start and end apart: 57, of which 28 were waited for; matrix products, arithmetic and copies ran while one was open for 5% of the time, Pallas kernels for 41%

profile of v2, /device:TPU:0, one launch (start us, length us, event | category | flops | bytes accessed | tf_op | source)
XLA Modules:
  0.0 281.2 jit_solution(17378195598264534081)
XLA Ops:
  1.9 3.2 %pack_first.1 = (bf16[768,768]{1,0:T(8,128)(2,1)}, bf16[384,768]{1,0:T(8,128)(2,1)}) custom-call(s32[2]{0:T(128)} %pad_add_fusion.meta_ref, bf16[576,768]{1,0:T(8,128)(2,1)} %bitcast.69, bf16[192,768]{1,0:T(8,128)(2,1)} %weight.5), custom_call_target="tpu_custom_call" | custom-call | flops 23000000512 | bytes 20000000 | tf_op jit(solution)/shard_map/pack_first/pallas_call | solution.py:72
  5.1 3.0 %collective-permute-start = (bf16[384,768]{1,0:T(8,128)(2,1)}, bf16[384,768]{1,0:T(8,128)(2,1)}, u32[]{:S(2)}, u32[]{:S(2)}) collective-permute-start(bf16[384,768]{1,0:T(8,128)(2,1)} %get-tuple-element.196), channel_id=1, source_target_pairs={{0,2},{1,3},{2,0},{3,1},{4,6},{5,7},{6,4},{7,5},{8,10},{9,11},{10,... | collective-permute-start | bytes 1769480 | tf_op jit(solution)/shard_map/ppermute | solution.py:36
  10.6 5.1 %embed.1 = (bf16[2,192,640]{2,1,0:T(8,128)(2,1)}, bf16[192,768]{1,0:T(8,128)(2,1)S(1)}, bf16[192,768]{1,0:T(8,128)(2,1)S(1)}, s32[256,8]{1,0:T(8,128)S(1)}) custom-call(s32[2]{0:T(128)S(1)} %copy-done.55, s32[8]{0:T(128)S(1)} %copy-done.50, s32[8,256]{1,0:T(8,128)S(1)} %copy-done.46, s32[8,128]{1,0:T(8,128)S(1)} %copy-done.48, ...), custom_call_target="tpu_custom_call" | custom-call | flops 57500000256 | bytes 50000000 | tf_op jit(solution)/shard_map/embed/pallas_call | solution.py:72
  17.1 4.9 %collective-permute-done.c2a = bf16[384,768]{1,0:T(8,128)(2,1)} collective-permute-done((bf16[384,768]{1,0:T(8,128)(2,1)}, bf16[384,768]{1,0:T(8,128)(2,1)}, u32[]{:S(2)}, u32[]{:S(2)}) %collective-permute-start) | collective-permute-done | bytes 589856 | tf_op jit(solution)/shard_map/ppermute | solution.py:36
  25.0 10.0 %collective-permute-done.2.e2 = bf16[2,192,640]{2,1,0:T(8,128)(2,1)} collective-permute-done((bf16[2,192,640]{2,1,0:T(8,128)(2,1)}, bf16[2,192,640]{2,1,0:T(8,128)(2,1)}, u32[]{:S(2)}, u32[]{:S(2)}) %collective-permute-start.2) | collective-permute-done | bytes 491552 | tf_op jit(solution)/shard_map/ppermute | solution.py:36
  44.0 7.5 %attention_first.1 = (f32[512,768]{1,0:T(8,128)S(1)}, f32[512,1]{1,0:T(8,128)S(1)}, bf16[512,768]{1,0:T(8,128)(2,1)S(1)}, bf16[3,512,192]{2,1,0:T(8,128)(2,1)S(1...) custom-call(s32[2]{0:T(128)S(1)} %copy-done.55, ...), custom_call_target="tpu_custom_call" | custom-call | flops 80499998720 | bytes 70000000 | tf_op jit(solution)/shard_map/attention_first/pallas_call | solution.py:72
  51.5 3.8 %collective-permute-done.5.c2b = bf16[384,768]{1,0:T(8,128)(2,1)S(1)} collective-permute-done((bf16[384,768]{1,0:T(8,128)(2,1)}, bf16[384,768]{1,0:T(8,128)(2,1)S(1)}, u32[]{:S(2)}, u32[]{:S(2)}) %collective-permute-start.5) | collective-permute-done | bytes 589856 | tf_op jit(solution)/shard_map/ppermute | solution.py:36
  59.8 2.6 collective-permute-start.14
  64.0 8.8 %attention_second.1 = (f32[512,768]{1,0:T(8,128)S(1)}, f32[512,1]{1,0:T(8,128)S(1)}, bf16[512,768]{1,0:T(8,128)(2,1)S(1)}, bf16[3,512,192]{2,1,0:T(8,128)(2,1)S(...) custom-call(s32[2]{0:T(128)S(1)} %copy-done.55, ...), custom_call_target="tpu_custom_call" | custom-call | flops 92000002048 | bytes 80000000 | tf_op jit(solution)/shard_map/attention_second/pallas_call | solution.py:72
  73.0 3.8 %collective-permute-done.18.d2a = bf16[384,768]{1,0:T(8,128)(2,1)S(1)} collective-permute-done((bf16[384,768]{1,0:T(8,128)(2,1)S(1)}, bf16[384,768]{1,0:T(8,128)(2,1)S(1)}, u32[]{:S(2)}, u32[]{:S(2)}) %collective-permute-start.18) | collective-permute-done | bytes 589856 | tf_op jit(solution)/shard_map/ppermute | solution.py:36
  79.4 6.4 %mlp_first.1 = (bf16[512,768]{1,0:T(8,128)(2,1)S(1)}, bf16[512,768]{1,0:T(8,128)(2,1)S(1)}, f32[512,768]{1,0:T(8,128)S(1)}, f32[512,768]{1,0:T(8,128)S(1)}, f32[512,768]{1,0:T(8,128)S(1)}) custom-call(s32[2]{0:T(128)S(1)} %copy-done.55, bf16[512,768]{1,0:T(8,128)(2,1)S(1)} %get-tuple-element.236.h1b_ref, f32[8,4096]{1,0:T(8,128)S(1)} %concatenate.9.b0.s0, ...), custom_call_target="tpu_custom_call" | custom-call | flops 80499998720 | bytes 70000000 | tf_op jit(solution)/shard_map/mlp_first/pallas_call | solution.py:72
  87.6 2.6 collective-permute-done.19.d2b
  93.1 7.6 %mlp_second.1 = (bf16[512,768]{1,0:T(8,128)(2,1)S(1)}, bf16[512,768]{1,0:T(8,128)(2,1)S(1)}, f32[512,768]{1,0:T(8,128)S(1)}, f32[512,768]{1,0:T(8,128)S(1)}, f32...) custom-call(s32[2]{0:T(128)S(1)} %copy-done.55, ...), custom_call_target="tpu_custom_call" | custom-call | flops 80499998720 | bytes 70000000 | tf_op jit(solution)/shard_map/mlp_second/pallas_call | solution.py:72
  105.2 8.7 %head.1 = (f32[512,768]{1,0:T(8,128)S(1)}, bf16[512,768]{1,0:T(8,128)(2,1)S(1)}, f32[1,128]{1,0:T(1,128)S(1)}, f32[1,2304]{1,0:T(1,128)S(1)}, f32[3,768]{1,0:T(4...) custom-call(s32[2]{0:T(128)S(1)} %copy-done.55, s32[8]{0:T(128)S(1)} %copy-done.51, ...), custom_call_target="tpu_custom_call" | custom-call | flops 103499997184 | bytes 90000000 | tf_op jit(solution)/shard_map/head/pallas_call | solution.py:72
  120.6 7.3 %up_send.1 = (bf16[2,768,768]{2,1,0:T(8,128)(2,1)S(1)}, f32[2,8,768]{2,1,0:T(8,128)S(1)}, f32[512,768]{1,0:T(8,128)S(1)}, f32[2,1,768]{2,1,0:T(1,128)S(1)}) custom-call(s32[2]{0:T(128)S(1)} %copy-done.55, bf16[512,768]{1,0:T(8,128)(2,1)S(1)} %get-tuple-element.268.dzb_ref, bf16[512,768]{1,0:T(8,128)(2,1)S(1)} %get-tuple-element.236.h1b_ref, ...), custom_call_target="tpu_custom_call" | custom-call | flops 69000003584 | bytes 60000000 | tf_op jit(solution)/shard_map/up_send/pallas_call | solution.py:72
  128.1 3.3 %down_keep.1 = (bf16[384,768]{1,0:T(8,128)(2,1)}, bf16[384,768]{1,0:T(8,128)(2,1)S(1)}, f32[768,768]{1,0:T(8,128)S(1)}, f32[2,8,768]{2,1,0:T(8,128)S(1)}) custom-call(bf16[512,768]{1,0:T(8,128)(2,1)S(1)} %get-tuple-element.268.dzb_ref, bf16[512,768]{1,0:T(8,128)(2,1)S(1)} %get-tuple-element.262.a0, bf16[512,768]{1,0:T(8,128)(2,1)S(1)} %get-tuple-element.263.a2, ...), custom_call_target="tpu_custom_call" | custom-call | flops 46000001024 | bytes 40000000 | tf_op jit(solution)/shard_map/down_keep/pallas_call | solution.py:72
  133.5 10.3 %up_keep.1 = (bf16[576,768]{1,0:T(8,128)(2,1)}, bf16[576,768]{1,0:T(8,128)(2,1)S(1)}, f32[768,768]{1,0:T(8,128)S(1)}, f32[2,8,768]{2,1,0:T(8,128)S(1)}, f32[512,...) custom-call(s32[2]{0:T(128)S(1)} %copy-done.55, ...), custom_call_target="tpu_custom_call" | custom-call | flops 92000002048 | bytes 80000000 | tf_op jit(solution)/shard_map/up_keep/pallas_call | solution.py:72
  144.0 12.2 %attention_send.1 = (bf16[2,768,768]{2,1,0:T(8,128)(2,1)S(1)}, f32[2,16,2496]{2,1,0:T(8,128)S(1)}, f32[512,768]{1,0:T(8,128)S(1)}) custom-call(s32[2]{0:T(128)S(1)} %copy-done.55, bf16[512,768]{1,0:T(8,128)(2,1)S(1)} %get-tuple-element.289.dz1b_ref, bf16[512,768]{1,0:T(8,128)(2,1)S(1)} %copy-done.73, bf16[3,512,192]{2,1,0:T(8,128)(2,1)S(1)} %copy-done.75, ...), custom_call_target="tpu_custom_call" | custom-call | flops 149500002304 | bytes 130000000 | tf_op jit(solution)/shard_map/attention_send/pallas_call | solution.py:72
  158.0 2.8 %collective-permute-done.35.near_ref = bf16[2,768,768]{2,1,0:T(8,128)(2,1)S(1)} collective-permute-done((bf16[2,768,768]{2,1,0:T(8,128)(2,1)S(1)}, bf16[2,768,768]{2,1,0:T(8,128)(2,1)S(1)}, u32[]{:S(2)}, u32[]{:S(2)}) %collective-permute-start.35) | collective-permute-done | bytes 2359328 | tf_op jit(solution)/shard_map/ppermute | solution.py:36
  160.9 15.3 %attention_keep.1 = (bf16[768,768]{1,0:T(8,128)(2,1)S(1)}, f32[768,768]{1,0:T(8,128)S(1)}, f32[2,16,2496]{2,1,0:T(8,128)S(1)}, f32[2,16,2496]{2,1,0:T(8,128)S(1)...) custom-call(s32[2]{0:T(128)S(1)} %copy-done.55, ...), custom_call_target="tpu_custom_call" | custom-call | flops 172499992576 | bytes 150000000 | tf_op jit(solution)/shard_map/attention_keep/pallas_call | solution.py:72
  182.5 5.0 %collective-permute-done.38 = f32[16,2496]{1,0:T(8,128)S(1)} collective-permute-done((f32[16,2496]{1,0:T(8,128)S(1)}, f32[16,2496]{1,0:T(8,128)S(1)}, u32[]{:S(2)}, u32[]{:S(2)}) %collective-permute-start.38) | collective-permute-done | bytes 159776 | tf_op jit(solution)/shard_map/ppermute | solution.py:36
  188.5 3.6 %collective-permute-done.39 = f32[8,2496]{1,0:T(8,128)S(1)} collective-permute-done((f32[8,2496]{1,0:T(8,128)S(1)}, f32[8,2496]{1,0:T(8,128)S(1)}, u32[]{:S(2)}, u32[]{:S(2)}) %collective-permute-start.39) | collective-permute-done | bytes 79904 | tf_op jit(solution)/shard_map/ppermute | solution.py:36
  192.0 5.9 %collective-permute-done.36.r2 = bf16[2,512,192]{2,1,0:T(8,128)(2,1)S(1)} collective-permute-done((bf16[2,512,192]{2,1,0:T(8,128)(2,1)S(1)}, bf16[2,512,192]{2,1,0:T(8,128)(2,1)S(1)}, u32[]{:S(2)}, u32[]{:S(2)}) %collective-permute-start.36) | collective-permute-done | bytes 393248 | tf_op jit(solution)/shard_map/ppermute | solution.py:36
  208.6 4.1 %scatter.1 = bf16[192,2304]{1,0:T(8,128)(2,1)S(1)} custom-call(s32[256,8]{1,0:T(8,128)S(1)} %copy-done.67, bf16[512,192]{1,0:T(8,128)(2,1)S(1)} %copy-done.65, bf16[512,192]{1,0:T(8,128)(2,1)} %collective-permute-done.43.r1, bf16[2,512,192]{2,1,0:T(8,128)(2,1)S(1)} %collective-permute-done.36.r2, bf16[2,512,192]{2,1,0:T(8,128)(2,1)} %collective-permute-done.44.r3, ...), custom_call_target="tpu_custom_call" | custom-call | flops 5750000128 | bytes 5000000 | tf_op jit(solution)/shard_map/scatter/pallas_call | solution.py:72
  217.2 5.6 %collective-permute-done.40.got_b.refs_1_ = bf16[576,768]{1,0:T(8,128)(2,1)S(1)} collective-permute-done((bf16[576,768]{1,0:T(8,128)(2,1)}, bf16[576,768]{1,0:T(8,128)(2,1)S(1)}, u32[]{:S(2)}, u32[]{:S(2)}) %collective-permute-start.40) | collective-permute-done | bytes 884768 | tf_op jit(solution)/shard_map/ppermute | solution.py:36
  226.6 6.5 %collective-permute-done.45 = f32[8,4032]{1,0:T(8,128)S(1)} collective-permute-done((f32[8,4032]{1,0:T(8,128)S(1)}, f32[8,4032]{1,0:T(8,128)S(1)}, u32[]{:S(2)}, u32[]{:S(2)}) %collective-permute-start.45) | collective-permute-done | bytes 129056 | tf_op jit(solution)/shard_map/ppermute | solution.py:36
  234.0 4.1 %collective-permute-done.47 = f32[8,4032]{1,0:T(8,128)S(1)} collective-permute-done((f32[8,4032]{1,0:T(8,128)S(1)}, f32[8,4032]{1,0:T(8,128)S(1)}, u32[]{:S(2)}, u32[]{:S(2)}) %collective-permute-start.47) | collective-permute-done | bytes 129056 | tf_op jit(solution)/shard_map/ppermute | solution.py:36
  238.9 5.5 %collective-permute-done.48 = f32[8,4032]{1,0:T(8,128)S(1)} collective-permute-done((f32[8,4032]{1,0:T(8,128)S(1)}, f32[8,4032]{1,0:T(8,128)S(1)}, u32[]{:S(2)}, u32[]{:S(2)}) %collective-permute-start.48) | collective-permute-done | bytes 129056 | tf_op jit(solution)/shard_map/ppermute | solution.py:36
  245.0 2.5 collective-permute-done.51.got.refs_0_
  249.4 5.1 %update.4 = (f32[768,768]{1,0:T(8,128)}, f32[768,768]{1,0:T(8,128)}, f32[768,768]{1,0:T(8,128)}) custom-call(f32[768,768]{1,0:T(8,128)S(1)} %copy-done.63, bf16[768,768]{1,0:T(8,128)(2,1)S(1)} %copy-done.16, f32[768,768]{1,0:T(8,128)S(1)} %copy-done.10, f32[8,768]{1,0:T(8,128)S(1)} %copy-done.53, f32[8,768]{1,0:T(8,128)S(1)} %get-tuple-element.380.second_ref, ...), custom_call_target="tpu_custom_call" | custom-call | flops 4600000000 | bytes 4000000 | tf_op jit(solution)/shard_map/update/pallas_call | solution.py:72
  256.5 4.7 %update.5 = (f32[768,768]{1,0:T(8,128)}, f32[768,768]{1,0:T(8,128)}, f32[768,768]{1,0:T(8,128)}) custom-call(f32[768,768]{1,0:T(8,128)S(1)} %copy-done.61, bf16[768,768]{1,0:T(8,128)(2,1)S(1)} %copy-done.19, f32[768,768]{1,0:T(8,128)S(1)} %copy-done.11, f32[8,768]{1,0:T(8,128)S(1)} %copy-done.52, f32[8,768]{1,0:T(8,128)S(1)} %get-tuple-element.379.second_ref, ...), custom_call_target="tpu_custom_call" | custom-call | flops 4600000000 | bytes 4000000 | tf_op jit(solution)/shard_map/update/pallas_call | solution.py:72
  274.3 3.4 %update.6 = (f32[576,768]{1,0:T(8,128)}, f32[576,768]{1,0:T(8,128)}, f32[576,768]{1,0:T(8,128)}) custom-call(f32[768,768]{1,0:T(8,128)S(1)} %copy-done.59, bf16[576,768]{1,0:T(8,128)(2,1)S(1)} %bitcast.70, f32[576,768]{1,0:T(8,128)S(1)} %bitcast.68, f32[8,576]{1,0:T(8,128)S(1)} %get-tuple-element.392.first_ref, f32[8,768]{1,0:T(8,128)S(1)} %copy-done.54, ...), custom_call_target="tpu_custom_call" | custom-call | flops 4600000000 | bytes 4000000 | tf_op jit(solution)/shard_map/update/pallas_call | solution.py:72
  (375 shorter events, 93.3 us)
Async XLA Ops:
  0.7 38.6 %collective-permute-start.7 = (bf16[768,768]{1,0:T(8,128)(2,1)}, bf16[768,768]{1,0:T(8,128)(2,1)}, u32[]{:S(2)}, u32[]{:S(2)}) collective-permute-start(bf16[768,768]{1,0:T(8,128)(2,1)} %weight.4), channel_id=1, source_target_pairs={{0,1},{1,0},{2,3},{3,2},{4,5},{5,4},{6,7},{7,6},{8,9},{9,8},{10,11... | collective-permute-start | bytes 3538952 | tf_op jit(solution)/shard_map/ppermute | solution.py:36
  1.2 38.2 %collective-permute-start.8 = (bf16[768,768]{1,0:T(8,128)(2,1)}, bf16[768,768]{1,0:T(8,128)(2,1)}, u32[]{:S(2)}, u32[]{:S(2)}) collective-permute-start(bf16[768,768]{1,0:T(8,128)(2,1)} %weight.3), channel_id=1, source_target_pairs={{0,1},{1,0},{2,3},{3,2},{4,5},{5,4},{6,7},{7,6},{8,9},{9,8},{10,11... | collective-permute-start | bytes 3538952 | tf_op jit(solution)/shard_map/ppermute | solution.py:36
  5.1 16.9 %collective-permute-start = (bf16[384,768]{1,0:T(8,128)(2,1)}, bf16[384,768]{1,0:T(8,128)(2,1)}, u32[]{:S(2)}, u32[]{:S(2)}) collective-permute-start(bf16[384,768]{1,0:T(8,128)(2,1)} %get-tuple-element.196), channel_id=1, source_target_pairs={{0,2},{1,3},{2,0},{3,1},{4,6},{5,7},{6,4},{7,5},{8,10},{9,11},{10,... | collective-permute-start | bytes 1769480 | tf_op jit(solution)/shard_map/ppermute | solution.py:36
  8.1 32.8 %collective-permute-start.9 = (bf16[768,768]{1,0:T(8,128)(2,1)}, bf16[768,768]{1,0:T(8,128)(2,1)S(1)}, u32[]{:S(2)}, u32[]{:S(2)}) collective-permute-start(bf16[768,768]{1,0:T(8,128)(2,1)} %get-tuple-element.209.c0), channel_id=1, source_target_pairs={{0,1},{1,0},{2,3},{3,2},{4,5},{5,4},{6,7},{7,6},{8,9},{9,8},{10,11... | collective-permute-start | bytes 3538952 | tf_op jit(solution)/shard_map/ppermute | solution.py:36
  10.0 28.6 %collective-permute-start.10 = (bf16[192,2304]{1,0:T(8,128)(2,1)S(1)}, bf16[192,2304]{1,0:T(8,128)(2,1)}, u32[]{:S(2)}, u32[]{:S(2)}) collective-permute-start(bf16[192,2304]{1,0:T(8,128)(2,1)S(1)} %get-tuple-element.200.table_ref.t0), channel_id=1, source_target_pairs={{0,1},{1,0},{2,3},{3,2},{4,5},{5,4},{6,7},{7,6},{8,9},{9,8},{10,11... | collective-permute-start | bytes 2654216 | tf_op jit(solution)/shard_map/ppermute | solution.py:36
  22.0 13.0 %collective-permute-start.2 = (bf16[2,192,640]{2,1,0:T(8,128)(2,1)}, bf16[2,192,640]{2,1,0:T(8,128)(2,1)}, u32[]{:S(2)}, u32[]{:S(2)}) collective-permute-start(bf16[2,192,640]{2,1,0:T(8,128)(2,1)} %get-tuple-element.201), channel_id=1, source_target_pairs={{0,2},{1,3},{2,0},{3,1},{4,6},{5,7},{6,4},{7,5},{8,10},{9,11},{10,... | collective-permute-start | bytes 1474568 | tf_op jit(solution)/shard_map/ppermute | solution.py:36
  39.4 15.9 %collective-permute-start.5 = (bf16[384,768]{1,0:T(8,128)(2,1)}, bf16[384,768]{1,0:T(8,128)(2,1)S(1)}, u32[]{:S(2)}, u32[]{:S(2)}) collective-permute-start(bf16[384,768]{1,0:T(8,128)(2,1)} %collective-permute-done.c2a), channel_id=1, source_target_pairs={{0,4},{4,0},{8,12},{12,8},{16,20},{20,16},{24,28},{28,24},{1,5},{5... | collective-permute-start | bytes 1769480 | tf_op jit(solution)/shard_map/ppermute | solution.py:36
  40.9 10.6 %collective-permute-start.6 = (f32[8,4096]{1,0:T(8,128)S(1)}, f32[8,4096]{1,0:T(8,128)S(1)}, u32[]{:S(2)}, u32[]{:S(2)}) collective-permute-start(f32[8,4096]{1,0:T(8,128)S(1)} %concatenate.9.b0.s0), channel_id=1, source_target_pairs={{0,2},{1,3},{2,0},{3,1},{4,6},{5,7},{6,4},{7,5},{8,10},{9,11},{10,... | collective-permute-start | bytes 393224 | tf_op jit(solution)/shard_map/ppermute | solution.py:36
  42.4 16.8 %collective-permute-start.4 = (bf16[384,768]{1,0:T(8,128)(2,1)}, bf16[384,768]{1,0:T(8,128)(2,1)}, u32[]{:S(2)}, u32[]{:S(2)}) collective-permute-start(bf16[384,768]{1,0:T(8,128)(2,1)} %copy-done.37), channel_id=1, source_target_pairs={{0,2},{1,3},{2,0},{3,1},{4,6},{5,7},{6,4},{7,5},{8,10},{9,11},{10,... | collective-permute-start | bytes 1769480 | tf_op jit(solution)/shard_map/ppermute | solution.py:36
  55.4 8.5 %collective-permute-start.16 = (bf16[384,768]{1,0:T(8,128)(2,1)}, bf16[384,768]{1,0:T(8,128)(2,1)S(1)}, u32[]{:S(2)}, u32[]{:S(2)}) collective-permute-start(bf16[384,768]{1,0:T(8,128)(2,1)} %collective-permute-done.c2a), channel_id=1, source_target_pairs={{0,1},{1,0},{2,3},{3,2},{4,5},{5,4},{6,7},{7,6},{8,9},{9,8},{10,11... | collective-permute-start | bytes 1769480 | tf_op jit(solution)/shard_map/ppermute | solution.py:36
  55.4 8.6 %collective-permute-start.17 = (bf16[384,768]{1,0:T(8,128)(2,1)S(1)}, bf16[384,768]{1,0:T(8,128)(2,1)S(1)}, u32[]{:S(2)}, u32[]{:S(2)}) collective-permute-start(bf16[384,768]{1,0:T(8,128)(2,1)S(1)} %collective-permute-done.5.c2b), channel_id=1, source_target_pairs={{0,1},{1,0},{2,3},{3,2},{4,5},{5,4},{6,7},{7,6},{8,9},{9,8},{10,11... | collective-permute-start | bytes 1769480 | tf_op jit(solution)/shard_map/ppermute | solution.py:36
  59.2 26.7 %collective-permute-start.21 = (bf16[384,768]{1,0:T(8,128)(2,1)}, bf16[384,768]{1,0:T(8,128)(2,1)}, u32[]{:S(2)}, u32[]{:S(2)}) collective-permute-start(bf16[384,768]{1,0:T(8,128)(2,1)} %collective-permute-done.4.u2a), channel_id=1, source_target_pairs={{0,4},{4,0},{8,12},{12,8},{16,20},{20,16},{24,28},{28,24},{1,5},{5... | collective-permute-start | bytes 1769480 | tf_op jit(solution)/shard_map/ppermute | solution.py:36
  59.8 13.1 %collective-permute-start.14 = (f32[8,128]{1,0:T(8,128)S(1)}, f32[8,128]{1,0:T(8,128)S(1)}, u32[]{:S(2)}, u32[]{:S(2)}) collective-permute-start(f32[8,128]{1,0:T(8,128)S(1)} %add.72), channel_id=1, source_target_pairs={{0,16},{4,20},{8,24},{12,28},{16,0},{20,4},{24,8},{28,12},{1,17},{... | collective-permute-start | bytes 12296 | tf_op jit(solution)/shard_map/ppermute | solution.py:36
  62.4 14.3 %collective-permute-start.18 = (bf16[384,768]{1,0:T(8,128)(2,1)S(1)}, bf16[384,768]{1,0:T(8,128)(2,1)S(1)}, u32[]{:S(2)}, u32[]{:S(2)}) collective-permute-start(bf16[384,768]{1,0:T(8,128)(2,1)S(1)} %copy-done.36), channel_id=1, source_target_pairs={{0,2},{1,3},{2,0},{3,1},{4,6},{5,7},{6,4},{7,5},{8,10},{9,11},{10,... | collective-permute-start | bytes 1769480 | tf_op jit(solution)/shard_map/ppermute | solution.py:36
  76.7 13.4 %collective-permute-start.19 = (bf16[384,768]{1,0:T(8,128)(2,1)S(1)}, bf16[384,768]{1,0:T(8,128)(2,1)S(1)}, u32[]{:S(2)}, u32[]{:S(2)}) collective-permute-start(bf16[384,768]{1,0:T(8,128)(2,1)S(1)} %collective-permute-done.18.d2a), channel_id=1, source_target_pairs={{0,4},{4,0},{8,12},{12,8},{16,20},{20,16},{24,28},{28,24},{1,5},{5... | collective-permute-start | bytes 1769480 | tf_op jit(solution)/shard_map/ppermute | solution.py:36
  77.9 9.6 %collective-permute-start.20 = (bf16[96,2304]{1,0:T(8,128)(2,1)S(1)}, bf16[96,2304]{1,0:T(8,128)(2,1)S(1)}, u32[]{:S(2)}, u32[]{:S(2)}) collective-permute-start(bf16[96,2304]{1,0:T(8,128)(2,1)S(1)} %copy-done.39), channel_id=1, source_target_pairs={{0,2},{1,3},{2,0},{3,1},{4,6},{5,7},{6,4},{7,5},{8,10},{9,11},{10,... | collective-permute-start | bytes 1327112 | tf_op jit(solution)/shard_map/ppermute | solution.py:36
  90.6 12.1 %collective-permute-start.26 = (bf16[96,2304]{1,0:T(8,128)(2,1)S(1)}, bf16[96,2304]{1,0:T(8,128)(2,1)S(1)}, u32[]{:S(2)}, u32[]{:S(2)}) collective-permute-start(bf16[96,2304]{1,0:T(8,128)(2,1)S(1)} %collective-permute-done.20.t2a), channel_id=1, source_target_pairs={{0,4},{4,0},{8,12},{12,8},{16,20},{20,16},{24,28},{28,24},{1,5},{5... | collective-permute-start | bytes 1327112 | tf_op jit(solution)/shard_map/ppermute | solution.py:36
  116.2 11.8 %collective-permute-start.30 = (bf16[2,768,768]{2,1,0:T(8,128)(2,1)S(1)}, bf16[2,768,768]{2,1,0:T(8,128)(2,1)S(1)}, u32[]{:S(2)}, u32[]{:S(2)}) collective-permute-start(bf16[2,768,768]{2,1,0:T(8,128)(2,1)S(1)} %get-tuple-element.255), channel_id=1, source_target_pairs={{0,1},{1,0},{2,3},{3,2},{4,5},{5,4},{6,7},{7,6},{8,9},{9,8},{10,11... | collective-permute-start | bytes 7077896 | tf_op jit(solution)/shard_map/ppermute | solution.py:36
  119.1 37.1 %collective-permute-start.32 = (bf16[192,2304]{1,0:T(8,128)(2,1)}, bf16[192,2304]{1,0:T(8,128)(2,1)}, u32[]{:S(2)}, u32[]{:S(2)}) collective-permute-start(bf16[192,2304]{1,0:T(8,128)(2,1)} %fusion.1), channel_id=1, source_target_pairs={{0,2},{1,3},{2,0},{3,1},{4,6},{5,7},{6,4},{7,5},{8,10},{9,11},{10,... | collective-permute-start | bytes 2654216 | tf_op jit(solution)/shard_map/ppermute | solution.py:36
  132.8 23.4 %collective-permute-start.31 = (bf16[384,768]{1,0:T(8,128)(2,1)}, bf16[384,768]{1,0:T(8,128)(2,1)}, u32[]{:S(2)}, u32[]{:S(2)}) collective-permute-start(bf16[384,768]{1,0:T(8,128)(2,1)} %get-tuple-element.265), channel_id=1, source_target_pairs={{0,2},{1,3},{2,0},{3,1},{4,6},{5,7},{6,4},{7,5},{8,10},{9,11},{10,... | collective-permute-start | bytes 1769480 | tf_op jit(solution)/shard_map/ppermute | solution.py:36
  156.5 22.2 %collective-permute-start.34 = (bf16[576,768]{1,0:T(8,128)(2,1)}, bf16[576,768]{1,0:T(8,128)(2,1)}, u32[]{:S(2)}, u32[]{:S(2)}) collective-permute-start(bf16[576,768]{1,0:T(8,128)(2,1)} %get-tuple-element.288), channel_id=1, source_target_pairs={{0,2},{1,3},{2,0},{3,1},{4,6},{5,7},{6,4},{7,5},{8,10},{9,11},{10,... | collective-permute-start | bytes 2654216 | tf_op jit(solution)/shard_map/ppermute | solution.py:36
  182.0 16.0 %collective-permute-start.36 = (bf16[2,512,192]{2,1,0:T(8,128)(2,1)S(1)}, bf16[2,512,192]{2,1,0:T(8,128)(2,1)S(1)}, u32[]{:S(2)}, u32[]{:S(2)}) collective-permute-start(bf16[2,512,192]{2,1,0:T(8,128)(2,1)S(1)} %get-tuple-element.306), channel_id=1, source_target_pairs={{0,2},{1,3},{2,0},{3,1},{4,6},{5,7},{6,4},{7,5},{8,10},{9,11},{10,... | collective-permute-start | bytes 1179656 | tf_op jit(solution)/shard_map/ppermute | solution.py:36
  188.5 16.8 %collective-permute-start.43 = (bf16[512,192]{1,0:T(8,128)(2,1)}, bf16[512,192]{1,0:T(8,128)(2,1)}, u32[]{:S(2)}, u32[]{:S(2)}) collective-permute-start(bf16[512,192]{1,0:T(8,128)(2,1)} %get-tuple-element.323), channel_id=1, source_target_pairs={{0,1},{1,0},{2,3},{3,2},{4,5},{5,4},{6,7},{7,6},{8,9},{9,8},{10,11... | collective-permute-start | bytes 589832 | tf_op jit(solution)/shard_map/ppermute | solution.py:36
  200.2 22.7 %collective-permute-start.40 = (bf16[576,768]{1,0:T(8,128)(2,1)}, bf16[576,768]{1,0:T(8,128)(2,1)S(1)}, u32[]{:S(2)}, u32[]{:S(2)}) collective-permute-start(bf16[576,768]{1,0:T(8,128)(2,1)} %copy-done.22), channel_id=1, source_target_pairs={{0,2},{1,3},{2,0},{3,1},{4,6},{5,7},{6,4},{7,5},{8,10},{9,11},{10,... | collective-permute-start | bytes 2654216 | tf_op jit(solution)/shard_map/ppermute | solution.py:36
  204.7 8.0 %collective-permute-start.42 = (f32[8,2496]{1,0:T(8,128)S(1)}, f32[8,2496]{1,0:T(8,128)S(1)}, u32[]{:S(2)}, u32[]{:S(2)}) collective-permute-start(f32[8,2496]{1,0:T(8,128)S(1)} %add.78), channel_id=1, source_target_pairs={{0,16},{4,20},{8,24},{12,28},{16,0},{20,4},{24,8},{28,12},{1,17},{... | collective-permute-start | bytes 239624 | tf_op jit(solution)/shard_map/ppermute | solution.py:36
  212.8 13.0 %collective-permute-start.46 = (bf16[96,2304]{1,0:T(8,128)(2,1)S(1)}, bf16[96,2304]{1,0:T(8,128)(2,1)S(1)}, u32[]{:S(2)}, u32[]{:S(2)}) collective-permute-start(bf16[96,2304]{1,0:T(8,128)(2,1)S(1)} %broadcast_select_fusion.2), channel_id=1, source_target_pairs={{0,4},{4,0},{8,12},{12,8},{16,20},{20,16},{24,28},{28,24},{1,5},{5... | collective-permute-start | bytes 1327112 | tf_op jit(solution)/shard_map/ppermute | solution.py:36
  215.8 31.7 %collective-permute-start.51 = (bf16[768,768]{1,0:T(8,128)(2,1)S(1)}, bf16[768,768]{1,0:T(8,128)(2,1)S(1)}, u32[]{:S(2)}, u32[]{:S(2)}) collective-permute-start(bf16[768,768]{1,0:T(8,128)(2,1)S(1)} %get-tuple-element.336), channel_id=1, source_target_pairs={{0,2},{1,3},{2,0},{3,1},{4,6},{5,7},{6,4},{7,5},{8,10},{9,11},{10,... | collective-permute-start | bytes 3538952 | tf_op jit(solution)/shard_map/ppermute | solution.py:36
  225.3 7.8 %collective-permute-start.45 = (f32[8,4032]{1,0:T(8,128)S(1)}, f32[8,4032]{1,0:T(8,128)S(1)}, u32[]{:S(2)}, u32[]{:S(2)}) collective-permute-start(f32[8,4032]{1,0:T(8,128)S(1)} %right_mlp.1), channel_id=1, source_target_pairs={{0,16},{4,20},{8,24},{12,28},{16,0},{20,4},{24,8},{28,12},{1,17},{... | collective-permute-start | bytes 387080 | tf_op jit(solution)/shard_map/ppermute | solution.py:36
  226.0 12.2 %collective-permute-start.49 = (bf16[48,2304]{1,0:T(8,128)(2,1)S(1)}, bf16[48,2304]{1,0:T(8,128)(2,1)S(1)}, u32[]{:S(2)}, u32[]{:S(2)}) collective-permute-start(bf16[48,2304]{1,0:T(8,128)(2,1)S(1)} %broadcast_select_fusion.5), channel_id=1, source_target_pairs={{0,8},{4,12},{8,0},{12,4},{16,24},{20,28},{24,16},{28,20},{1,9},{5... | collective-permute-start | bytes 663560 | tf_op jit(solution)/shard_map/ppermute | solution.py:36
  238.3 10.8 %collective-permute-start.50 = (bf16[48,2304]{1,0:T(8,128)(2,1)S(1)}, bf16[48,2304]{1,0:T(8,128)(2,1)S(1)}, u32[]{:S(2)}, u32[]{:S(2)}) collective-permute-start(bf16[48,2304]{1,0:T(8,128)(2,1)S(1)} %add_convert_fusion.3), channel_id=1, source_target_pairs={{0,16},{4,20},{8,24},{12,28},{16,0},{20,4},{24,8},{28,12},{1,17},{... | collective-permute-start | bytes 663560 | tf_op jit(solution)/shard_map/ppermute | solution.py:36
  254.6 8.8 %collective-permute-start.55 = (f32[8,1344]{1,0:T(8,128)S(1)}, f32[8,1344]{1,0:T(8,128)S(1)}, u32[]{:S(2)}, u32[]{:S(2)}) collective-permute-start(f32[8,1344]{1,0:T(8,128)S(1)} %add.86), channel_id=1, source_target_pairs={{0,4},{4,0},{8,12},{12,8},{16,20},{20,16},{24,28},{28,24},{1,5},{5... | collective-permute-start | bytes 129032 | tf_op jit(solution)/shard_map/ppermute | solution.py:36
  262.4 15.4 %collective-permute-start.54 = (bf16[96,2304]{1,0:T(8,128)(2,1)S(1)}, bf16[96,2304]{1,0:T(8,128)(2,1)S(1)}, u32[]{:S(2)}, u32[]{:S(2)}) collective-permute-start(bf16[96,2304]{1,0:T(8,128)(2,1)S(1)} %pad_maximum_fusion.1), channel_id=1, source_target_pairs={{0,4},{4,0},{8,12},{12,8},{16,20},{20,16},{24,28},{28,24},{1,5},{5... | collective-permute-start | bytes 1327112 | tf_op jit(solution)/shard_map/ppermute | solution.py:36
  (138 other events, 1447.8 us)

commit v3 on v2

--- a/solution.py
+++ b/solution.py
@@ -665,7 +665,7 @@
 
 def update(replicas, part, gots, first_row, weight, moment, first, second):
     rows, cols = weight.shape
-    block = 256
+    block = 128
     spec = pl.BlockSpec((rows, block), lambda i: (0, i))
     out = shape(rows, cols)
     mine = lambda size: pl.BlockSpec((size, block), lambda i: (first_row // size, i))

time: 286 us -> 290 us (1.014)
  Pallas kernels: 124 us -> 129 us
    pallas_call x22, Pallas kernels: 124 us -> 129 us  [call(): pl.pallas_call(kernel, out_shape=out_shape, in_specs=in_specs, scratch_sh...]
  transfers between devices with their start and end apart: 57 -> 57, of which waited for: 28 -> 27; matrix products, arithmetic and copies ran while one was open for 5% -> 5% of each run, Pallas kernels for 41% -> 42%
where the time goes in v3:
time: 290 us; the launch traced here: 285 us
  Pallas kernels  129 us (44%)
  waiting for transfers between devices  82.1 us (28%)
  starting transfers between devices  44.4 us (15%)
  local copies, waits for them, and re-layouts  14.6 us (5%)
  other arithmetic  12.7 us (4%)
  between operations  3.2 us (1%)
    pallas_call x22, Pallas kernels, call(): pl.pallas_call(kernel, out_shape=out_shape, in_specs=in_specs, scratch_sh...  129 us
    ppermute x57, waiting for transfers between devices, across(): return lax.ppermute(x, axis, [(i, i ^ bit) for i in range(size)])  82.1 us
    ppermute x57, starting transfers between devices, across(): return lax.ppermute(x, axis, [(i, i ^ bit) for i in range(size)])  44.4 us
    unnamed x226, local copies, waits for them, and re-layouts  11.9 us
  transfers between devices with their start and end apart: 57, of which 27 were waited for; matrix products, arithmetic and copies ran while one was open for 5% of the time, Pallas kernels for 42%

profile of v3, /device:TPU:0, one launch (start us, length us, event | category | flops | bytes accessed | tf_op | source)
XLA Modules:
  0.0 285.4 jit_solution(10179513863445432149)
XLA Ops:
  1.9 3.2 %pack_first.1 = (bf16[768,768]{1,0:T(8,128)(2,1)}, bf16[384,768]{1,0:T(8,128)(2,1)}) custom-call(s32[2]{0:T(128)} %pad_add_fusion.meta_ref, bf16[576,768]{1,0:T(8,128)(2,1)} %bitcast.69, bf16[192,768]{1,0:T(8,128)(2,1)} %weight.5), custom_call_target="tpu_custom_call" | custom-call | flops 23000000512 | bytes 20000000 | tf_op jit(solution)/shard_map/pack_first/pallas_call | solution.py:72
  5.1 3.0 %collective-permute-start = (bf16[384,768]{1,0:T(8,128)(2,1)}, bf16[384,768]{1,0:T(8,128)(2,1)}, u32[]{:S(2)}, u32[]{:S(2)}) collective-permute-start(bf16[384,768]{1,0:T(8,128)(2,1)} %get-tuple-element.196), channel_id=1, source_target_pairs={{0,2},{1,3},{2,0},{3,1},{4,6},{5,7},{6,4},{7,5},{8,10},{9,11},{10,... | collective-permute-start | bytes 1769480 | tf_op jit(solution)/shard_map/ppermute | solution.py:36
  10.6 5.1 %embed.1 = (bf16[2,192,640]{2,1,0:T(8,128)(2,1)}, bf16[192,768]{1,0:T(8,128)(2,1)S(1)}, bf16[192,768]{1,0:T(8,128)(2,1)S(1)}, s32[256,8]{1,0:T(8,128)S(1)}) custom-call(s32[2]{0:T(128)S(1)} %copy-done.55, s32[8]{0:T(128)S(1)} %copy-done.50, s32[8,256]{1,0:T(8,128)S(1)} %copy-done.46, s32[8,128]{1,0:T(8,128)S(1)} %copy-done.48, ...), custom_call_target="tpu_custom_call" | custom-call | flops 57500000256 | bytes 50000000 | tf_op jit(solution)/shard_map/embed/pallas_call | solution.py:72
  17.1 4.9 %collective-permute-done.c2a = bf16[384,768]{1,0:T(8,128)(2,1)} collective-permute-done((bf16[384,768]{1,0:T(8,128)(2,1)}, bf16[384,768]{1,0:T(8,128)(2,1)}, u32[]{:S(2)}, u32[]{:S(2)}) %collective-permute-start) | collective-permute-done | bytes 589856 | tf_op jit(solution)/shard_map/ppermute | solution.py:36
  25.0 10.0 %collective-permute-done.2.e2 = bf16[2,192,640]{2,1,0:T(8,128)(2,1)} collective-permute-done((bf16[2,192,640]{2,1,0:T(8,128)(2,1)}, bf16[2,192,640]{2,1,0:T(8,128)(2,1)}, u32[]{:S(2)}, u32[]{:S(2)}) %collective-permute-start.2) | collective-permute-done | bytes 491552 | tf_op jit(solution)/shard_map/ppermute | solution.py:36
  44.0 7.8 %attention_first.1 = (f32[512,768]{1,0:T(8,128)S(1)}, f32[512,1]{1,0:T(8,128)S(1)}, bf16[512,768]{1,0:T(8,128)(2,1)S(1)}, bf16[3,512,192]{2,1,0:T(8,128)(2,1)S(1...) custom-call(s32[2]{0:T(128)S(1)} %copy-done.55, ...), custom_call_target="tpu_custom_call" | custom-call | flops 80499998720 | bytes 70000000 | tf_op jit(solution)/shard_map/attention_first/pallas_call | solution.py:72
  51.9 3.5 %collective-permute-done.5.c2b = bf16[384,768]{1,0:T(8,128)(2,1)S(1)} collective-permute-done((bf16[384,768]{1,0:T(8,128)(2,1)}, bf16[384,768]{1,0:T(8,128)(2,1)S(1)}, u32[]{:S(2)}, u32[]{:S(2)}) %collective-permute-start.5) | collective-permute-done | bytes 589856 | tf_op jit(solution)/shard_map/ppermute | solution.py:36
  59.8 2.6 collective-permute-start.14
  64.0 8.8 %attention_second.1 = (f32[512,768]{1,0:T(8,128)S(1)}, f32[512,1]{1,0:T(8,128)S(1)}, bf16[512,768]{1,0:T(8,128)(2,1)S(1)}, bf16[3,512,192]{2,1,0:T(8,128)(2,1)S(...) custom-call(s32[2]{0:T(128)S(1)} %copy-done.55, ...), custom_call_target="tpu_custom_call" | custom-call | flops 92000002048 | bytes 80000000 | tf_op jit(solution)/shard_map/attention_second/pallas_call | solution.py:72
  73.0 3.8 %collective-permute-done.18.d2a = bf16[384,768]{1,0:T(8,128)(2,1)S(1)} collective-permute-done((bf16[384,768]{1,0:T(8,128)(2,1)S(1)}, bf16[384,768]{1,0:T(8,128)(2,1)S(1)}, u32[]{:S(2)}, u32[]{:S(2)}) %collective-permute-start.18) | collective-permute-done | bytes 589856 | tf_op jit(solution)/shard_map/ppermute | solution.py:36
  79.4 6.3 %mlp_first.1 = (bf16[512,768]{1,0:T(8,128)(2,1)S(1)}, bf16[512,768]{1,0:T(8,128)(2,1)S(1)}, f32[512,768]{1,0:T(8,128)S(1)}, f32[512,768]{1,0:T(8,128)S(1)}, f32[512,768]{1,0:T(8,128)S(1)}) custom-call(s32[2]{0:T(128)S(1)} %copy-done.55, bf16[512,768]{1,0:T(8,128)(2,1)S(1)} %get-tuple-element.236.h1b_ref, f32[8,4096]{1,0:T(8,128)S(1)} %concatenate.9.b0.s0, ...), custom_call_target="tpu_custom_call" | custom-call | flops 80499998720 | bytes 70000000 | tf_op jit(solution)/shard_map/mlp_first/pallas_call | solution.py:72
  87.6 2.6 collective-permute-done.19.d2b
  93.1 7.6 %mlp_second.1 = (bf16[512,768]{1,0:T(8,128)(2,1)S(1)}, bf16[512,768]{1,0:T(8,128)(2,1)S(1)}, f32[512,768]{1,0:T(8,128)S(1)}, f32[512,768]{1,0:T(8,128)S(1)}, f32...) custom-call(s32[2]{0:T(128)S(1)} %copy-done.55, ...), custom_call_target="tpu_custom_call" | custom-call | flops 80499998720 | bytes 70000000 | tf_op jit(solution)/shard_map/mlp_second/pallas_call | solution.py:72
  105.2 8.5 %head.1 = (f32[512,768]{1,0:T(8,128)S(1)}, bf16[512,768]{1,0:T(8,128)(2,1)S(1)}, f32[1,128]{1,0:T(1,128)S(1)}, f32[1,2304]{1,0:T(1,128)S(1)}, f32[3,768]{1,0:T(4...) custom-call(s32[2]{0:T(128)S(1)} %copy-done.55, s32[8]{0:T(128)S(1)} %copy-done.51, ...), custom_call_target="tpu_custom_call" | custom-call | flops 103499997184 | bytes 90000000 | tf_op jit(solution)/shard_map/head/pallas_call | solution.py:72
  120.4 7.3 %up_send.1 = (bf16[2,768,768]{2,1,0:T(8,128)(2,1)S(1)}, f32[2,8,768]{2,1,0:T(8,128)S(1)}, f32[512,768]{1,0:T(8,128)S(1)}, f32[2,1,768]{2,1,0:T(1,128)S(1)}) custom-call(s32[2]{0:T(128)S(1)} %copy-done.55, bf16[512,768]{1,0:T(8,128)(2,1)S(1)} %get-tuple-element.268.dzb_ref, bf16[512,768]{1,0:T(8,128)(2,1)S(1)} %get-tuple-element.236.h1b_ref, ...), custom_call_target="tpu_custom_call" | custom-call | flops 69000003584 | bytes 60000000 | tf_op jit(solution)/shard_map/up_send/pallas_call | solution.py:72
  127.9 3.3 %down_keep.1 = (bf16[384,768]{1,0:T(8,128)(2,1)}, bf16[384,768]{1,0:T(8,128)(2,1)S(1)}, f32[768,768]{1,0:T(8,128)S(1)}, f32[2,8,768]{2,1,0:T(8,128)S(1)}) custom-call(bf16[512,768]{1,0:T(8,128)(2,1)S(1)} %get-tuple-element.268.dzb_ref, bf16[512,768]{1,0:T(8,128)(2,1)S(1)} %get-tuple-element.262.a0, bf16[512,768]{1,0:T(8,128)(2,1)S(1)} %get-tuple-element.263.a2, ...), custom_call_target="tpu_custom_call" | custom-call | flops 46000001024 | bytes 40000000 | tf_op jit(solution)/shard_map/down_keep/pallas_call | solution.py:72
  133.3 10.3 %up_keep.1 = (bf16[576,768]{1,0:T(8,128)(2,1)}, bf16[576,768]{1,0:T(8,128)(2,1)S(1)}, f32[768,768]{1,0:T(8,128)S(1)}, f32[2,8,768]{2,1,0:T(8,128)S(1)}, f32[512,...) custom-call(s32[2]{0:T(128)S(1)} %copy-done.55, ...), custom_call_target="tpu_custom_call" | custom-call | flops 92000002048 | bytes 80000000 | tf_op jit(solution)/shard_map/up_keep/pallas_call | solution.py:72
  143.8 12.2 %attention_send.1 = (bf16[2,768,768]{2,1,0:T(8,128)(2,1)S(1)}, f32[2,16,2496]{2,1,0:T(8,128)S(1)}, f32[512,768]{1,0:T(8,128)S(1)}) custom-call(s32[2]{0:T(128)S(1)} %copy-done.55, bf16[512,768]{1,0:T(8,128)(2,1)S(1)} %get-tuple-element.289.dz1b_ref, bf16[512,768]{1,0:T(8,128)(2,1)S(1)} %copy-done.73, bf16[3,512,192]{2,1,0:T(8,128)(2,1)S(1)} %copy-done.75, ...), custom_call_target="tpu_custom_call" | custom-call | flops 149500002304 | bytes 130000000 | tf_op jit(solution)/shard_map/attention_send/pallas_call | solution.py:72
  157.8 2.8 collective-permute-done.35.near_ref
  160.7 15.4 %attention_keep.1 = (bf16[768,768]{1,0:T(8,128)(2,1)S(1)}, f32[768,768]{1,0:T(8,128)S(1)}, f32[2,16,2496]{2,1,0:T(8,128)S(1)}, f32[2,16,2496]{2,1,0:T(8,128)S(1)...) custom-call(s32[2]{0:T(128)S(1)} %copy-done.55, ...), custom_call_target="tpu_custom_call" | custom-call | flops 172499992576 | bytes 150000000 | tf_op jit(solution)/shard_map/attention_keep/pallas_call | solution.py:72
  182.3 5.0 %collective-permute-done.38 = f32[16,2496]{1,0:T(8,128)S(1)} collective-permute-done((f32[16,2496]{1,0:T(8,128)S(1)}, f32[16,2496]{1,0:T(8,128)S(1)}, u32[]{:S(2)}, u32[]{:S(2)}) %collective-permute-start.38) | collective-permute-done | bytes 159776 | tf_op jit(solution)/shard_map/ppermute | solution.py:36
  188.3 3.6 %collective-permute-done.39 = f32[8,2496]{1,0:T(8,128)S(1)} collective-permute-done((f32[8,2496]{1,0:T(8,128)S(1)}, f32[8,2496]{1,0:T(8,128)S(1)}, u32[]{:S(2)}, u32[]{:S(2)}) %collective-permute-start.39) | collective-permute-done | bytes 79904 | tf_op jit(solution)/shard_map/ppermute | solution.py:36
  191.8 5.9 %collective-permute-done.36.r2 = bf16[2,512,192]{2,1,0:T(8,128)(2,1)S(1)} collective-permute-done((bf16[2,512,192]{2,1,0:T(8,128)(2,1)S(1)}, bf16[2,512,192]{2,1,0:T(8,128)(2,1)S(1)}, u32[]{:S(2)}, u32[]{:S(2)}) %collective-permute-start.36) | collective-permute-done | bytes 393248 | tf_op jit(solution)/shard_map/ppermute | solution.py:36
  208.4 4.1 %scatter.1 = bf16[192,2304]{1,0:T(8,128)(2,1)S(1)} custom-call(s32[256,8]{1,0:T(8,128)S(1)} %copy-done.67, bf16[512,192]{1,0:T(8,128)(2,1)S(1)} %copy-done.65, bf16[512,192]{1,0:T(8,128)(2,1)} %collective-permute-done.43.r1, bf16[2,512,192]{2,1,0:T(8,128)(2,1)S(1)} %collective-permute-done.36.r2, bf16[2,512,192]{2,1,0:T(8,128)(2,1)} %collective-permute-done.44.r3, ...), custom_call_target="tpu_custom_call" | custom-call | flops 5750000128 | bytes 5000000 | tf_op jit(solution)/shard_map/scatter/pallas_call | solution.py:72
  217.0 5.6 %collective-permute-done.40.got_b.refs_1_ = bf16[576,768]{1,0:T(8,128)(2,1)S(1)} collective-permute-done((bf16[576,768]{1,0:T(8,128)(2,1)}, bf16[576,768]{1,0:T(8,128)(2,1)S(1)}, u32[]{:S(2)}, u32[]{:S(2)}) %collective-permute-start.40) | collective-permute-done | bytes 884768 | tf_op jit(solution)/shard_map/ppermute | solution.py:36
  226.3 6.5 %collective-permute-done.45 = f32[8,4032]{1,0:T(8,128)S(1)} collective-permute-done((f32[8,4032]{1,0:T(8,128)S(1)}, f32[8,4032]{1,0:T(8,128)S(1)}, u32[]{:S(2)}, u32[]{:S(2)}) %collective-permute-start.45) | collective-permute-done | bytes 129056 | tf_op jit(solution)/shard_map/ppermute | solution.py:36
  233.8 4.1 %collective-permute-done.47 = f32[8,4032]{1,0:T(8,128)S(1)} collective-permute-done((f32[8,4032]{1,0:T(8,128)S(1)}, f32[8,4032]{1,0:T(8,128)S(1)}, u32[]{:S(2)}, u32[]{:S(2)}) %collective-permute-start.47) | collective-permute-done | bytes 129056 | tf_op jit(solution)/shard_map/ppermute | solution.py:36
  238.6 5.4 %collective-permute-done.48 = f32[8,4032]{1,0:T(8,128)S(1)} collective-permute-done((f32[8,4032]{1,0:T(8,128)S(1)}, f32[8,4032]{1,0:T(8,128)S(1)}, u32[]{:S(2)}, u32[]{:S(2)}) %collective-permute-start.48) | collective-permute-done | bytes 129056 | tf_op jit(solution)/shard_map/ppermute | solution.py:36
  249.2 6.4 %update.4 = (f32[768,768]{1,0:T(8,128)}, f32[768,768]{1,0:T(8,128)}, f32[768,768]{1,0:T(8,128)}) custom-call(f32[768,768]{1,0:T(8,128)S(1)} %copy-done.63, bf16[768,768]{1,0:T(8,128)(2,1)S(1)} %copy-done.16, f32[768,768]{1,0:T(8,128)S(1)} %copy-done.10, f32[8,768]{1,0:T(8,128)S(1)} %copy-done.53, f32[8,768]{1,0:T(8,128)S(1)} %get-tuple-element.380.second_ref, ...), custom_call_target="tpu_custom_call" | custom-call | flops 4600000000 | bytes 4000000 | tf_op jit(solution)/shard_map/update/pallas_call | solution.py:72
  256.8 5.9 %update.5 = (f32[768,768]{1,0:T(8,128)}, f32[768,768]{1,0:T(8,128)}, f32[768,768]{1,0:T(8,128)}) custom-call(f32[768,768]{1,0:T(8,128)S(1)} %copy-done.61, bf16[768,768]{1,0:T(8,128)(2,1)S(1)} %copy-done.19, f32[768,768]{1,0:T(8,128)S(1)} %copy-done.11, f32[8,768]{1,0:T(8,128)S(1)} %copy-done.52, f32[8,768]{1,0:T(8,128)S(1)} %get-tuple-element.379.second_ref, ...), custom_call_target="tpu_custom_call" | custom-call | flops 4600000000 | bytes 4000000 | tf_op jit(solution)/shard_map/update/pallas_call | solution.py:72
  273.8 3.2 %update.7 = (f32[192,768]{1,0:T(8,128)}, f32[192,768]{1,0:T(8,128)}, f32[192,768]{1,0:T(8,128)}) custom-call(f32[768,768]{1,0:T(8,128)S(1)} %copy-done.59, bf16[192,768]{1,0:T(8,128)(2,1)S(1)} %copy-done.40, f32[192,768]{1,0:T(8,128)S(1)} %copy-done.24, f32[8,192]{1,0:T(8,128)S(1)} %copy-done.56, f32[8,768]{1,0:T(8,128)S(1)} %get-tuple-element.390.second_ref, ...), custom_call_target="tpu_custom_call" | custom-call | flops 4600000000 | bytes 4000000 | tf_op jit(solution)/shard_map/update/pallas_call | solution.py:72
  277.6 4.2 %update.6 = (f32[576,768]{1,0:T(8,128)}, f32[576,768]{1,0:T(8,128)}, f32[576,768]{1,0:T(8,128)}) custom-call(f32[768,768]{1,0:T(8,128)S(1)} %copy-done.59, bf16[576,768]{1,0:T(8,128)(2,1)S(1)} %bitcast.70, f32[576,768]{1,0:T(8,128)S(1)} %bitcast.68, f32[8,576]{1,0:T(8,128)S(1)} %get-tuple-element.392.first_ref, f32[8,768]{1,0:T(8,128)S(1)} %copy-done.54, ...), custom_call_target="tpu_custom_call" | custom-call | flops 4600000000 | bytes 4000000 | tf_op jit(solution)/shard_map/update/pallas_call | solution.py:72
  (375 shorter events, 93.6 us)
Async XLA Ops:
  0.7 38.6 %collective-permute-start.7 = (bf16[768,768]{1,0:T(8,128)(2,1)}, bf16[768,768]{1,0:T(8,128)(2,1)}, u32[]{:S(2)}, u32[]{:S(2)}) collective-permute-start(bf16[768,768]{1,0:T(8,128)(2,1)} %weight.4), channel_id=1, source_target_pairs={{0,1},{1,0},{2,3},{3,2},{4,5},{5,4},{6,7},{7,6},{8,9},{9,8},{10,11... | collective-permute-start | bytes 3538952 | tf_op jit(solution)/shard_map/ppermute | solution.py:36
  1.2 38.2 %collective-permute-start.8 = (bf16[768,768]{1,0:T(8,128)(2,1)}, bf16[768,768]{1,0:T(8,128)(2,1)}, u32[]{:S(2)}, u32[]{:S(2)}) collective-permute-start(bf16[768,768]{1,0:T(8,128)(2,1)} %weight.3), channel_id=1, source_target_pairs={{0,1},{1,0},{2,3},{3,2},{4,5},{5,4},{6,7},{7,6},{8,9},{9,8},{10,11... | collective-permute-start | bytes 3538952 | tf_op jit(solution)/shard_map/ppermute | solution.py:36
  5.1 16.9 %collective-permute-start = (bf16[384,768]{1,0:T(8,128)(2,1)}, bf16[384,768]{1,0:T(8,128)(2,1)}, u32[]{:S(2)}, u32[]{:S(2)}) collective-permute-start(bf16[384,768]{1,0:T(8,128)(2,1)} %get-tuple-element.196), channel_id=1, source_target_pairs={{0,2},{1,3},{2,0},{3,1},{4,6},{5,7},{6,4},{7,5},{8,10},{9,11},{10,... | collective-permute-start | bytes 1769480 | tf_op jit(solution)/shard_map/ppermute | solution.py:36
  8.1 32.8 %collective-permute-start.9 = (bf16[768,768]{1,0:T(8,128)(2,1)}, bf16[768,768]{1,0:T(8,128)(2,1)S(1)}, u32[]{:S(2)}, u32[]{:S(2)}) collective-permute-start(bf16[768,768]{1,0:T(8,128)(2,1)} %get-tuple-element.209.c0), channel_id=1, source_target_pairs={{0,1},{1,0},{2,3},{3,2},{4,5},{5,4},{6,7},{7,6},{8,9},{9,8},{10,11... | collective-permute-start | bytes 3538952 | tf_op jit(solution)/shard_map/ppermute | solution.py:36
  10.0 28.6 %collective-permute-start.10 = (bf16[192,2304]{1,0:T(8,128)(2,1)S(1)}, bf16[192,2304]{1,0:T(8,128)(2,1)}, u32[]{:S(2)}, u32[]{:S(2)}) collective-permute-start(bf16[192,2304]{1,0:T(8,128)(2,1)S(1)} %get-tuple-element.200.table_ref.t0), channel_id=1, source_target_pairs={{0,1},{1,0},{2,3},{3,2},{4,5},{5,4},{6,7},{7,6},{8,9},{9,8},{10,11... | collective-permute-start | bytes 2654216 | tf_op jit(solution)/shard_map/ppermute | solution.py:36
  22.0 13.0 %collective-permute-start.2 = (bf16[2,192,640]{2,1,0:T(8,128)(2,1)}, bf16[2,192,640]{2,1,0:T(8,128)(2,1)}, u32[]{:S(2)}, u32[]{:S(2)}) collective-permute-start(bf16[2,192,640]{2,1,0:T(8,128)(2,1)} %get-tuple-element.201), channel_id=1, source_target_pairs={{0,2},{1,3},{2,0},{3,1},{4,6},{5,7},{6,4},{7,5},{8,10},{9,11},{10,... | collective-permute-start | bytes 1474568 | tf_op jit(solution)/shard_map/ppermute | solution.py:36
  39.4 15.9 %collective-permute-start.5 = (bf16[384,768]{1,0:T(8,128)(2,1)}, bf16[384,768]{1,0:T(8,128)(2,1)S(1)}, u32[]{:S(2)}, u32[]{:S(2)}) collective-permute-start(bf16[384,768]{1,0:T(8,128)(2,1)} %collective-permute-done.c2a), channel_id=1, source_target_pairs={{0,4},{4,0},{8,12},{12,8},{16,20},{20,16},{24,28},{28,24},{1,5},{5... | collective-permute-start | bytes 1769480 | tf_op jit(solution)/shard_map/ppermute | solution.py:36
  40.9 10.9 %collective-permute-start.6 = (f32[8,4096]{1,0:T(8,128)S(1)}, f32[8,4096]{1,0:T(8,128)S(1)}, u32[]{:S(2)}, u32[]{:S(2)}) collective-permute-start(f32[8,4096]{1,0:T(8,128)S(1)} %concatenate.9.b0.s0), channel_id=1, source_target_pairs={{0,2},{1,3},{2,0},{3,1},{4,6},{5,7},{6,4},{7,5},{8,10},{9,11},{10,... | collective-permute-start | bytes 393224 | tf_op jit(solution)/shard_map/ppermute | solution.py:36
  42.4 16.8 %collective-permute-start.4 = (bf16[384,768]{1,0:T(8,128)(2,1)}, bf16[384,768]{1,0:T(8,128)(2,1)}, u32[]{:S(2)}, u32[]{:S(2)}) collective-permute-start(bf16[384,768]{1,0:T(8,128)(2,1)} %copy-done.37), channel_id=1, source_target_pairs={{0,2},{1,3},{2,0},{3,1},{4,6},{5,7},{6,4},{7,5},{8,10},{9,11},{10,... | collective-permute-start | bytes 1769480 | tf_op jit(solution)/shard_map/ppermute | solution.py:36
  55.4 8.5 %collective-permute-start.16 = (bf16[384,768]{1,0:T(8,128)(2,1)}, bf16[384,768]{1,0:T(8,128)(2,1)S(1)}, u32[]{:S(2)}, u32[]{:S(2)}) collective-permute-start(bf16[384,768]{1,0:T(8,128)(2,1)} %collective-permute-done.c2a), channel_id=1, source_target_pairs={{0,1},{1,0},{2,3},{3,2},{4,5},{5,4},{6,7},{7,6},{8,9},{9,8},{10,11... | collective-permute-start | bytes 1769480 | tf_op jit(solution)/shard_map/ppermute | solution.py:36
  55.4 8.6 %collective-permute-start.17 = (bf16[384,768]{1,0:T(8,128)(2,1)S(1)}, bf16[384,768]{1,0:T(8,128)(2,1)S(1)}, u32[]{:S(2)}, u32[]{:S(2)}) collective-permute-start(bf16[384,768]{1,0:T(8,128)(2,1)S(1)} %collective-permute-done.5.c2b), channel_id=1, source_target_pairs={{0,1},{1,0},{2,3},{3,2},{4,5},{5,4},{6,7},{7,6},{8,9},{9,8},{10,11... | collective-permute-start | bytes 1769480 | tf_op jit(solution)/shard_map/ppermute | solution.py:36
  59.2 26.6 %collective-permute-start.21 = (bf16[384,768]{1,0:T(8,128)(2,1)}, bf16[384,768]{1,0:T(8,128)(2,1)}, u32[]{:S(2)}, u32[]{:S(2)}) collective-permute-start(bf16[384,768]{1,0:T(8,128)(2,1)} %collective-permute-done.4.u2a), channel_id=1, source_target_pairs={{0,4},{4,0},{8,12},{12,8},{16,20},{20,16},{24,28},{28,24},{1,5},{5... | collective-permute-start | bytes 1769480 | tf_op jit(solution)/shard_map/ppermute | solution.py:36
  59.8 13.1 %collective-permute-start.14 = (f32[8,128]{1,0:T(8,128)S(1)}, f32[8,128]{1,0:T(8,128)S(1)}, u32[]{:S(2)}, u32[]{:S(2)}) collective-permute-start(f32[8,128]{1,0:T(8,128)S(1)} %add.72), channel_id=1, source_target_pairs={{0,16},{4,20},{8,24},{12,28},{16,0},{20,4},{24,8},{28,12},{1,17},{... | collective-permute-start | bytes 12296 | tf_op jit(solution)/shard_map/ppermute | solution.py:36
  62.4 14.3 %collective-permute-start.18 = (bf16[384,768]{1,0:T(8,128)(2,1)S(1)}, bf16[384,768]{1,0:T(8,128)(2,1)S(1)}, u32[]{:S(2)}, u32[]{:S(2)}) collective-permute-start(bf16[384,768]{1,0:T(8,128)(2,1)S(1)} %copy-done.36), channel_id=1, source_target_pairs={{0,2},{1,3},{2,0},{3,1},{4,6},{5,7},{6,4},{7,5},{8,10},{9,11},{10,... | collective-permute-start | bytes 1769480 | tf_op jit(solution)/shard_map/ppermute | solution.py:36
  76.7 13.4 %collective-permute-start.19 = (bf16[384,768]{1,0:T(8,128)(2,1)S(1)}, bf16[384,768]{1,0:T(8,128)(2,1)S(1)}, u32[]{:S(2)}, u32[]{:S(2)}) collective-permute-start(bf16[384,768]{1,0:T(8,128)(2,1)S(1)} %collective-permute-done.18.d2a), channel_id=1, source_target_pairs={{0,4},{4,0},{8,12},{12,8},{16,20},{20,16},{24,28},{28,24},{1,5},{5... | collective-permute-start | bytes 1769480 | tf_op jit(solution)/shard_map/ppermute | solution.py:36
  77.9 9.6 %collective-permute-start.20 = (bf16[96,2304]{1,0:T(8,128)(2,1)S(1)}, bf16[96,2304]{1,0:T(8,128)(2,1)S(1)}, u32[]{:S(2)}, u32[]{:S(2)}) collective-permute-start(bf16[96,2304]{1,0:T(8,128)(2,1)S(1)} %copy-done.39), channel_id=1, source_target_pairs={{0,2},{1,3},{2,0},{3,1},{4,6},{5,7},{6,4},{7,5},{8,10},{9,11},{10,... | collective-permute-start | bytes 1327112 | tf_op jit(solution)/shard_map/ppermute | solution.py:36
  90.6 12.1 %collective-permute-start.26 = (bf16[96,2304]{1,0:T(8,128)(2,1)S(1)}, bf16[96,2304]{1,0:T(8,128)(2,1)S(1)}, u32[]{:S(2)}, u32[]{:S(2)}) collective-permute-start(bf16[96,2304]{1,0:T(8,128)(2,1)S(1)} %collective-permute-done.20.t2a), channel_id=1, source_target_pairs={{0,4},{4,0},{8,12},{12,8},{16,20},{20,16},{24,28},{28,24},{1,5},{5... | collective-permute-start | bytes 1327112 | tf_op jit(solution)/shard_map/ppermute | solution.py:36
  116.0 11.8 %collective-permute-start.30 = (bf16[2,768,768]{2,1,0:T(8,128)(2,1)S(1)}, bf16[2,768,768]{2,1,0:T(8,128)(2,1)S(1)}, u32[]{:S(2)}, u32[]{:S(2)}) collective-permute-start(bf16[2,768,768]{2,1,0:T(8,128)(2,1)S(1)} %get-tuple-element.255), channel_id=1, source_target_pairs={{0,1},{1,0},{2,3},{3,2},{4,5},{5,4},{6,7},{7,6},{8,9},{9,8},{10,11... | collective-permute-start | bytes 7077896 | tf_op jit(solution)/shard_map/ppermute | solution.py:36
  118.9 37.1 %collective-permute-start.32 = (bf16[192,2304]{1,0:T(8,128)(2,1)}, bf16[192,2304]{1,0:T(8,128)(2,1)}, u32[]{:S(2)}, u32[]{:S(2)}) collective-permute-start(bf16[192,2304]{1,0:T(8,128)(2,1)} %fusion.1), channel_id=1, source_target_pairs={{0,2},{1,3},{2,0},{3,1},{4,6},{5,7},{6,4},{7,5},{8,10},{9,11},{10,... | collective-permute-start | bytes 2654216 | tf_op jit(solution)/shard_map/ppermute | solution.py:36
  132.6 23.4 %collective-permute-start.31 = (bf16[384,768]{1,0:T(8,128)(2,1)}, bf16[384,768]{1,0:T(8,128)(2,1)}, u32[]{:S(2)}, u32[]{:S(2)}) collective-permute-start(bf16[384,768]{1,0:T(8,128)(2,1)} %get-tuple-element.265), channel_id=1, source_target_pairs={{0,2},{1,3},{2,0},{3,1},{4,6},{5,7},{6,4},{7,5},{8,10},{9,11},{10,... | collective-permute-start | bytes 1769480 | tf_op jit(solution)/shard_map/ppermute | solution.py:36
  156.3 22.2 %collective-permute-start.34 = (bf16[576,768]{1,0:T(8,128)(2,1)}, bf16[576,768]{1,0:T(8,128)(2,1)}, u32[]{:S(2)}, u32[]{:S(2)}) collective-permute-start(bf16[576,768]{1,0:T(8,128)(2,1)} %get-tuple-element.288), channel_id=1, source_target_pairs={{0,2},{1,3},{2,0},{3,1},{4,6},{5,7},{6,4},{7,5},{8,10},{9,11},{10,... | collective-permute-start | bytes 2654216 | tf_op jit(solution)/shard_map/ppermute | solution.py:36
  181.7 16.0 %collective-permute-start.36 = (bf16[2,512,192]{2,1,0:T(8,128)(2,1)S(1)}, bf16[2,512,192]{2,1,0:T(8,128)(2,1)S(1)}, u32[]{:S(2)}, u32[]{:S(2)}) collective-permute-start(bf16[2,512,192]{2,1,0:T(8,128)(2,1)S(1)} %get-tuple-element.306), channel_id=1, source_target_pairs={{0,2},{1,3},{2,0},{3,1},{4,6},{5,7},{6,4},{7,5},{8,10},{9,11},{10,... | collective-permute-start | bytes 1179656 | tf_op jit(solution)/shard_map/ppermute | solution.py:36
  188.2 16.8 %collective-permute-start.43 = (bf16[512,192]{1,0:T(8,128)(2,1)}, bf16[512,192]{1,0:T(8,128)(2,1)}, u32[]{:S(2)}, u32[]{:S(2)}) collective-permute-start(bf16[512,192]{1,0:T(8,128)(2,1)} %get-tuple-element.323), channel_id=1, source_target_pairs={{0,1},{1,0},{2,3},{3,2},{4,5},{5,4},{6,7},{7,6},{8,9},{9,8},{10,11... | collective-permute-start | bytes 589832 | tf_op jit(solution)/shard_map/ppermute | solution.py:36
  199.9 22.7 %collective-permute-start.40 = (bf16[576,768]{1,0:T(8,128)(2,1)}, bf16[576,768]{1,0:T(8,128)(2,1)S(1)}, u32[]{:S(2)}, u32[]{:S(2)}) collective-permute-start(bf16[576,768]{1,0:T(8,128)(2,1)} %copy-done.22), channel_id=1, source_target_pairs={{0,2},{1,3},{2,0},{3,1},{4,6},{5,7},{6,4},{7,5},{8,10},{9,11},{10,... | collective-permute-start | bytes 2654216 | tf_op jit(solution)/shard_map/ppermute | solution.py:36
  204.5 8.0 %collective-permute-start.42 = (f32[8,2496]{1,0:T(8,128)S(1)}, f32[8,2496]{1,0:T(8,128)S(1)}, u32[]{:S(2)}, u32[]{:S(2)}) collective-permute-start(f32[8,2496]{1,0:T(8,128)S(1)} %add.78), channel_id=1, source_target_pairs={{0,16},{4,20},{8,24},{12,28},{16,0},{20,4},{24,8},{28,12},{1,17},{... | collective-permute-start | bytes 239624 | tf_op jit(solution)/shard_map/ppermute | solution.py:36
  212.6 13.0 %collective-permute-start.46 = (bf16[96,2304]{1,0:T(8,128)(2,1)S(1)}, bf16[96,2304]{1,0:T(8,128)(2,1)S(1)}, u32[]{:S(2)}, u32[]{:S(2)}) collective-permute-start(bf16[96,2304]{1,0:T(8,128)(2,1)S(1)} %broadcast_select_fusion.2), channel_id=1, source_target_pairs={{0,4},{4,0},{8,12},{12,8},{16,20},{20,16},{24,28},{28,24},{1,5},{5... | collective-permute-start | bytes 1327112 | tf_op jit(solution)/shard_map/ppermute | solution.py:36
  215.5 31.7 %collective-permute-start.51 = (bf16[768,768]{1,0:T(8,128)(2,1)S(1)}, bf16[768,768]{1,0:T(8,128)(2,1)S(1)}, u32[]{:S(2)}, u32[]{:S(2)}) collective-permute-start(bf16[768,768]{1,0:T(8,128)(2,1)S(1)} %get-tuple-element.336), channel_id=1, source_target_pairs={{0,2},{1,3},{2,0},{3,1},{4,6},{5,7},{6,4},{7,5},{8,10},{9,11},{10,... | collective-permute-start | bytes 3538952 | tf_op jit(solution)/shard_map/ppermute | solution.py:36
  225.0 7.8 %collective-permute-start.45 = (f32[8,4032]{1,0:T(8,128)S(1)}, f32[8,4032]{1,0:T(8,128)S(1)}, u32[]{:S(2)}, u32[]{:S(2)}) collective-permute-start(f32[8,4032]{1,0:T(8,128)S(1)} %right_mlp.1), channel_id=1, source_target_pairs={{0,16},{4,20},{8,24},{12,28},{16,0},{20,4},{24,8},{28,12},{1,17},{... | collective-permute-start | bytes 387080 | tf_op jit(solution)/shard_map/ppermute | solution.py:36
  225.8 12.2 %collective-permute-start.49 = (bf16[48,2304]{1,0:T(8,128)(2,1)S(1)}, bf16[48,2304]{1,0:T(8,128)(2,1)S(1)}, u32[]{:S(2)}, u32[]{:S(2)}) collective-permute-start(bf16[48,2304]{1,0:T(8,128)(2,1)S(1)} %broadcast_select_fusion.5), channel_id=1, source_target_pairs={{0,8},{4,12},{8,0},{12,4},{16,24},{20,28},{24,16},{28,20},{1,9},{5... | collective-permute-start | bytes 663560 | tf_op jit(solution)/shard_map/ppermute | solution.py:36
  238.1 10.8 %collective-permute-start.50 = (bf16[48,2304]{1,0:T(8,128)(2,1)S(1)}, bf16[48,2304]{1,0:T(8,128)(2,1)S(1)}, u32[]{:S(2)}, u32[]{:S(2)}) collective-permute-start(bf16[48,2304]{1,0:T(8,128)(2,1)S(1)} %add_convert_fusion.3), channel_id=1, source_target_pairs={{0,16},{4,20},{8,24},{12,28},{16,0},{20,4},{24,8},{28,12},{1,17},{... | collective-permute-start | bytes 663560 | tf_op jit(solution)/shard_map/ppermute | solution.py:36
  255.7 9.4 %collective-permute-start.55 = (f32[8,1344]{1,0:T(8,128)S(1)}, f32[8,1344]{1,0:T(8,128)S(1)}, u32[]{:S(2)}, u32[]{:S(2)}) collective-permute-start(f32[8,1344]{1,0:T(8,128)S(1)} %add.86), channel_id=1, source_target_pairs={{0,4},{4,0},{8,12},{12,8},{16,20},{20,16},{24,28},{28,24},{1,5},{5... | collective-permute-start | bytes 129032 | tf_op jit(solution)/shard_map/ppermute | solution.py:36
  263.8 18.0 %collective-permute-start.54 = (bf16[96,2304]{1,0:T(8,128)(2,1)S(1)}, bf16[96,2304]{1,0:T(8,128)(2,1)S(1)}, u32[]{:S(2)}, u32[]{:S(2)}) collective-permute-start(bf16[96,2304]{1,0:T(8,128)(2,1)S(1)} %pad_maximum_fusion.1), channel_id=1, source_target_pairs={{0,4},{4,0},{8,12},{12,8},{16,20},{20,16},{24,28},{28,24},{1,5},{5... | collective-permute-start | bytes 1327112 | tf_op jit(solution)/shard_map/ppermute | solution.py:36
  (138 other events, 1467.2 us)
